TPU v7x, 256 devices: a whole 4x4x8 slice. The times are simulated.
256 devices in a mesh: psg: 8 (over x, core), doc: 32 (over z, y).
Axes of the slice: x: 4, y: 4, z: 8, core: 2. Of those that a mesh axis runs over, the one named last changes fastest.
Arguments:
- hidden: bfloat16 [8, 32, 16, 128, 768], P(None, 'doc', 'psg'), may hold values from -6 to 6
- token_ids: int32 [8, 32, 16, 128], P(None, 'doc', 'psg'), may hold values from 0 to 30521, as said below
- passage_mask: int32 [8, 32, 16], P(None, 'doc', 'psg'), may hold values 0 or 1
- labels: int32 [8], replicated, may hold values from 0 to 31
- enc_weights: bfloat16 [4, 768, 768], replicated, may hold values from -0.21875 to 0.21875
- enc_gain: float32 [768], replicated, may hold values from 0.25 to 1.75
- agg_weights: bfloat16 [4, 768, 768], replicated, may hold values from -0.21875 to 0.21875
- agg_gain: float32 [768], replicated, may hold values from 0.25 to 1.75
- agg_cls: bfloat16 [768], replicated, may hold values from -6 to 6
- head_vector: float32 [768], replicated, may hold values from -1 to 1
- score_bias: float32 [], replicated, may hold values from 90 to 120
Outputs:
- scores: float32 [8, 32], P(None, 'doc')
- list_loss: float32 [], replicated
- weight_grads: float32 [2, 4, 589824], P(None, None, ('psg', 'doc'))
Inputs may be any that keep to these rules, and one draw needn't show every extreme that they name: `token_ids`: each passage's ids are nonzero from its first position up to its length and zero after it; the first id is never zero.
All inputs are finite; a program needn't handle non-finite values. No bound on the sum of `passage_mask` on one device may be relied on, other than what follows from the above.
Results may differ from a plain program's by a relative error of at most 0.013.
Values may be sent and summed in bfloat16 or wider, within the bound.
No kernel may reach another device: no remote copies, remote signals or barrier semaphores. Data moves between devices by JAX's collectives and lax.ppermute only.
A program may use at most 128 MiB of HBM per device.

v0:
```python
import jax
import jax.numpy as jnp
from jax import lax
from jax.sharding import PartitionSpec as P

HEADS = 12
HEAD = 64


exact_mode = lax.Precision.HIGHEST


def merged_2(array, axis, combine):
    everything = jax.tree.map(lambda part: lax.all_gather(part, axis), array)
    leading = jax.tree.map(lambda part: part[0], everything)

    def lap(k, so_far):
        return combine(so_far, jax.tree.map(lambda part: part[k], everything))

    return lax.fori_loop(1, lax.axis_size(axis), lap, leading)


def inner_rows(left, right):
    return lax.dot_general(
        left, right, (((0,), (0,)), ((), ())), preferred_element_type=jnp.float32
    )


def outer_rows(left, weight):
    return lax.dot_general(
        left, weight, (((1,), (1,)), ((), ())), preferred_element_type=jnp.float32
    )


def layer_norm(inputs, norm_gain):
    center = inputs - jnp.mean(inputs, axis=-1, keepdims=True)
    rscale = lax.rsqrt(jnp.mean(center * center, axis=-1, keepdims=True) + 1e-05)
    normed = center * rscale
    return (normed * norm_gain, normed, rscale)


def norm_back(grad_out, norm_gain, normed, rscale):
    grad_norm = grad_out * norm_gain
    return rscale * (
        grad_norm
        - jnp.mean(grad_norm, axis=-1, keepdims=True)
        - normed * jnp.mean(grad_norm * normed, axis=-1, keepdims=True)
    )


def encode(states, id_rows, enc_weights, enc_gain):
    row_count, length, model_width = states.shape
    flat_rows = states.reshape(row_count * length, model_width)
    pass_keys = jnp.dot(flat_rows, enc_weights[1], preferred_element_type=jnp.float32).reshape(
        row_count, length, HEADS, HEAD
    )
    values = jnp.dot(flat_rows, enc_weights[2], preferred_element_type=jnp.float32).reshape(
        row_count, length, HEADS, HEAD
    )
    first_rows = states[:, 0, :]
    cls_query = jnp.dot(first_rows, enc_weights[0], preferred_element_type=jnp.float32).reshape(
        row_count, HEADS, HEAD
    )
    valid_keys = (id_rows != 0)[:, None, :]
    logits = jnp.einsum("phe,pshe->phs", cls_query, pass_keys, precision=exact_mode) * HEAD ** (
        -0.5
    )
    logits = jnp.where(valid_keys, logits, -1e30)
    peak_val = jnp.max(logits, axis=-1, keepdims=True)
    raw_weights = jnp.where(valid_keys, jnp.exp(logits - peak_val), 0.0)
    soft_weights = raw_weights / jnp.sum(raw_weights, axis=-1, keepdims=True)
    attended = jnp.einsum("phs,pshe->phe", soft_weights, values, precision=exact_mode)
    attended_b = attended.reshape(row_count, model_width).astype(jnp.bfloat16)
    mixed_rows = first_rows.astype(jnp.float32) + jnp.dot(
        attended_b, enc_weights[3], preferred_element_type=jnp.float32
    )
    passage, normed, rscale = layer_norm(mixed_rows, enc_gain)
    saved = (pass_keys, values, cls_query, soft_weights, attended, attended_b, normed, rscale)
    return (passage.astype(jnp.bfloat16), saved)


def encode_back(states, saved, grad_passage, enc_weights, enc_gain):
    pass_keys, values, cls_query, soft_weights, attended, attended_b, normed, rscale = saved
    row_count, length, model_width = states.shape
    grad_mixed = norm_back(grad_passage, enc_gain, normed, rscale).astype(jnp.bfloat16)
    grad_out_w = inner_rows(attended_b, grad_mixed)
    grad_att = outer_rows(grad_mixed, enc_weights[3]).reshape(row_count, HEADS, HEAD)
    grad_values = jnp.einsum("phs,phe->pshe", soft_weights, grad_att, precision=exact_mode)
    along_val = jnp.einsum("phe,pshe->phs", grad_att, values, precision=exact_mode)
    base_dot = jnp.sum(grad_att * attended, axis=-1, keepdims=True)
    grad_logits = soft_weights * (along_val - base_dot) * HEAD ** (-0.5)
    grad_keys = jnp.einsum("phs,phe->pshe", grad_logits, cls_query, precision=exact_mode)
    grad_query = jnp.einsum("phs,pshe->phe", grad_logits, pass_keys, precision=exact_mode).reshape(
        row_count, model_width
    )
    flat_rows = states.reshape(row_count * length, model_width)
    grad_key_w = inner_rows(
        flat_rows, grad_keys.reshape(row_count * length, model_width).astype(jnp.bfloat16)
    )
    grad_value_w = inner_rows(
        flat_rows, grad_values.reshape(row_count * length, model_width).astype(jnp.bfloat16)
    )
    grad_query_w = inner_rows(states[:, 0, :], grad_query.astype(jnp.bfloat16))
    return jnp.stack([grad_query_w, grad_key_w, grad_value_w, grad_out_w])


def pool_local(flat_pass, mask_rows, agg_weights, agg_cls):
    doc_count, slot_count = mask_rows.shape
    cls_row = agg_cls[None, :]
    cls_query = jnp.dot(cls_row, agg_weights[0], preferred_element_type=jnp.float32).reshape(
        HEADS, HEAD
    )
    cls_key = jnp.dot(cls_row, agg_weights[1], preferred_element_type=jnp.float32).reshape(
        HEADS, HEAD
    )
    cls_value = jnp.dot(cls_row, agg_weights[2], preferred_element_type=jnp.float32).reshape(
        HEADS, HEAD
    )
    pass_keys = jnp.dot(flat_pass, agg_weights[1], preferred_element_type=jnp.float32).reshape(
        doc_count, slot_count, HEADS, HEAD
    )
    values = jnp.dot(flat_pass, agg_weights[2], preferred_element_type=jnp.float32).reshape(
        doc_count, slot_count, HEADS, HEAD
    )
    valid_keys = (mask_rows != 0)[:, None, :]
    logits = jnp.einsum("he,pshe->phs", cls_query, pass_keys, precision=exact_mode) * HEAD ** (-0.5)
    logits = jnp.where(valid_keys, logits, -1e30)
    peak_local = jnp.max(logits, axis=-1)
    raw_weights = jnp.where(valid_keys, jnp.exp(logits - peak_local[..., None]), 0.0)
    total_local = jnp.sum(raw_weights, axis=-1)
    sums_local = jnp.einsum("phs,pshe->phe", raw_weights, values, precision=exact_mode).reshape(
        doc_count, HEADS * HEAD
    )
    extras = (cls_query, cls_key, cls_value, pass_keys, values, logits, valid_keys)
    return ((peak_local, total_local, sums_local), extras)


def pool_finish(merged, extras, agg_weights, agg_gain, agg_cls, head_vector, score_bias):
    peak_m, total_m, sums_m = merged
    cls_query, cls_key, cls_value, pass_keys, values, logits, valid_keys = extras
    doc_count = peak_m.shape[0]
    cls_logit = jnp.sum(cls_query * cls_key, axis=-1) * HEAD ** (-0.5)
    peak_val = jnp.maximum(peak_m, cls_logit[None, :])
    factor = jnp.exp(peak_m - peak_val)
    cls_raw = jnp.exp(cls_logit[None, :] - peak_val)
    totals = total_m * factor + cls_raw
    pooled = (
        sums_m.reshape(doc_count, HEADS, HEAD) * factor[..., None]
        + cls_raw[..., None] * cls_value[None]
    ) / totals[..., None]
    soft_weights = (
        jnp.where(valid_keys, jnp.exp(logits - peak_val[..., None]), 0.0) / totals[..., None]
    )
    cls_prob = cls_raw / totals
    pooled_b = pooled.reshape(doc_count, HEADS * HEAD).astype(jnp.bfloat16)
    mixed_rows = agg_cls.astype(jnp.float32)[None, :] + jnp.dot(
        pooled_b, agg_weights[3], preferred_element_type=jnp.float32
    )
    normal_out, normed, rscale = layer_norm(mixed_rows, agg_gain)
    score_rows = score_bias + jnp.sum(normal_out * head_vector[None, :], axis=-1)
    saved = (
        cls_query,
        cls_key,
        cls_value,
        pass_keys,
        values,
        soft_weights,
        cls_prob,
        pooled,
        pooled_b,
        normed,
        rscale,
    )
    return (score_rows, saved)


def pool_back(grad_score, saved, flat_pass, agg_weights, agg_gain, agg_cls, head_vector, lead_flag):
    (
        cls_query,
        cls_key,
        cls_value,
        pass_keys,
        values,
        soft_weights,
        cls_prob,
        pooled,
        pooled_b,
        normed,
        rscale,
    ) = saved
    doc_count, slot_count = (soft_weights.shape[0], soft_weights.shape[2])
    model_width = flat_pass.shape[1]
    scale_qk = HEAD ** (-0.5)
    grad_out = grad_score[:, None] * head_vector[None, :]
    grad_mixed = norm_back(grad_out, agg_gain, normed, rscale).astype(jnp.bfloat16)
    grad_out_w = inner_rows(pooled_b, grad_mixed) * lead_flag
    grad_pool = outer_rows(grad_mixed, agg_weights[3]).reshape(doc_count, HEADS, HEAD)
    base_dot = jnp.sum(grad_pool * pooled, axis=-1)
    grad_values = jnp.einsum("phs,phe->pshe", soft_weights, grad_pool, precision=exact_mode)
    along_val = jnp.einsum("phe,pshe->phs", grad_pool, values, precision=exact_mode)
    grad_logits = soft_weights * (along_val - base_dot[..., None]) * scale_qk
    grad_keys = jnp.einsum("phs,he->pshe", grad_logits, cls_query, precision=exact_mode)
    cls_grad_value = cls_prob[..., None] * grad_pool
    cls_grad_logit = (
        cls_prob * (jnp.sum(grad_pool * cls_value[None], axis=-1) - base_dot) * scale_qk
    )
    cls_grad_key = cls_grad_logit[..., None] * cls_query[None]
    grad_query = jnp.einsum(
        "phs,pshe->he", grad_logits, pass_keys, precision=exact_mode
    ) + lead_flag * jnp.einsum("ph,he->he", cls_grad_logit, cls_key, precision=exact_mode)
    cls_float = agg_cls.astype(jnp.float32)
    key_rows = grad_keys.reshape(doc_count * slot_count, model_width).astype(jnp.bfloat16)
    value_rows = grad_values.reshape(doc_count * slot_count, model_width).astype(jnp.bfloat16)
    query_vector = grad_query.reshape(model_width)
    grad_query_w = cls_float[:, None] * query_vector[None, :]
    grad_key_w = (
        inner_rows(flat_pass, key_rows)
        + lead_flag
        * cls_float[:, None]
        * jnp.sum(cls_grad_key, axis=0).reshape(model_width)[None, :]
    )
    grad_value_w = (
        inner_rows(flat_pass, value_rows)
        + lead_flag
        * cls_float[:, None]
        * jnp.sum(cls_grad_value, axis=0).reshape(model_width)[None, :]
    )
    grad_pass = outer_rows(key_rows, agg_weights[1]) + outer_rows(value_rows, agg_weights[2])
    factors = (query_vector, pooled_b, grad_mixed)
    return ((grad_query_w, grad_key_w, grad_value_w, grad_out_w), grad_pass, factors)


def combine_pool(left_part, right_part):
    peak_one, total_one, sums_one = left_part
    peak_two, total_two, sums_two = right_part
    peak_new = jnp.maximum(peak_one, peak_two)
    factor_one = jnp.exp(peak_one - peak_new)
    factor_two = jnp.exp(peak_two - peak_new)
    row_count, head_count = peak_new.shape
    merged_sums = (
        sums_one.reshape(row_count, head_count, -1) * factor_one[..., None]
        + sums_two.reshape(row_count, head_count, -1) * factor_two[..., None]
    )
    return (
        peak_new,
        total_one * factor_one + total_two * factor_two,
        merged_sums.reshape(sums_one.shape),
    )


def reduce_grads(stacked):
    return lax.psum_scatter(stacked, ("psg", "doc"), scatter_dimension=1, tiled=True)


def per_device(
    hidden,
    token_ids,
    passage_mask,
    labels,
    enc_weights,
    enc_gain,
    agg_weights,
    agg_gain,
    agg_cls,
    head_vector,
    score_bias,
):
    query_count, cand_count, slot_count, length, model_width = hidden.shape
    doc_count = query_count * cand_count
    flat_width = model_width * model_width
    states = hidden.reshape(doc_count * slot_count, length, model_width)
    flat_pass, enc_saved = encode(
        states, token_ids.reshape(doc_count * slot_count, length), enc_weights, enc_gain
    )
    local_stats, extras = pool_local(
        flat_pass, passage_mask.reshape(doc_count, slot_count), agg_weights, agg_cls
    )
    merged = merged_2(local_stats, "psg", combine_pool)
    score_rows, saved = pool_finish(
        merged, extras, agg_weights, agg_gain, agg_cls, head_vector, score_bias
    )
    scores = score_rows.reshape(query_count, cand_count)
    cand_index = lax.axis_index("doc") * cand_count + jnp.arange(cand_count, dtype=jnp.int32)
    label_hits = (labels[:, None] == cand_index[None, :]).astype(jnp.float32)
    all_scores = lax.all_gather(scores, "doc", axis=1, tiled=True)
    peak_val = jnp.max(all_scores, axis=1)
    totals = jnp.sum(jnp.exp(all_scores - peak_val[:, None]), axis=1)
    every_hits = (
        labels[:, None] == jnp.arange(all_scores.shape[1], dtype=jnp.int32)[None, :]
    ).astype(jnp.float32)
    label_score = jnp.sum(all_scores * every_hits, axis=1)
    list_loss = jnp.mean(jnp.log(totals) + peak_val - label_score)
    grad_score = (jnp.exp(scores - peak_val[:, None]) / totals[:, None] - label_hits) / query_count
    lead_flag = (lax.axis_index("psg") == 0).astype(jnp.float32)
    agg_parts, grad_pass, factors = pool_back(
        grad_score.reshape(doc_count),
        saved,
        flat_pass,
        agg_weights,
        agg_gain,
        agg_cls,
        head_vector,
        lead_flag,
    )
    enc_grads = encode_back(states, enc_saved, grad_pass, enc_weights, enc_gain)
    stacked = jnp.concatenate([enc_grads, jnp.stack(agg_parts)]).reshape(8, flat_width)
    shares = reduce_grads(stacked)
    return (scores, list_loss, shares.reshape(2, 4, -1))


def solution(mesh):
    placed = (
        P(None, "doc", "psg", None, None),
        P(None, "doc", "psg", None),
        P(None, "doc", "psg"),
        P(),
        P(),
        P(),
        P(),
        P(),
        P(),
        P(),
        P(),
    )
    return jax.shard_map(
        per_device,
        mesh=mesh,
        in_specs=placed,
        out_specs=(P(None, "doc"), P(), P(None, None, ("psg", "doc"))),
        check_vma=False,
    )
```

profile of v0, /device:TPU:2, one launch (start us, length us, event | category | flops | bytes accessed | tf_op | source)
XLA Modules:
  0.0 796.9 jit_solution(16984377847974502435)
XLA Ops:
  13.4 3.7 fusion.116
  17.1 2.4 copy.130
  25.2 4.3 fusion.115
  31.1 2.9 copy.190
  35.8 5.0 fusion.121
  40.9 2.6 fusion.120
  43.5 5.4 fusion.51
  49.9 10.0 %fusion.49 = f32[16,12,1,64]{3,2,1,0:T(1,128)S(1)} fusion(f32[16,128,12,64]{1,3,2,0:T(8,128)S(1)} %fusion.121, f32[16,12,128,1]{2,0,1,3:T(8,128)S(1)} %fusion.159), kind=kOutput, calls=%fused_computation.63 | convolution fusion | flops 18874368 | bytes 6438912 | tf_op jit(solution)/shard_map/phs,pshe->phe/dot_general | solution.py:72
  75.3 13.8 %all-gather = f32[64,12]{1,0:T(8,128)} all-gather(f32[8,12]{1,0:T(8,128)S(1)} %bitcast_reduce_fusion), channel_id=2, replica_groups=mesh['psg'=8,'doc'=32] {'psg'}, dimensions={0}, use_global_device_ids=true | all-gather | bytes 3456 | tf_op jit(solution)/shard_map/all_gather | solution.py:14
  93.5 3.8 copy.200
  103.4 12.5 %all-gather.1 = f32[64,12]{1,0:T(8,128)S(1)} all-gather(f32[8,12]{1,0:T(8,128)S(1)} %copy-done.44), channel_id=3, replica_groups=mesh['psg'=8,'doc'=32] {'psg'}, dimensions={0}, use_global_device_ids=true | all-gather | bytes 3456 | tf_op jit(solution)/shard_map/all_gather | solution.py:14
  116.9 12.8 %all_gather.22 = f32[8,8,768]{2,1,0:T(8,128)S(1)} all-gather(f32[1,8,768]{2,1,0:T(8,128)S(1)} %all_gather_reshape.3), channel_id=1, replica_groups=mesh['psg'=8,'doc'=32] {'psg'}, dimensions={0}, use_global_device_ids=true | all-gather | bytes 221184 | tf_op jit(solution)/shard_map/all_gather | solution.py:14
  129.7 7.8 while.19
  144.2 42.0 %all-gather.2 = f32[32,1,8]{2,1,0:T(1,128)S(1)} all-gather(f32[1,1,8]{2,1,0:T(1,128)S(1)} %fusion.100), channel_id=1, replica_groups=mesh['psg'=8,'doc'=32] {'doc'}, dimensions={0}, use_global_device_ids=true | all-gather | bytes 1056 | tf_op jit(solution)/shard_map/all_gather | solution.py:285
  189.1 2.6 multiply_reduce_fusion.2
  226.6 7.5 fusion.47
  234.3 11.9 %fusion.45 = bf16[16,12,1,64]{3,2,1,0:T(2,128)(2,1)S(1)} fusion(f32[16,128,12,64]{1,3,2,0:T(8,128)} %copy-done, f32[16,12,128,1]{2,0,1,3:T(8,128)S(1)} %bitcast.351), kind=kOutput, calls=%fused_computation.59 | convolution fusion | flops 18874368 | bytes 6414336 | tf_op jit(solution)/shard_map/phs,pshe->phe/dot_general | solution.py:93
  246.3 5.5 copy.199
  253.7 3.2 copy.150
  256.9 5.6 copy.194
  262.4 3.9 copy.204
  266.9 3.8 copy.202
  271.2 4.0 copy.203
  275.4 4.0 copy.201
  281.4 4.0 fusion.13
  287.5 3.8 copy.198
  293.3 4.0 fusion.10
  297.3 2.3 copy.152
  299.6 3.8 copy.196
  303.4 2.5 mul.420
  305.9 49.3 %concatenate.25 = f32[8,589824]{1,0:T(8,128)} concatenate(f32[1,589824]{1,0:T(1,128)} %bitcast.330, f32[1,589824]{1,0:T(1,128)} %bitcast.335, f32[1,589824]{1,0:T(1,128)} %bitcast.334, f32[1,589824]{1,0:T(1,128)} %bitcast.329, f32[1,589824]{1,0:T(1,128)S(1)} %mul.420, f32[1,589824]{1,0:T(1,128)} %bitcast.332, f32[1,589824]{1,0:T(1,128)} %bitcast.333, f32[1,589824]{1,0:T(1,128)} %bitcast.331), dimensions={0} | concatenate | bytes 37748736 | tf_op jit(solution)/shard_map/concatenate | solution.py:306
  355.9 431.2 %reduce-scatter.2.cloned.1.call-done = f32[8,2304]{1,0:T(8,128)} async-done(((f32[8,589824]{1,0:T(8,128)}), f32[8,2304]{1,0:T(8,128)}) %reduce-scatter.2.cloned.1.call-update) | async-done | bytes 73744 | tf_op jit(solution)/shard_map/reduce_scatter | solution.py:252
  (279 shorter events, 104.6 us)
Async XLA Ops:
  7.2 780.0 %reduce-scatter.2.cloned.1.call-start = ((), (), s32[]{:S(2)}) async-start(), calls=%async_computation.1 | async-start | bytes 18948096 | tf_op jit(solution)/shard_map/reduce_scatter | solution.py:252
  7.9 26.1 %copy-start.32 = (bf16[768,1,1]{0,1,2:T(2,128)(2,1)}, bf16[768,1,1]{0,1,2:T(2,128)(2,1)S(1)}, u32[]{:S(2)}) copy-start(bf16[768,1,1]{0,1,2:T(2,128)(2,1)S(1)} %reshape.272) | copy-start | bytes 4612
  35.8 5.0 copy-start.31
  35.8 5.1 copy-start.7
  35.8 5.1 copy-start.59
  40.8 9.1 %copy-start.1 = (f32[16,128,12,64]{1,3,2,0:T(8,128)}, f32[16,128,12,64]{1,3,2,0:T(8,128)S(1)}, u32[]{:S(2)}) copy-start(f32[16,128,12,64]{1,3,2,0:T(8,128)S(1)} %fusion.121) | copy-start | bytes 18874372
  43.5 5.4 copy-start
  43.5 5.4 copy-start.57
  49.2 10.8 %copy-start.26 = (f32[16,12]{0,1:T(8,128)}, f32[16,12]{0,1:T(8,128)S(1)}, u32[]{:S(2)}) copy-start(f32[16,12]{0,1:T(8,128)S(1)} %get-tuple-element.235) | copy-start | bytes 2308
  64.5 4.6 copy-start.45
  65.1 4.0 copy-start.53
  99.2 4.2 copy-start.44
  99.2 16.7 %copy-start.40 = (f32[8,12,2,1]{1,2,0,3:T(2,128)S(1)}, f32[8,12,2,1]{1,2,0,3:T(2,128)}, u32[]{:S(2)}) copy-start(f32[8,12,2,1]{1,2,0,3:T(2,128)} %get-tuple-element.227) | copy-start | bytes 2308
  102.7 41.0 %copy-start.24 = (f32[8,2,12,64]{3,0,2,1:T(8,128)}, f32[8,2,12,64]{3,0,2,1:T(8,128)S(1)}, u32[]{:S(2)}) copy-start(f32[8,2,12,64]{3,0,2,1:T(8,128)S(1)} %fusion.79) | copy-start | bytes 147460
  102.7 39.3 %copy-start.34 = (f32[768]{0:T(1024)S(1)}, f32[768]{0:T(1024)}, u32[]{:S(2)}) copy-start(f32[768]{0:T(1024)} %convert_element_type.80) | copy-start | bytes 9220
  129.7 14.2 %copy-start.36 = (f32[768]{0:T(1024)S(1)}, f32[768]{0:T(1024)}, u32[]{:S(2)}) copy-start(f32[768]{0:T(1024)} %param.22) | copy-start | bytes 9220
  129.7 14.2 %copy-start.37 = (f32[768]{0:T(1024)S(1)}, f32[768]{0:T(1024)}, u32[]{:S(2)}) copy-start(f32[768]{0:T(1024)} %param.20) | copy-start | bytes 9220
  129.7 56.6 %copy-start.58 = (s32[8]{0:T(128)S(1)}, s32[8]{0:T(128)}, u32[]{:S(2)}) copy-start(s32[8]{0:T(128)} %param.16) | copy-start | bytes 100
  143.7 44.0 %copy-start.15 = (f32[8,768]{1,0:T(8,128)}, f32[8,768]{1,0:T(8,128)S(1)}, u32[]{:S(2)}) copy-start(f32[8,768]{1,0:T(8,128)S(1)} %get-tuple-element.240) | copy-start | bytes 73732
  143.7 43.9 %copy-start.47 = (f32[8]{0:T(128)}, f32[8]{0:T(128)S(1)}, u32[]{:S(2)}) copy-start(f32[8]{0:T(128)S(1)} %broadcast_multiply_fusion.3) | copy-start | bytes 100
  143.9 43.7 %copy-start.55 = (f32[8]{0:T(128)}, f32[8]{0:T(128)S(1)}, u32[]{:S(2)}) copy-start(f32[8]{0:T(128)S(1)} %add_rsqrt_fusion) | copy-start | bytes 100
  186.3 6.1 copy-start.25
  214.1 8.3 %copy-start.46 = (f32[16]{0:T(128)S(1)}, f32[16]{0:T(128)}, u32[]{:S(2)}) copy-start(f32[16]{0:T(128)} %copy-done.45) | copy-start | bytes 196
  214.1 8.3 %copy-start.54 = (f32[16]{0:T(128)S(1)}, f32[16]{0:T(128)}, u32[]{:S(2)}) copy-start(f32[16]{0:T(128)} %copy-done.53) | copy-start | bytes 196
  218.7 5.6 copy-start.12
  226.6 7.5 copy-start.9
  226.6 7.5 copy-start.27
  246.3 5.5 copy-start.19
  262.4 3.9 copy-start.35
  262.4 3.9 copy-start.43
  271.2 4.0 copy-start.41
  275.4 4.0 copy-start.18
  (31 other events, 76.0 us)
Sparse Core Ops, SparseCore 0:
  355.4 431.7 reduce-scatter.1
where the time goes:
time: 807 us; the launch traced here: 797 us
  waiting for transfers between devices  431 us (53%)
  local copies, waits for them, and re-layouts  151 us (19%)
  matrix products  81.5 us (10%)
  blocking collectives  81.1 us (10%)
  other arithmetic  33.9 us (4%)
  between operations  17.6 us (2%)
    reduce_scatter x1, waiting for transfers between devices, reduce_grads(): lax.psum_scatter(stacked, ('psg', 'doc'), scatter_dimension=1, tiled=True)  431 us
    concatenate x1, local copies, waits for them, and re-layouts, per_device(): jnp.concatenate([enc_grads, jnp.stack(agg_parts)]).reshape(8, flat_width)  49.3 us
    unnamed x137, local copies, waits for them, and re-layouts  46 us
    all_gather x1, blocking collectives, per_device(): all_scores = lax.all_gather(scores, 'doc', axis=1, tiled=True)  42 us
    all_gather x3, blocking collectives, merged_2(): everything = jax.tree.map(lambda part: lax.all_gather(part, axis), array)  39 us
  transfers between devices with their start and end apart: 1, of which 1 were waited for; matrix products, arithmetic and copies ran while one was open for 0% of the time, Pallas kernels for 0%

commit v1 on v0

v1 whole, which is shorter than its diff:
```python
import jax
import jax.numpy as jnp
from jax import lax
from jax.experimental import pallas as pl
from jax.experimental.pallas import tpu as pltpu
from jax.sharding import PartitionSpec as P

HEADS = 12
HEAD = 64
D = 768
SEQ = 128
QUERIES = 8
SLOTS = 2
LOCAL = QUERIES * SLOTS
PSG_DEV = 8
DOC_DEV = 32
GROUP = PSG_DEV * LOCAL
ROWS = D // PSG_DEV
SHARE = ROWS // DOC_DEV
PAD_HEADS = 16
PAY = 120
SCALE = HEAD ** (-0.5)
VMEM_LIMIT = 56 * 1024 * 1024

f32 = jnp.float32
bf16 = jnp.bfloat16


def dot_nn(a, b):
    return lax.dot_general(a, b, (((1,), (0,)), ((), ())), preferred_element_type=f32)


def dot_nt(a, b):
    return lax.dot_general(a, b, (((1,), (1,)), ((), ())), preferred_element_type=f32)


def dot_tn(a, b):
    return lax.dot_general(a, b, (((0,), (0,)), ((), ())), preferred_element_type=f32)


def halves(x):
    hi = x.astype(bf16)
    lo = (x - hi.astype(f32)).astype(bf16)
    return hi, lo


def two_part(dot, x, w):
    n = x.shape[0]
    both = dot(jnp.concatenate(halves(x), axis=0), w)
    return both[:n] + both[n:]


def iota(shape, dim):
    return lax.broadcasted_iota(jnp.int32, shape, dim)


def head_mask():
    return iota((PAD_HEADS, D), 0) == (iota((PAD_HEADS, D), 1) >> 6)


def spread(rows, mask):
    n = rows.shape[0]
    wide = jnp.where(mask[None], rows[:, None, :], 0.0)
    return wide.reshape(n * PAD_HEADS, D)


def fold(rows, mask):
    n = rows.shape[0] // PAD_HEADS
    wide = jnp.where(mask[None], rows.reshape(n, PAD_HEADS, D), 0.0)
    return jnp.sum(wide, axis=1)


def norm_parts(x):
    center = x - jnp.mean(x, axis=-1, keepdims=True)
    rscale = lax.rsqrt(jnp.mean(center * center, axis=-1, keepdims=True) + 1e-05)
    return center * rscale, rscale


def norm_back(grad_out, gain, normed, rscale):
    grad_norm = grad_out * gain
    return rscale * (
        grad_norm
        - jnp.mean(grad_norm, axis=-1, keepdims=True)
        - normed * jnp.mean(grad_norm * normed, axis=-1, keepdims=True)
    )


def pick_rows(first):
    r = iota((ROWS, D), 0)
    want = first + SHARE * (r & (DOC_DEV - 1)) + (r >> 5)
    return jnp.where(iota((ROWS, D), 1) == want, 1.0, 0.0).astype(bf16)


def forward_kernel(
    hid_ref, ids_ref, mask_ref, far_ref, pay_ref, soft_ref, z_ref, h0_s, z_s, we_ref, sems
):
    loads = [pltpu.make_async_copy(far_ref.at[n], we_ref.at[n], sems.at[n]) for n in range(3)]
    for load in loads:
        load.start()
    order = [(q, sl) for sl in range(SLOTS) for q in range(QUERIES)]
    for p, (q, sl) in enumerate(order):
        h0_s[p : p + 1, :] = hid_ref[q, sl, 0:16, :].astype(f32)[0:1, :]
    mask = head_mask()
    h0 = h0_s[...].astype(bf16)
    loads[0].wait()
    query = dot_nn(h0, we_ref[0]) * SCALE
    loads[1].wait()
    qk = two_part(dot_nt, spread(query, mask), we_ref[1])
    qk_hi, qk_lo = halves(qk)
    logits, valid = [], []
    for p, (q, sl) in enumerate(order):
        at = slice(p * PAD_HEADS, (p + 1) * PAD_HEADS)
        both = dot_nt(jnp.concatenate([qk_hi[at], qk_lo[at]], axis=0), hid_ref[q, sl])
        logits.append(both[:PAD_HEADS] + both[PAD_HEADS:])
        valid.append(jnp.broadcast_to(ids_ref[q, sl : sl + 1, :], (PAD_HEADS, SEQ)))
    logits = jnp.concatenate(logits, axis=0)
    valid = jnp.concatenate(valid, axis=0) != 0
    logits = jnp.where(valid, logits, -1e30)
    peak = jnp.max(logits, axis=-1, keepdims=True)
    raw = jnp.where(valid, jnp.exp(logits - peak), 0.0)
    soft = raw / jnp.sum(raw, axis=-1, keepdims=True)
    soft_ref[...] = soft
    soft_hi, soft_lo = halves(soft)
    z_all = []
    for p, (q, sl) in enumerate(order):
        at = slice(p * PAD_HEADS, (p + 1) * PAD_HEADS)
        both = dot_nn(jnp.concatenate([soft_hi[at], soft_lo[at]], axis=0), hid_ref[q, sl])
        z = both[:PAD_HEADS] + both[PAD_HEADS:]
        z_all.append(z)
        for c in range(D // 128):
            z_s[c, pl.ds(p, PAD_HEADS, stride=LOCAL), :] = z[:, c * 128 : (c + 1) * 128]
    z_all = jnp.concatenate(z_all, axis=0)
    for c in range(D // 128):
        z_ref[:, c * 128 : (c + 1) * 128] = z_s[c, : HEADS * LOCAL, :].astype(bf16)
    loads[2].wait()
    attended = fold(two_part(dot_nn, z_all, we_ref[2]), mask).astype(bf16)
    keep = mask_ref[...]
    keep = jnp.concatenate(
        [jnp.broadcast_to(keep[:, sl : sl + 1], (QUERIES, 128)) for sl in range(SLOTS)], axis=0
    )
    keep = jnp.where(keep != 0, 1.0, 0.0).astype(bf16)
    row = jnp.concatenate([h0, attended, keep], axis=1)
    for i in range(PSG_DEV):
        pay_ref[i] = row


def backward_kernel(
    got_ref,
    hid_ref,
    soft_ref,
    z_ref,
    we_ref,
    gain_e_ref,
    wa_ref,
    gain_a_ref,
    cls_ref,
    head_ref,
    bias_ref,
    score_ref,
    pay_ref,
    query_ref,
    gatt_ref,
    gmix_ref,
    zagg_ref,
    pooled_ref,
    small_ref,
    m_ref,
    u_s,
):
    me = lax.axis_index("psg")
    mask = head_mask()
    got = got_ref[...].reshape(GROUP, 2 * D + 128)
    h0 = got[:, :D]
    att = got[:, D : 2 * D]
    keep = got[:, 2 * D :]
    query_ref[...] = dot_nn(h0, we_ref[0])
    gain_e = gain_e_ref[...]
    gain_a = gain_a_ref[...]
    head = head_ref[...]
    cls_b = cls_ref[...]
    cls_f = cls_b.astype(f32)
    normed_e, rscale_e = norm_parts(h0.astype(f32) + dot_nn(att, we_ref[3]))
    passage = (normed_e * gain_e).astype(bf16)

    cls_8 = jnp.broadcast_to(cls_f, (QUERIES, D)).astype(bf16)
    cls_query = dot_nn(cls_8, wa_ref[0])
    kq = two_part(dot_nt, jnp.where(mask, cls_query[0:1], 0.0), wa_ref[1])
    logit = two_part(dot_nt, kq, passage) * SCALE
    cls_logit = jnp.sum(kq * cls_f, axis=-1, keepdims=True) * SCALE
    lane_one = jnp.where(iota((16, 128), 1) == 0, 1.0, 0.0).astype(bf16)
    present = dot_nt(lane_one, keep)
    shape3 = (QUERIES, PAD_HEADS, GROUP)
    valid = ((iota(shape3, 2) & (QUERIES - 1)) == iota(shape3, 0)) & (present[None] > 0.5)
    logit3 = jnp.where(valid, logit[None], -1e30)
    peak = jnp.maximum(jnp.max(logit3, axis=-1, keepdims=True), cls_logit[None])
    raw = jnp.where(valid, jnp.exp(logit3 - peak), 0.0)
    cls_raw = jnp.exp(cls_logit[None] - peak)
    total = jnp.sum(raw, axis=-1, keepdims=True) + cls_raw
    soft = (raw / total).reshape(QUERIES * PAD_HEADS, GROUP)
    cls_prob = (cls_raw / total).reshape(QUERIES * PAD_HEADS, 1)
    zagg = two_part(dot_nn, soft, passage) + cls_prob * cls_f
    zagg_ref[...] = zagg.astype(bf16)
    pooled = fold(two_part(dot_nn, zagg, wa_ref[2]), mask)
    pooled_b = jnp.concatenate([pooled, jnp.zeros_like(pooled)], axis=0).astype(bf16)
    pooled_ref[...] = pooled_b
    mixed_a = cls_f + dot_nn(pooled_b, wa_ref[3])[:QUERIES]
    normed_a, rscale_a = norm_parts(mixed_a)
    score = bias_ref[0, 0] + jnp.sum(normed_a * gain_a * head, axis=-1, keepdims=True)
    score = jnp.broadcast_to(score, (QUERIES, 128))
    for j in range(DOC_DEV):
        score_ref[j] = score

    gmix_a = norm_back(jnp.broadcast_to(head, (QUERIES, D)), gain_a, normed_a, rscale_a)
    gmix_a16 = jnp.concatenate([gmix_a, jnp.zeros_like(gmix_a)], axis=0).astype(bf16)
    gpool = dot_nt(gmix_a16, wa_ref[3])[:QUERIES]
    gpv = two_part(dot_nt, spread(gpool, mask), wa_ref[2])
    base = jnp.sum(gpv * zagg, axis=-1, keepdims=True)
    along = two_part(dot_nt, gpv, passage)
    glogit = soft * (along - base) * SCALE
    cls_glogit = cls_prob * (jnp.sum(gpv * cls_f, axis=-1, keepdims=True) - base) * SCALE
    m = two_part(dot_nn, glogit, passage) + cls_glogit * cls_f
    m_ref[...] = m
    small_ref[0] = gpool
    small_ref[1] = gmix_a
    small_ref[2] = fold(two_part(dot_nn, m, wa_ref[1]), mask)
    small_ref[3] = cls_query
    kq_wide = jnp.broadcast_to(kq[None], (QUERIES, PAD_HEADS, D)).reshape(QUERIES * PAD_HEADS, D)
    left = jnp.concatenate([glogit, soft], axis=0).astype(bf16)
    right = jnp.concatenate([kq_wide, gpv], axis=0).astype(bf16)
    gpass = dot_tn(left, right)

    gmix_e = norm_back(gpass, gain_e, normed_e, rscale_e)
    gmix_ref[...] = gmix_e
    gatt_ref[...] = dot_nt(gmix_e.astype(bf16), we_ref[3])
    mine = gatt_ref[pl.ds(pl.multiple_of(me * LOCAL, LOCAL), LOCAL), :]
    wv = two_part(dot_nt, spread(mine, mask), we_ref[2])
    wv_hi, wv_lo = halves(wv)
    order = [(q, sl) for sl in range(SLOTS) for q in range(QUERIES)]
    along_e = []
    for p, (q, sl) in enumerate(order):
        at = slice(p * PAD_HEADS, (p + 1) * PAD_HEADS)
        both = dot_nt(jnp.concatenate([wv_hi[at], wv_lo[at]], axis=0), hid_ref[q, sl])
        along_e.append(both[:PAD_HEADS] + both[PAD_HEADS:])
    along_e = jnp.concatenate(along_e, axis=0)
    soft_e = soft_ref[...]
    base_e = jnp.sum(soft_e * along_e, axis=-1, keepdims=True)
    gl_hi, gl_lo = halves(soft_e * (along_e - base_e) * SCALE)
    u_all = []
    for p, (q, sl) in enumerate(order):
        at = slice(p * PAD_HEADS, (p + 1) * PAD_HEADS)
        both = dot_nn(jnp.concatenate([gl_hi[at], gl_lo[at]], axis=0), hid_ref[q, sl])
        u = both[:PAD_HEADS] + both[PAD_HEADS:]
        u_all.append(u)
        for c in range(D // 128):
            u_s[c, pl.ds(p, PAD_HEADS, stride=LOCAL), :] = u[:, c * 128 : (c + 1) * 128]
    u_all = jnp.concatenate(u_all, axis=0)
    gquery = fold(two_part(dot_nn, u_all, we_ref[1]), mask).astype(bf16)
    u_rows = jnp.concatenate([u_s[c, : HEADS * LOCAL, :] for c in range(D // 128)], axis=1).astype(bf16)
    zu = jnp.concatenate([z_ref[...], u_rows[128:], u_rows[:128]], axis=0)
    for i in range(PSG_DEV):
        pay_ref[i, :ROWS, :] = dot_nt(pick_rows(ROWS * i), zu).astype(bf16)
        pay_ref[i, ROWS : ROWS + 16, :] = gquery[:, : D // 2]
        pay_ref[i, ROWS + 16 :, :] = gquery[:, D // 2 :]


def weights_kernel(
    all_ref,
    own_ref,
    labels_ref,
    recv_ref,
    got_ref,
    query_ref,
    gatt_ref,
    gmix_ref,
    zagg_ref,
    pooled_ref,
    small_ref,
    m_ref,
    pay_ref,
    loss_ref,
    out_s,
):
    me = lax.axis_index("psg")
    doc = lax.axis_index("doc")
    everything = all_ref[...]
    labels = jnp.broadcast_to(labels_ref[...], (QUERIES, 128))
    peak = jnp.max(everything, axis=0)
    total = jnp.sum(jnp.exp(everything - peak[None]), axis=0)
    hits = iota((DOC_DEV, QUERIES, 128), 0) == labels[None]
    label_score = jnp.sum(jnp.where(hits, everything, 0.0), axis=0)
    losses = jnp.log(total) + peak - label_score
    loss_ref[...] = jnp.sum(losses[:, 0:1], axis=0, keepdims=True) / QUERIES
    own_hit = jnp.where(labels == doc, 1.0, 0.0)
    g8 = (jnp.exp(own_ref[0] - peak) / total - own_hit) / QUERIES
    g8 = jnp.broadcast_to(g8[:, 0:1], (QUERIES, D))
    g16 = jnp.concatenate([g8, g8], axis=0)
    g_group = jnp.concatenate([g16] * PSG_DEV, axis=0)
    g_heads = jnp.broadcast_to(g8[:, None, :], (QUERIES, PAD_HEADS, D)).reshape(QUERIES * PAD_HEADS, D)
    mask = head_mask()

    def put(at, rows):
        for k in range(SHARE):
            for c in range(D // 128):
                out_s[pl.ds(at + k * (D // 128) + c, DOC_DEV, stride=PAY), :] = rows[
                    k * DOC_DEV : (k + 1) * DOC_DEV, c * 128 : (c + 1) * 128
                ]

    pick = pick_rows(me * ROWS)
    got = got_ref[...].reshape(GROUP, 2 * D + 128)
    gq = jnp.concatenate(
        [
            jnp.concatenate([recv_ref[s, ROWS : ROWS + 16, :], recv_ref[s, ROWS + 16 :, :]], axis=1)
            for s in range(PSG_DEV)
        ],
        axis=0,
    )
    h0_t = dot_nt(pick, got[:, :D]).astype(bf16)
    put(0, dot_nn(h0_t, (gq.astype(f32) * g_group).astype(bf16)))
    att_t = dot_nt(pick, got[:, D : 2 * D]).astype(bf16)
    put(54, dot_nn(att_t, (gmix_ref[...] * g_group).astype(bf16)))
    key_head = iota((16, D), 0)
    key_head = jnp.where(key_head < 4, -1, jnp.where(key_head < 8, key_head + 4, key_head - 8))
    key_mask = key_head == (iota((16, D), 1) >> 6)
    gk = jnp.zeros((ROWS, D), f32)
    gv = jnp.zeros((ROWS, D), f32)
    for s in range(PSG_DEV):
        at = slice(s * LOCAL, (s + 1) * LOCAL)
        q_rows = query_ref[at, :] * g16
        a_rows = gatt_ref[at, :] * g16
        q_wide = jnp.where(key_mask[:, None, :], q_rows[None], 0.0).reshape(16 * LOCAL, D)
        a_wide = jnp.where(mask[:, None, :], a_rows[None], 0.0).reshape(16 * LOCAL, D)
        gv = gv + dot_nn(recv_ref[s, :ROWS, :256], a_wide.astype(bf16))
        gk = gk + dot_nn(recv_ref[s, :ROWS, 128:], q_wide.astype(bf16))
    put(18, gk)
    put(36, gv)
    za_t = dot_nt(pick, zagg_ref[...]).astype(bf16)
    put(72, dot_nn(za_t, spread(small_ref[0] * g8, mask).astype(bf16)))
    pooled_t = dot_nt(pick, pooled_ref[...]).astype(bf16)
    gmix_a = small_ref[1] * g8
    gmix_a = jnp.concatenate([gmix_a, jnp.zeros_like(gmix_a)], axis=0).astype(bf16)
    put(90, dot_nn(pooled_t, gmix_a))
    qvec = jnp.sum(small_ref[2] * g8, axis=0, keepdims=True)
    for c in range(D // 128):
        out_s[pl.ds(108 + c, DOC_DEV, stride=PAY), :] = jnp.broadcast_to(
            qvec[:, c * 128 : (c + 1) * 128], (DOC_DEV, 128)
        )
    m_sum = jnp.sum((m_ref[...] * g_heads).reshape(QUERIES, PAD_HEADS, D), axis=0)
    m_tile = jnp.concatenate([m_sum] * 8, axis=0)
    m_hi, m_lo = halves(m_tile)
    m_t = dot_nt(pick, m_hi) + dot_nt(pick, m_lo)
    lane_k = iota((DOC_DEV, 128), 1) >> 4
    m_row = jnp.zeros((DOC_DEV, 128), f32)
    for k in range(SHARE):
        m_row = jnp.where(lane_k == k, m_t[k * DOC_DEV : (k + 1) * DOC_DEV], m_row)
    out_s[pl.ds(114, DOC_DEV, stride=PAY), :] = m_row
    for r in range(115, PAY):
        out_s[pl.ds(r, DOC_DEV, stride=PAY), :] = jnp.zeros((DOC_DEV, 128), f32)
    pay_ref[...] = out_s[...].astype(bf16).reshape(DOC_DEV, PAY, 128)


def finish_kernel(recv_ref, small_ref, cls_ref, out_ref):
    first = lax.axis_index("psg") * ROWS + lax.axis_index("doc") * SHARE
    total = recv_ref[0].astype(f32)
    for j in range(1, DOC_DEV):
        total = total + recv_ref[j].astype(f32)
    place = {0: (0, 0), 18: (0, 1), 36: (0, 2), 54: (0, 3), 72: (1, 2), 90: (1, 3)}
    for at, (layer, proj) in place.items():
        for r in range(18):
            out_ref[layer, proj : proj + 1, r * 128 : (r + 1) * 128] = total[at + r : at + r + 1, :]
    cls_f = cls_ref[...].astype(f32)
    m_row = jnp.broadcast_to(total[114:115, :], (16, 128))
    m_row = jnp.where((iota((16, 128), 1) >> 4) == iota((16, 128), 0), m_row, 0.0)
    expand = (iota((128, D), 0) & (PAD_HEADS - 1)) == (iota((128, D), 1) >> 6)
    expand = jnp.where(expand, 1.0, 0.0).astype(bf16)
    m_wide = two_part(dot_nn, m_row, expand)
    keys = m_wide * small_ref[3, 0:1, :]
    for k in range(SHARE):
        value = jnp.sum(jnp.where(iota((1, D), 1) == first + k, cls_f, 0.0), axis=-1, keepdims=True)
        for c in range(D // 128):
            lanes = slice(k * D + c * 128, k * D + (c + 1) * 128)
            out_ref[1, 0:1, lanes] = value * total[108 + c : 109 + c, :]
            out_ref[1, 1:2, lanes] = keys[k : k + 1, c * 128 : (c + 1) * 128]


def call(kernel, out_shape, scratch, specs, *operands):
    return pl.pallas_call(
        kernel,
        out_shape=out_shape,
        in_specs=specs,
        scratch_shapes=scratch,
        compiler_params=pltpu.CompilerParams(vmem_limit_bytes=VMEM_LIMIT),
        name=kernel.__name__,
    )(*operands)


def per_device(
    hidden,
    token_ids,
    passage_mask,
    labels,
    enc_weights,
    enc_gain,
    agg_weights,
    agg_gain,
    agg_cls,
    head_vector,
    score_bias,
):
    shape = jax.ShapeDtypeStruct
    whole = pl.BlockSpec(memory_space=pltpu.VMEM)
    scalar = pl.BlockSpec(memory_space=pltpu.SMEM)
    states = hidden.reshape(QUERIES, SLOTS, SEQ, D)
    width = 2 * D + 128
    pay_1, soft, z_rows = call(
        forward_kernel,
        (
            shape((PSG_DEV, LOCAL, width), bf16),
            shape((LOCAL * PAD_HEADS, SEQ), f32),
            shape((HEADS * LOCAL, D), bf16),
        ),
        [
            pltpu.VMEM((LOCAL, D), f32),
            pltpu.VMEM((D // 128, LOCAL * PAD_HEADS, 128), f32),
            pltpu.VMEM((3, D, D), bf16),
            pltpu.SemaphoreType.DMA((3,)),
        ],
        [whole, whole, whole, pl.BlockSpec(memory_space=pl.ANY)],
        states,
        token_ids.reshape(QUERIES, SLOTS, SEQ),
        passage_mask.reshape(QUERIES, SLOTS),
        enc_weights,
    )
    got = lax.all_to_all(pay_1, "psg", 0, 0, tiled=True)
    score, pay_2, query, gatt, gmix, zagg, pooled, small, m = call(
        backward_kernel,
        (
            shape((DOC_DEV, QUERIES, 128), f32),
            shape((PSG_DEV, ROWS + 32, 2 * HEADS * LOCAL), bf16),
            shape((GROUP, D), f32),
            shape((GROUP, D), f32),
            shape((GROUP, D), f32),
            shape((QUERIES * PAD_HEADS, D), bf16),
            shape((16, D), bf16),
            shape((4, QUERIES, D), f32),
            shape((QUERIES * PAD_HEADS, D), f32),
        ),
        [pltpu.VMEM((D // 128, LOCAL * PAD_HEADS, 128), f32)],
        [whole] * 10 + [scalar],
        got,
        states,
        soft,
        z_rows,
        enc_weights,
        enc_gain.reshape(1, D),
        agg_weights,
        agg_gain.reshape(1, D),
        agg_cls.reshape(1, D),
        head_vector.reshape(1, D),
        score_bias.reshape(1, 1),
    )
    everything = lax.all_to_all(score, "doc", 0, 0, tiled=True)
    recv = lax.all_to_all(pay_2, "psg", 0, 0, tiled=True)
    pay_3, loss = call(
        weights_kernel,
        (shape((DOC_DEV, PAY, 128), bf16), shape((1, 1), f32)),
        [pltpu.VMEM((DOC_DEV * PAY, 128), f32)],
        [whole] * 12,
        everything,
        score,
        labels.reshape(QUERIES, 1),
        recv,
        got,
        query,
        gatt,
        gmix,
        zagg,
        pooled,
        small,
        m,
    )
    shares = lax.all_to_all(pay_3, "doc", 0, 0, tiled=True)
    grads = call(
        finish_kernel,
        shape((2, 4, SHARE * D), f32),
        [],
        [whole] * 3,
        shares,
        small,
        agg_cls.reshape(1, D),
    )
    return (score[0, :, 0:1], loss.reshape(()), grads)


def solution(mesh):
    placed = (
        P(None, "doc", "psg", None, None),
        P(None, "doc", "psg", None),
        P(None, "doc", "psg"),
        P(),
        P(),
        P(),
        P(),
        P(),
        P(),
        P(),
        P(),
    )
    return jax.shard_map(
        per_device,
        mesh=mesh,
        in_specs=placed,
        out_specs=(P(None, "doc"), P(), P(None, None, ("psg", "doc"))),
        check_vma=False,
    )
```

time: 807 us -> 119 us (0.15); the launches traced: 797 us -> 117 us
  waiting for transfers between devices: 431 us -> 41.6 us
  local copies, waits for them, and re-layouts: 151 us -> 8.43 us
  matrix products: 81.5 us -> 0 us
  blocking collectives: 81.1 us -> 21.3 us
  other arithmetic: 33.9 us -> 0 us
  Pallas kernels: 0 us -> 30.2 us
  between operations: 17.6 us -> 1.35 us
  starting transfers between devices: 0.04 us -> 14.5 us
    reduce_scatter x1 -> x0, waiting for transfers between devices: 431 us -> none  [reduce_grads(): lax.psum_scatter(stacked, ('psg', 'doc'), scatter_dimension=1, tiled=True)]
    dot_general x29 -> x0, matrix products: 81.5 us -> none  [the longest x7 14.3 us: inner_rows(): lax.dot_general(left, right, (((0,), (0,)), ((), ())), preferred_element_...]
    all_gather x4 -> x0, blocking collectives: 81.1 us -> none  [the longest x1 42 us: per_device(): all_scores = lax.all_gather(scores, 'doc', axis=1, tiled=True)]
    concatenate x1 -> x0, local copies, waits for them, and re-layouts: 49.3 us -> none  [per_device(): jnp.concatenate([enc_grads, jnp.stack(agg_parts)]).reshape(8, flat_width)]
    unnamed x137 -> x16, local copies, waits for them, and re-layouts: 46 us -> 2.71 us
    all_to_all x0 -> x3, waiting for transfers between devices: none -> 41.6 us  [the longest x1 25.7 us: per_device(): shares = lax.all_to_all(pay_3, 'doc', 0, 0, tiled=True)]
    pallas_call x0 -> x4, Pallas kernels: none -> 30.2 us  [call(): pl.pallas_call(kernel, out_shape=out_shape, in_specs=specs, scratch_shape...]
    dot_general x19 -> x0, local copies, waits for them, and re-layouts: 21.4 us -> none  [the longest x3 7.51 us: inner_rows(): lax.dot_general(left, right, (((0,), (0,)), ((), ())), preferred_element_...]
  transfers between devices with their start and end apart: 1 -> 3, of which waited for: 1 -> 3; matrix products, arithmetic and copies ran while one was open for 0% -> 4% of each run, Pallas kernels for 0% -> 0%
where the time goes in v1:
time: 119 us; the launch traced here: 117 us
  waiting for transfers between devices  41.6 us (35%)
  Pallas kernels  30.2 us (25%)
  blocking collectives  21.3 us (18%)
  starting transfers between devices  14.5 us (12%)
  local copies, waits for them, and re-layouts  8.43 us (7%)
  between operations  1.35 us (1%)
    pallas_call x4, Pallas kernels, call(): pl.pallas_call(kernel, out_shape=out_shape, in_specs=specs, scratch_shape...  30.2 us
    all_to_all x1, waiting for transfers between devices, per_device(): shares = lax.all_to_all(pay_3, 'doc', 0, 0, tiled=True)  25.7 us
    all_to_all x1, blocking collectives, per_device(): everything = lax.all_to_all(score, 'doc', 0, 0, tiled=True)  21.3 us
    all_to_all x1, waiting for transfers between devices, per_device(): recv = lax.all_to_all(pay_2, 'psg', 0, 0, tiled=True)  11 us
    all_to_all x1, starting transfers between devices, per_device(): got = lax.all_to_all(pay_1, 'psg', 0, 0, tiled=True)  5.65 us
    all_to_all x1, starting transfers between devices, per_device(): recv = lax.all_to_all(pay_2, 'psg', 0, 0, tiled=True)  4.92 us
    all_to_all x1, waiting for transfers between devices, per_device(): got = lax.all_to_all(pay_1, 'psg', 0, 0, tiled=True)  4.82 us
    all_to_all x1, starting transfers between devices, per_device(): shares = lax.all_to_all(pay_3, 'doc', 0, 0, tiled=True)  3.93 us
  transfers between devices with their start and end apart: 3, of which 3 were waited for; matrix products, arithmetic and copies ran while one was open for 4% of the time, Pallas kernels for 0%

profile of v1, /device:TPU:2, one launch (start us, length us, event | category | flops | bytes accessed | tf_op | source)
XLA Modules:
  0.0 117.4 jit_solution(3215116141035331118)
XLA Ops:
  0.6 0.0 copy-start.6
  0.6 0.0 copy-start.3
  0.7 0.0 copy-start.4
  0.7 0.0 copy-start.5
  0.7 1.4 %copy.16.mask_ref = s32[8,2]{1,0:T(8,128)} copy(s32[8,2]{0,1:T(2,128)} %bitcast.11) | data formatting | bytes 128 | tf_op jit(solution)/shard_map/reshape | solution.py:430
  2.0 8.0 %forward_kernel.1 = (bf16[8,16,1664]{2,1,0:T(8,128)(2,1)}, f32[256,128]{1,0:T(8,128)}, bf16[192,768]{1,0:T(8,128)(2,1)}) custom-call(bf16[8,2,128,768]{3,2,1,0:T(8,128)(2,1)} %bitcast.8, s32[8,2,128]{2,1,0:T(2,128)} %bitcast.10, s32[8,2]{1,0:T(8,128)} %copy.16.mask_ref, bf16[4,768,768]{2,1,0:T(8,128)(2,1)} %we_ref.1), custom_call_target="tpu_custom_call" | custom-call | tf_op jit(solution)/shard_map/forward_kernel/pallas_call | solution.py:386
  10.0 5.7 %all-to-all-start = ((bf16[8,16,1664]{2,1,0:T(8,128)(2,1)}), bf16[8,16,1664]{2,1,0:T(8,128)(2,1)S(1)}, u32[]{:S(2)}, u32[]{:S(2)}) async-start(bf16[8,16,1664]{2,1,0:T(8,128)(2,1)} %get-tuple-element.17), calls=%async_computation | async-start | bytes 851968 | tf_op jit(solution)/shard_map/all_to_all | solution.py:433
  15.7 0.0 copy-done.6
  15.7 0.6 reshape.42.cls_ref
  16.3 0.0 copy-done.3
  16.3 0.6 reshape.40.gain_e_ref
  16.9 0.0 copy-done.4
  16.9 0.6 reshape.41.gain_a_ref
  17.5 0.0 copy-done.5
  17.5 0.6 reshape.43.head_ref
  18.7 4.8 %all-to-all-done.got_ref = bf16[8,16,1664]{2,1,0:T(8,128)(2,1)S(1)} async-done(((bf16[8,16,1664]{2,1,0:T(8,128)(2,1)}), bf16[8,16,1664]{2,1,0:T(8,128)(2,1)S(1)}, u32[]{:S(2)}, u32[]{:S(2)}) %all-to-all-start) | async-done | bytes 426016 | tf_op jit(solution)/shard_map/all_to_all | solution.py:433
  23.5 0.0 copy-start.1
  23.5 0.8 copy-done.1
  24.3 0.0 copy-start.7
  24.3 15.1 %backward_kernel.1 = (f32[32,8,128]{2,1,0:T(8,128)}, bf16[8,128,384]{2,1,0:T(8,128)(2,1)}, f32[128,768]{1,0:T(8,128)}, f32[128,768]{1,0:T(8,128)}, f32[128,768]{...) custom-call(bf16[8,16,1664]{2,1,0:T(8,128)(2,1)} %copy-done.1, ...), custom_call_target="tpu_custom_call" | custom-call | tf_op jit(solution)/shard_map/backward_kernel/pallas_call | solution.py:386
  39.5 21.3 %all_to_all.20.all_ref = f32[32,8,128]{2,1,0:T(8,128)} all-to-all(f32[32,8,128]{2,1,0:T(8,128)} %get-tuple-element.20.own_ref), channel_id=1, replica_groups=mesh['psg'=8,'doc'=32] {'doc'}, dimensions={0} | all-to-all | bytes 262144 | tf_op jit(solution)/shard_map/all_to_all | solution.py:461
  60.8 4.9 %all-to-all-start.2 = ((bf16[8,128,384]{2,1,0:T(8,128)(2,1)}), bf16[8,128,384]{2,1,0:T(8,128)(2,1)S(1)}, u32[]{:S(2)}, u32[]{:S(2)}) async-start(bf16[8,128,384]{2,1,0:T(8,128)(2,1)} %get-tuple-element.21), calls=%async_computation.2 | async-start | bytes 1572864 | tf_op jit(solution)/shard_map/all_to_all | solution.py:462
  65.7 0.0 copy-done.7
  65.7 0.7 copy.17.labels_ref
  66.4 11.0 %all-to-all-done.2.recv_ref = bf16[8,128,384]{2,1,0:T(8,128)(2,1)S(1)} async-done(((bf16[8,128,384]{2,1,0:T(8,128)(2,1)}), bf16[8,128,384]{2,1,0:T(8,128)(2,1)S(1)}, u32[]{:S(2)}, u32[]{:S(2)}) %all-to-all-start.2) | async-done | bytes 786464 | tf_op jit(solution)/shard_map/all_to_all | solution.py:462
  77.4 0.9 copy-done.2
  78.4 5.0 %weights_kernel.1 = (bf16[32,120,128]{2,1,0:T(8,128)(2,1)}, f32[1,1]{1,0:T(1,128)}) custom-call(f32[32,8,128]{2,1,0:T(8,128)} %all_to_all.20.all_ref, f32[32,8,128]{2,1,0:T(8,128)} %get-tuple-element.20.own_ref, s32[8,1]{1,0:T(8,128)} %copy.17.labels_ref, bf16[8,128,384]{2,1,0:T(8,128)(2,1)} %copy-done.2, bf16[8,16,1664]{2,1,0:T(8,128)(2,1)} %copy-done.1, ...), custom_call_target="tpu_custom_call" | custom-call | tf_op jit(solution)/shard_map/weights_kernel/pallas_call | solution.py:386
  83.4 3.9 %all-to-all-start.3 = ((bf16[32,120,128]{2,1,0:T(8,128)(2,1)}), bf16[32,120,128]{2,1,0:T(8,128)(2,1)S(1)}, u32[]{:S(2)}, u32[]{:S(2)}) async-start(bf16[32,120,128]{2,1,0:T(8,128)(2,1)} %get-tuple-element.30), calls=%async_computation.3 | async-start | bytes 1966080 | tf_op jit(solution)/shard_map/all_to_all | solution.py:481
  87.3 1.3 %slice_reduce_fusion = f32[8]{0:T(128)} fusion(f32[32,8,128]{2,1,0:T(8,128)} %get-tuple-element.20.own_ref), kind=kLoop, calls=%fused_computation | loop fusion | bytes 64 | tf_op jit(solution)/shard_map/slice | solution.py:491
  88.6 25.7 %all-to-all-done.3.recv_ref = bf16[32,120,128]{2,1,0:T(8,128)(2,1)S(1)} async-done(((bf16[32,120,128]{2,1,0:T(8,128)(2,1)}), bf16[32,120,128]{2,1,0:T(8,128)(2,1)S(1)}, u32[]{:S(2)}, u32[]{:S(2)}) %all-to-all-start.3) | async-done | bytes 983072 | tf_op jit(solution)/shard_map/all_to_all | solution.py:481
  114.3 0.9 copy-done
  115.3 2.1 %finish_kernel.1 = f32[2,4,2304]{2,1,0:T(4,128)} custom-call(bf16[32,120,128]{2,1,0:T(8,128)(2,1)} %copy-done, f32[4,8,768]{2,1,0:T(8,128)} %get-tuple-element.27.small_ref, bf16[1,768]{1,0:T(2,128)(2,1)} %reshape.42.cls_ref), custom_call_target="tpu_custom_call" | custom-call | tf_op jit(solution)/shard_map/finish_kernel/pallas_call | solution.py:386
  (2 shorter events, 0.0 us)
Async XLA Ops:
  0.6 15.0 %copy-start.6 = (bf16[768]{0:T(1024)(128)(2,1)S(1)}, bf16[768]{0:T(1024)(128)(2,1)}, u32[]{:S(2)}) copy-start(bf16[768]{0:T(1024)(128)(2,1)} %param.19) | copy-start | bytes 4612
  0.6 15.6 %copy-start.3 = (f32[768]{0:T(1024)S(1)}, f32[768]{0:T(1024)}, u32[]{:S(2)}) copy-start(f32[768]{0:T(1024)} %param.16) | copy-start | bytes 9220
  0.7 16.2 %copy-start.4 = (f32[768]{0:T(1024)S(1)}, f32[768]{0:T(1024)}, u32[]{:S(2)}) copy-start(f32[768]{0:T(1024)} %param.18) | copy-start | bytes 9220
  0.7 16.8 %copy-start.5 = (f32[768]{0:T(1024)S(1)}, f32[768]{0:T(1024)}, u32[]{:S(2)}) copy-start(f32[768]{0:T(1024)} %param.20) | copy-start | bytes 9220
  10.0 13.5 %all-to-all-start = ((bf16[8,16,1664]{2,1,0:T(8,128)(2,1)}), bf16[8,16,1664]{2,1,0:T(8,128)(2,1)S(1)}, u32[]{:S(2)}, u32[]{:S(2)}) async-start(bf16[8,16,1664]{2,1,0:T(8,128)(2,1)} %get-tuple-element.17), calls=%async_computation | async-start | bytes 851968 | tf_op jit(solution)/shard_map/all_to_all | solution.py:433
  23.5 0.8 copy-start.1
  24.3 41.4 %copy-start.7 = (s32[8]{0:T(128)S(1)}, s32[8]{0:T(128)}, u32[]{:S(2)}) copy-start(s32[8]{0:T(128)} %param.14) | copy-start | bytes 100
  60.8 16.6 %all-to-all-start.2 = ((bf16[8,128,384]{2,1,0:T(8,128)(2,1)}), bf16[8,128,384]{2,1,0:T(8,128)(2,1)S(1)}, u32[]{:S(2)}, u32[]{:S(2)}) async-start(bf16[8,128,384]{2,1,0:T(8,128)(2,1)} %get-tuple-element.21), calls=%async_computation.2 | async-start | bytes 1572864 | tf_op jit(solution)/shard_map/all_to_all | solution.py:462
  77.4 0.9 copy-start.2
  83.4 31.0 %all-to-all-start.3 = ((bf16[32,120,128]{2,1,0:T(8,128)(2,1)}), bf16[32,120,128]{2,1,0:T(8,128)(2,1)S(1)}, u32[]{:S(2)}, u32[]{:S(2)}) async-start(bf16[32,120,128]{2,1,0:T(8,128)(2,1)} %get-tuple-element.30), calls=%async_computation.3 | async-start | bytes 1966080 | tf_op jit(solution)/shard_map/all_to_all | solution.py:481
  114.3 0.9 copy-start

commit v2 on v1

v2 whole, which is shorter than its diff:
```python
import jax
import jax.numpy as jnp
from jax import lax
from jax.experimental import pallas as pl
from jax.experimental.pallas import tpu as pltpu
from jax.sharding import PartitionSpec as P

HEADS = 12
HEAD = 64
D = 768
SEQ = 128
QUERIES = 8
SLOTS = 2
LOCAL = QUERIES * SLOTS
PSG_DEV = 8
DOC_DEV = 32
GROUP = PSG_DEV * LOCAL
ROWS = D // PSG_DEV
SHARE = ROWS // DOC_DEV
PAD_HEADS = 16
SCALE = HEAD ** (-0.5)

f32 = jnp.float32
bf16 = jnp.bfloat16


def dot_nn(a, b):
    return lax.dot_general(a, b, (((1,), (0,)), ((), ())), preferred_element_type=f32)


def dot_nt(a, b):
    return lax.dot_general(a, b, (((1,), (1,)), ((), ())), preferred_element_type=f32)


def dot_tn(a, b):
    return lax.dot_general(a, b, (((0,), (0,)), ((), ())), preferred_element_type=f32)


def halves(x):
    hi = x.astype(bf16)
    lo = (x - hi.astype(f32)).astype(bf16)
    return hi, lo


def two_part(dot, x, w):
    n = x.shape[0]
    both = dot(jnp.concatenate(halves(x), axis=0), w)
    return both[:n] + both[n:]


def iota(shape, dim):
    return lax.broadcasted_iota(jnp.int32, shape, dim)


def head_mask():
    return iota((PAD_HEADS, D), 0) == (iota((PAD_HEADS, D), 1) >> 6)


def spread(rows, mask):
    n = rows.shape[0]
    wide = jnp.where(mask[None], rows[:, None, :], 0.0)
    return wide.reshape(n * PAD_HEADS, D)


def fold(rows, mask):
    n = rows.shape[0] // PAD_HEADS
    wide = jnp.where(mask[None], rows.reshape(n, PAD_HEADS, D), 0.0)
    return jnp.sum(wide, axis=1)


QUAD = 4 * HEAD


def quad_mask():
    return iota((4, 1, QUAD), 0) == (iota((4, 1, QUAD), 2) >> 6)


def images(rows, w):
    n = rows.shape[0]
    parts = []
    for at in range(0, D, QUAD):
        wide = jnp.where(quad_mask(), rows[None, :, at : at + QUAD], 0.0).reshape(4 * n, QUAD)
        parts.append(two_part(dot_nt, wide, w[:, at : at + QUAD]))
    return jnp.concatenate(parts, axis=0)


def head_sums(rows, w):
    n = rows.shape[0] // HEADS
    parts = []
    for g, at in enumerate(range(0, D, QUAD)):
        out = two_part(dot_nn, rows[4 * n * g : 4 * n * (g + 1)], w[:, at : at + QUAD])
        parts.append(jnp.sum(jnp.where(quad_mask(), out.reshape(4, n, QUAD), 0.0), axis=0))
    return jnp.concatenate(parts, axis=1)


def norm_parts(x):
    center = x - jnp.mean(x, axis=-1, keepdims=True)
    rscale = lax.rsqrt(jnp.mean(center * center, axis=-1, keepdims=True) + 1e-05)
    return center * rscale, rscale


def norm_back(grad_out, gain, normed, rscale):
    grad_norm = grad_out * gain
    return rscale * (
        grad_norm
        - jnp.mean(grad_norm, axis=-1, keepdims=True)
        - normed * jnp.mean(grad_norm * normed, axis=-1, keepdims=True)
    )


def pick_rows(first):
    r = iota((ROWS, D), 0)
    want = first + SHARE * (r & (DOC_DEV - 1)) + (r >> 5)
    return jnp.where(iota((ROWS, D), 1) == want, 1.0, 0.0).astype(bf16)


def column(row):
    n = row.shape[1]
    wide = jnp.broadcast_to(row, (QUERIES, n))
    hit = iota((QUERIES, n), 0) == iota((QUERIES, n), 1)
    return jnp.sum(jnp.where(hit, wide, jnp.zeros_like(wide)), axis=1, keepdims=True)


def pack_columns(rows):
    half = ROWS // 2
    out = dot_nt(jnp.concatenate([pick_rows(ROWS * i) for i in range(PSG_DEV)], axis=0), rows)
    rest = out[:, 128:]
    high = [
        jnp.concatenate([rest[at : at + half], rest[at + half : at + ROWS]], axis=1)
        for at in range(0, D, ROWS)
    ]
    return out[:, :128].astype(bf16), jnp.concatenate(high, axis=0).astype(bf16)


def unpack_columns(low, high):
    both = jnp.concatenate([high, high], axis=0)
    keep = (iota((ROWS, 128), 0) < ROWS // 2) == (iota((ROWS, 128), 1) < 64)
    both = jnp.where(keep, both, jnp.zeros_like(both))
    return jnp.concatenate([low, both], axis=1)


def head_rows(rows):
    shape = (16, 1, D)
    head = iota(shape, 0)
    head = jnp.where(head < HEADS, head, head - 4)
    keep = head == (iota(shape, 2) >> 6)
    return jnp.where(keep, rows[None], jnp.zeros_like(rows)[None]).reshape(16 * LOCAL, D)


def put(out_s, at, rows, pay):
    for k in range(SHARE):
        for c in range(D // 128):
            out_s[pl.ds(at + k * (D // 128) + c, DOC_DEV, stride=pay), :] = rows[
                k * DOC_DEV : (k + 1) * DOC_DEV, c * 128 : (c + 1) * 128
            ]


def heads_at(p):
    return slice(p * PAD_HEADS, (p + 1) * PAD_HEADS)


def to_scratch(rows, scratch):
    for c in range(D // 128):
        scratch[c, : HEADS * LOCAL, :] = rows[:, c * 128 : (c + 1) * 128]
        scratch[c, HEADS * LOCAL :, :] = jnp.zeros(((PAD_HEADS - HEADS) * LOCAL, 128), f32)


def against_rows(scratch, rows_of):
    parts = [None] * LOCAL
    for q in range(QUERIES):
        rows = rows_of(q)
        for sl in range(SLOTS):
            p = sl * QUERIES + q
            x = [scratch[c, pl.ds(p, PAD_HEADS, stride=LOCAL), :] for c in range(D // 128)]
            left = jnp.concatenate(halves(jnp.concatenate(x, axis=1)), axis=0)
            out = dot_nt(left, rows[sl * SEQ : (sl + 1) * SEQ])
            parts[p] = out[:PAD_HEADS] + out[PAD_HEADS:]
    return jnp.concatenate(parts, axis=0)


def sum_rows(x, rows_of):
    hi, lo = halves(x)
    parts = [None] * LOCAL
    blank = jnp.zeros((PAD_HEADS, SEQ), bf16)
    for q in range(QUERIES):
        a, b = heads_at(q), heads_at(QUERIES + q)
        left = [[hi[a], blank], [blank, hi[b]], [lo[a], blank], [blank, lo[b]]]
        left = jnp.concatenate([jnp.concatenate(row, axis=1) for row in left], axis=0)
        out = dot_nn(left, rows_of(q))
        parts[q] = out[0:16] + out[32:48]
        parts[QUERIES + q] = out[16:32] + out[48:64]
    return parts


def by_head(parts, scratch):
    for p, part in enumerate(parts):
        for c in range(D // 128):
            scratch[c, pl.ds(p, PAD_HEADS, stride=LOCAL), :] = part[:, c * 128 : (c + 1) * 128]
    return jnp.concatenate([scratch[c, : HEADS * LOCAL, :] for c in range(D // 128)], axis=1)


def forward_kernel(
    top_ref, w_ref, hid_ref, ids_ref, mask_ref, wv_ref, pay_ref, soft_ref, z_ref, h0_s, qk_s, z_s
):
    for sl in range(SLOTS):
        for q in range(QUERIES):
            p = sl * QUERIES + q
            h0_s[p : p + 1, :] = top_ref[q, sl].astype(f32)[0:1, :]
    h0 = h0_s[...].astype(bf16)
    query = dot_nn(h0, w_ref[0][...]) * SCALE
    to_scratch(images(query, w_ref[1].ready()), qk_s)
    rows_of = lambda q: hid_ref[q][...].reshape(SLOTS * SEQ, D)
    logits = against_rows(qk_s, rows_of)
    valid = [
        jnp.broadcast_to(ids_ref[q, sl : sl + 1, :], (PAD_HEADS, SEQ))
        for sl in range(SLOTS)
        for q in range(QUERIES)
    ]
    valid = jnp.concatenate(valid, axis=0) != 0
    logits = jnp.where(valid, logits, -1e30)
    peak = jnp.max(logits, axis=-1, keepdims=True)
    raw = jnp.where(valid, jnp.exp(logits - peak), 0.0)
    soft = raw / jnp.sum(raw, axis=-1, keepdims=True)
    soft_ref.send(soft)
    z = by_head(sum_rows(soft, rows_of), z_s)
    z_ref.send(z.astype(bf16))
    attended = head_sums(z, wv_ref[2].ready())
    keep = [
        jnp.broadcast_to(column(mask_ref[sl : sl + 1, :]), (QUERIES, 128)) for sl in range(SLOTS)
    ]
    keep = jnp.where(jnp.concatenate(keep, axis=0) != 0, 1.0, 0.0).astype(bf16)
    row = jnp.concatenate([h0, attended.astype(bf16), keep], axis=1)
    for i in range(PSG_DEV):
        pay_ref[i] = row


def class_kernel(after_ref, vec_ref, wa_ref, out_ref):
    cls_f = vec_ref[3:4, :]
    cls_8 = jnp.broadcast_to(cls_f, (QUERIES, D)).astype(bf16)
    cls_query = dot_nn(cls_8, wa_ref[0][...])
    kq = two_part(dot_nt, jnp.where(head_mask(), cls_query[0:1], 0.0), wa_ref[1][...])
    out_ref[0] = jnp.broadcast_to(cls_query[0:1], (PAD_HEADS, D))
    out_ref[1] = kq
    cls_logit = jnp.sum(kq * cls_f, axis=-1, keepdims=True) * SCALE
    out_ref[2] = jnp.broadcast_to(cls_logit, (PAD_HEADS, D))


def score_kernel(
    got_ref,
    we_ref,
    vec_ref,
    class_ref,
    wa_ref,
    score_ref,
    own_ref,
    normed_ref,
    rscale_ref,
    zagg_ref,
    soft_ref,
    small_ref,
):
    got = got_ref[...].reshape(GROUP, 2 * D + 128)
    h0 = got[:, :D]
    att = got[:, D : 2 * D]
    keep = got[:, 2 * D :]
    lane_one = jnp.where(iota((16, 128), 1) == 0, 1.0, 0.0).astype(bf16)
    present = dot_nt(lane_one, keep)[0:1]
    shape3 = (HEADS, QUERIES, GROUP)
    valid = ((iota(shape3, 2) & (QUERIES - 1)) == iota(shape3, 1)) & (present[None] > 0.5)
    normed_e, rscale_e = norm_parts(h0.astype(f32) + dot_nn(att, we_ref[3][...]))
    normed_ref.send(normed_e)
    rscale_ref.send(jnp.broadcast_to(rscale_e, (GROUP, 128)))
    passage = (normed_e * vec_ref[0:1, :]).astype(bf16)
    cls_f = vec_ref[3:4, :]
    logit = two_part(dot_nt, class_ref[1], passage)[:HEADS] * SCALE
    cls_logit = class_ref[2][:HEADS, 0:1]
    logit3 = jnp.where(valid, logit[:, None, :], -1e30)
    cls_logit = cls_logit[:, None, :]
    peak = jnp.maximum(jnp.max(logit3, axis=-1, keepdims=True), cls_logit)
    raw = jnp.where(valid, jnp.exp(logit3 - peak), 0.0)
    cls_raw = jnp.exp(cls_logit - peak)
    total = jnp.sum(raw, axis=-1, keepdims=True) + cls_raw
    soft = (raw / total).reshape(HEADS * QUERIES, GROUP)
    cls_prob = (cls_raw / total).reshape(HEADS * QUERIES, 1)
    soft_ref[0] = soft
    soft_ref[1] = jnp.broadcast_to(cls_prob, (HEADS * QUERIES, GROUP))
    soft_ref.send()
    zagg = two_part(dot_nn, soft, passage) + cls_prob * cls_f
    zagg_ref.send(zagg)
    pooled = head_sums(zagg, wa_ref[2].ready())
    small_ref[2] = pooled
    pooled_b = jnp.concatenate([pooled, jnp.zeros_like(pooled)], axis=0).astype(bf16)
    normed_a, rscale_a = norm_parts(cls_f + dot_nn(pooled_b, wa_ref[3][...])[:QUERIES])
    small_ref[0] = normed_a
    small_ref[1] = jnp.broadcast_to(rscale_a, (QUERIES, D))
    small_ref.send()
    score = jnp.sum(normed_a * vec_ref[1:2, :] * vec_ref[2:3, :], axis=-1, keepdims=True)
    score = jnp.broadcast_to(score + vec_ref[4:5, 0:1], (QUERIES, 128))
    own_ref.send(score)
    diagonal = iota((QUERIES, 128), 0) == iota((QUERIES, 128), 1)
    row = jnp.sum(jnp.where(diagonal, score, 0.0), axis=0, keepdims=True)
    for j in range(DOC_DEV):
        score_ref[j] = row


def backward_kernel(
    z_ref,
    vec_ref,
    small_ref,
    wa_ref,
    zagg_ref,
    normed_ref,
    soft_ref,
    class_ref,
    rscale_ref,
    we_ref,
    hid_ref,
    soft_e_ref,
    wk_ref,
    pay_ref,
    gatt_ref,
    gmix_ref,
    gpv_ref,
    glogit_ref,
    back_ref,
    wv_s,
    u_s,
):
    half = ROWS // 2

    def pay(at, rows):
        low, high = pack_columns(rows.astype(bf16))
        for i in range(PSG_DEV):
            pay_ref[i, at : at + ROWS, :] = low[i * ROWS : (i + 1) * ROWS]
            pay_ref[i, at + ROWS : at + ROWS + half, :] = high[i * half : (i + 1) * half]

    z_ref.ready()
    for fetched in (zagg_ref, normed_ref, soft_ref, class_ref, rscale_ref):
        fetched.begin()
    we_ref[3].begin()
    we_ref[2].begin()
    pay(0, z_ref[...])
    me = lax.axis_index("psg")
    head = jnp.broadcast_to(vec_ref[2:3, :], (QUERIES, D))
    gmix_a = norm_back(head, vec_ref[1:2, :], small_ref[0], small_ref[1][:, 0:1])
    back_ref[1] = gmix_a
    gmix_a16 = jnp.concatenate([gmix_a, jnp.zeros_like(gmix_a)], axis=0).astype(bf16)
    wa_ref[2].ready()
    for q in range(QUERIES):
        hid_ref[q].begin()
    soft_e_ref.begin()
    wk_ref[1].begin()
    gpool = dot_nt(gmix_a16, wa_ref[3][...])[:QUERIES]
    back_ref[0] = gpool
    back_ref.send()
    gpv = images(gpool, wa_ref[2].ready())
    gpv_ref.send(gpv)
    base = jnp.sum(gpv * zagg_ref[...], axis=-1, keepdims=True)
    normed_e = normed_ref[...]
    gain_e = vec_ref[0:1, :]
    passage = (normed_e * gain_e).astype(bf16)
    along = two_part(dot_nt, gpv, passage)
    soft = soft_ref[0]
    glogit = soft * (along - base) * SCALE
    glogit_ref[0] = glogit
    glogit_ref[1] = jnp.broadcast_to(base, (HEADS * QUERIES, GROUP))
    glogit_ref.send()
    kq_wide = jnp.broadcast_to(class_ref[1][:HEADS, None, :], (HEADS, QUERIES, D))
    kq_wide = kq_wide.reshape(HEADS * QUERIES, D)
    left = jnp.concatenate([glogit, soft], axis=0).astype(bf16)
    right = jnp.concatenate([kq_wide, gpv], axis=0).astype(bf16)
    gpass = dot_tn(left, right)
    gmix_e = norm_back(gpass, gain_e, normed_e, rscale_ref[:, 0:1])
    gmix_ref.send(gmix_e)
    gatt_ref.send(dot_nt(gmix_e.astype(bf16), we_ref[3][...]))
    mine = gatt_ref[pl.ds(pl.multiple_of(me * LOCAL, LOCAL), LOCAL), :]
    to_scratch(images(mine, we_ref[2].ready()), wv_s)
    rows_of = lambda q: hid_ref[q][...].reshape(SLOTS * SEQ, D)
    along_e = against_rows(wv_s, rows_of)
    soft_e = soft_e_ref[...]
    base_e = jnp.sum(soft_e * along_e, axis=-1, keepdims=True)
    u = by_head(sum_rows(soft_e * (along_e - base_e) * SCALE, rows_of), u_s)
    gquery = head_sums(u, wk_ref[1].ready()).astype(bf16)
    for i in range(PSG_DEV):
        for c in range(D // 128):
            pay_ref[i, 288 + 16 * c : 304 + 16 * c, :] = gquery[:, c * 128 : (c + 1) * 128]
    pay(144, u)


EARLY = 64
LATE = 56


def early_kernel(
    all_ref,
    own_ref,
    labels_ref,
    gatt_ref,
    gmix_ref,
    got_ref,
    zagg_ref,
    back_ref,
    small_ref,
    vec_ref,
    soft_ref,
    gpv_ref,
    glogit_ref,
    normed_ref,
    we_ref,
    wa_ref,
    pay_ref,
    loss_ref,
    g_ref,
    right_ref,
    left_ref,
    score_ref,
    out_s,
):
    diagonal = iota((QUERIES, 128), 0) == iota((QUERIES, 128), 1)
    row = jnp.sum(jnp.where(diagonal, own_ref[...], 0.0), axis=0, keepdims=True)
    score_ref[...] = row[:, :QUERIES]
    me = lax.axis_index("psg")
    doc = lax.axis_index("doc")
    everything = all_ref[...]
    labels = labels_ref[...]
    lane_labels = jnp.concatenate([labels, jnp.full((1, 120), -1, jnp.int32)], axis=1)
    peak = jnp.max(everything, axis=0)
    total = jnp.sum(jnp.exp(everything - peak[None]), axis=0)
    hits = iota((DOC_DEV, 1, 128), 0) == lane_labels[None]
    label_score = jnp.sum(jnp.where(hits, everything, 0.0), axis=0)
    losses = jnp.log(total) + peak - label_score
    losses = jnp.where(iota((1, 128), 1) < QUERIES, losses, 0.0)
    loss_ref[...] = jnp.sum(losses, axis=1, keepdims=True) / QUERIES
    own_hit = jnp.where(column(labels) == doc, 1.0, 0.0)
    g8 = (jnp.exp(own_ref[:, 0:1] - column(peak)) / column(total) - own_hit) / QUERIES
    g8 = jnp.broadcast_to(g8, (QUERIES, D))
    g16 = jnp.concatenate([g8, g8], axis=0)
    g_ref[...] = g16
    g_group = jnp.concatenate([g16] * PSG_DEV, axis=0)
    g_heads = jnp.concatenate([g8] * HEADS, axis=0)
    pick = pick_rows(me * ROWS)
    got = got_ref[...].reshape(GROUP, 2 * D + 128)
    left_ref[...] = dot_nt(pick, got[:, :D]).astype(bf16)
    right_ref[1] = (gatt_ref[...] * g_group).astype(bf16)
    att_t = dot_nt(pick, got[:, D : 2 * D]).astype(bf16)
    put(out_s, 0, dot_nn(att_t, (gmix_ref[...] * g_group).astype(bf16)), EARLY)
    zagg_t = dot_nt(pick, zagg_ref[...].astype(bf16)).astype(bf16)
    shape3 = (HEADS, 1, D)
    own_head = iota(shape3, 0) == (iota(shape3, 2) >> 6)
    gpool = jnp.where(own_head, (back_ref[0] * g8)[None], 0.0).reshape(HEADS * QUERIES, D)
    put(out_s, 18, dot_nn(zagg_t, gpool.astype(bf16)), EARLY)
    blank = jnp.zeros((120, D), f32)
    pooled = jnp.concatenate([small_ref[2], blank], axis=0).astype(bf16)
    pooled_t = dot_nt(pick, pooled).astype(bf16)
    gmix_a = jnp.concatenate([back_ref[1] * g8, blank], axis=0).astype(bf16)
    put(out_s, 36, dot_nn(pooled_t, gmix_a), EARLY)
    cls_f = vec_ref[3:4, :]
    along = jnp.sum(gpv_ref[...] * cls_f, axis=-1, keepdims=True)
    cls_glogit = soft_ref[1][:, 0:1] * (along - glogit_ref[1][:, 0:1]) * SCALE
    passage = (normed_ref[...] * vec_ref[0:1, :]).astype(bf16)
    m = two_part(dot_nn, glogit_ref[0], passage) + cls_glogit * cls_f
    m_sum = jnp.sum((m * g_heads).reshape(HEADS, QUERIES, D), axis=1)
    m_sum = jnp.concatenate([m_sum, jnp.zeros((PAD_HEADS - HEADS, D), f32)], axis=0)
    right_ref[0] = (dot_nn(got[:, :D], we_ref[0][...]) * g_group).astype(bf16)
    qvec = fold(two_part(dot_nn, m_sum, wa_ref[1][...]), head_mask())
    for c in range(D // 128):
        out_s[pl.ds(54 + c, DOC_DEV, stride=EARLY), :] = jnp.broadcast_to(
            qvec[:, c * 128 : (c + 1) * 128], (DOC_DEV, 128)
        )
    m_hi, m_lo = halves(jnp.concatenate([m_sum] * 8, axis=0))
    m_t = dot_nt(pick, m_hi) + dot_nt(pick, m_lo)
    lane_k = iota((DOC_DEV, 128), 1) >> 4
    m_row = jnp.zeros((DOC_DEV, 128), f32)
    for k in range(SHARE):
        m_row = jnp.where(lane_k == k, m_t[k * DOC_DEV : (k + 1) * DOC_DEV], m_row)
    out_s[pl.ds(60, DOC_DEV, stride=EARLY), :] = m_row
    for r in range(61, EARLY):
        out_s[pl.ds(r, DOC_DEV, stride=EARLY), :] = jnp.zeros((DOC_DEV, 128), f32)
    pay_ref[...] = out_s[...].astype(bf16).reshape(DOC_DEV, EARLY, 128)


def late_kernel(recv_ref, left_ref, right_ref, g_ref, early_ref, pay_ref, out_s):
    g16 = g_ref[...]
    gq = []
    gk = jnp.zeros((ROWS, D), f32)
    gv = jnp.zeros((ROWS, D), f32)
    for s in range(PSG_DEV):
        at = slice(s * LOCAL, (s + 1) * LOCAL)
        block = recv_ref[s]
        gv = gv + dot_nn(unpack_columns(block[:96], block[96:144]), head_rows(right_ref[1, at, :]))
        gk = gk + dot_nn(
            unpack_columns(block[144:240], block[240:288]), head_rows(right_ref[0, at, :])
        )
        parts = [block[288 + 16 * c : 304 + 16 * c] for c in range(D // 128)]
        gq.append((jnp.concatenate(parts, axis=1).astype(f32) * g16).astype(bf16))
    put(out_s, 0, dot_nn(left_ref[...], jnp.concatenate(gq, axis=0)), LATE)
    put(out_s, 18, gk, LATE)
    put(out_s, 36, gv, LATE)
    for r in range(54, LATE):
        out_s[pl.ds(r, DOC_DEV, stride=LATE), :] = jnp.zeros((DOC_DEV, 128), f32)
    late = out_s[...].astype(bf16).reshape(DOC_DEV, LATE, 128)
    pay_ref[...] = jnp.concatenate([early_ref[...], late], axis=1)


def finish_kernel(recv_ref, class_ref, vec_ref, out_ref):
    first = lax.axis_index("psg") * ROWS + lax.axis_index("doc") * SHARE
    total = recv_ref[0].astype(f32)
    for j in range(1, DOC_DEV):
        total = total + recv_ref[j].astype(f32)
    place = [
        (EARLY, 0, 0),
        (EARLY + 18, 0, 1),
        (EARLY + 36, 0, 2),
        (0, 0, 3),
        (18, 1, 2),
        (36, 1, 3),
    ]
    for at, layer, proj in place:
        for r in range(18):
            out_ref[layer, proj : proj + 1, r * 128 : (r + 1) * 128] = total[at + r : at + r + 1, :]
    cls_f = vec_ref[3:4, :]
    m_row = jnp.broadcast_to(total[60:61, :], (16, 128))
    m_row = jnp.where((iota((16, 128), 1) >> 4) == iota((16, 128), 0), m_row, 0.0)
    expand = (iota((128, D), 0) & (PAD_HEADS - 1)) == (iota((128, D), 1) >> 6)
    expand = jnp.where(expand, 1.0, 0.0).astype(bf16)
    keys = two_part(dot_nn, m_row, expand) * class_ref[0, 0:1, :]
    for k in range(SHARE):
        value = jnp.sum(jnp.where(iota((1, D), 1) == first + k, cls_f, 0.0), axis=-1, keepdims=True)
        for c in range(D // 128):
            lanes = slice(k * D + c * 128, k * D + (c + 1) * 128)
            out_ref[1, 0:1, lanes] = value * total[54 + c : 55 + c, :]
            out_ref[1, 1:2, lanes] = keys[k : k + 1, c * 128 : (c + 1) * 128]


WHOLE = pl.BlockSpec(memory_space=pltpu.VMEM)
SCALAR = pl.BlockSpec(memory_space=pltpu.SMEM)
FAR = pl.BlockSpec(memory_space=pl.ANY)


TOP = "top"


class Fetched:
    def __init__(self, src, dst, sem):
        self.copy = pltpu.make_async_copy(src, dst, sem)
        self.dst = dst
        self.started = False
        self.waiting = True

    def begin(self):
        if not self.started:
            self.copy.start()
            self.started = True

    def ready(self):
        self.begin()
        if self.waiting:
            self.copy.wait()
            self.waiting = False
        return self.dst

    def __getitem__(self, index):
        return self.ready()[index]


class Sent:
    def __init__(self, buf, dst, sem):
        self.buf = buf
        self.copy = pltpu.make_async_copy(buf, dst, sem)
        self.going = False

    def __getitem__(self, index):
        return self.buf[index]

    def __setitem__(self, index, value):
        self.buf[index] = value

    def send(self, value=None):
        if value is not None:
            self.buf[...] = value
        self.copy.start()
        self.going = True


def call(kernel, out_shape, scratch, operands, limit=56, first=99):
    single = not isinstance(out_shape, tuple)
    out_shape = (out_shape,) if single else out_shape
    specs, values, plans, buffers = [], [], [], []
    for operand in operands:
        parts = None
        spec = FAR
        if isinstance(operand, tuple):
            if isinstance(operand[0], pl.BlockSpec):
                spec, operand = operand
            else:
                operand, parts = operand
        if spec is FAR:
            operand = pltpu.with_memory_space_constraint(operand, pltpu.HBM)
            plans.append((len(values), parts))
            size = operand.shape if parts is None else (len(parts),) + operand.shape[1:]
            if parts is TOP:
                size = operand.shape[:2] + (16,) + operand.shape[3:]
            buffers.append(pltpu.VMEM(size, operand.dtype))
        specs.append(spec)
        values.append(operand)
    n_sems = sum(1 if parts in (None, TOP) else len(parts) for _, parts in plans)
    n_in, n_buf, n_out = len(values), len(buffers), len(out_shape)

    def body(*refs):
        ins = list(refs[:n_in])
        outs = refs[n_in : n_in + n_out]
        own = refs[n_in + n_out : -1 - n_buf - n_out]
        bufs = refs[-1 - n_buf - n_out : -1 - n_out]
        out_bufs = refs[-1 - n_out : -1]
        sems = refs[-1]
        started = []
        for (at, parts), buf in zip(plans, bufs):
            if parts is None or parts is TOP:
                ref = ins[at] if parts is None else ins[at].at[:, :, pl.ds(0, 16), :]
                ins[at] = Fetched(ref, buf, sems.at[len(started)])
                started.append(ins[at])
            else:
                ref, ins[at] = ins[at], {}
                for n, part in enumerate(parts):
                    ins[at][part] = Fetched(ref.at[part], buf.at[n], sems.at[len(started)])
                    started.append(ins[at][part])
        for fetched in started[:first]:
            fetched.begin()
        sent = [Sent(*both, sems.at[n_sems + n]) for n, both in enumerate(zip(out_bufs, outs))]
        kernel(*ins, *sent, *own)
        for out in sent:
            if not out.going:
                out.send()
        for fetched in started:
            fetched.ready()
        for out in sent:
            out.copy.wait()

    outs = pl.pallas_call(
        body,
        out_shape=tuple(pltpu.HBM(leaf.shape, leaf.dtype) for leaf in out_shape),
        in_specs=specs,
        out_specs=tuple(FAR for leaf in out_shape),
        scratch_shapes=list(scratch)
        + buffers
        + [pltpu.VMEM(leaf.shape, leaf.dtype) for leaf in out_shape]
        + [pltpu.SemaphoreType.DMA((n_sems + n_out,))],
        compiler_params=pltpu.CompilerParams(vmem_limit_bytes=limit * 1024 * 1024),
        name=kernel.__name__,
    )(*values)
    return outs[0] if single else outs


def per_device(
    hidden,
    token_ids,
    passage_mask,
    labels,
    enc_weights,
    enc_gain,
    agg_weights,
    agg_gain,
    agg_cls,
    head_vector,
    score_bias,
):
    shape = jax.ShapeDtypeStruct
    states = hidden.reshape(QUERIES, SLOTS, SEQ, D)
    vectors = [enc_gain, agg_gain, head_vector, agg_cls.astype(f32), jnp.full((D,), score_bias)]
    vectors = jnp.stack(vectors + [jnp.zeros((D,), f32)] * 3)
    head_scratch = pltpu.VMEM((D // 128, LOCAL * PAD_HEADS, 128), f32)
    pairs = HEADS * QUERIES
    group = shape((GROUP, D), f32)
    pay_1, soft_e, z_rows = call(
        forward_kernel,
        (
            shape((PSG_DEV, LOCAL, 2 * D + 128), bf16),
            shape((LOCAL * PAD_HEADS, SEQ), f32),
            shape((HEADS * LOCAL, D), bf16),
        ),
        [pltpu.VMEM((LOCAL, D), f32), head_scratch, head_scratch],
        (
            (states, TOP),
            (enc_weights, (0, 1)),
            (states, tuple(range(QUERIES))),
            token_ids.reshape(QUERIES, SLOTS, SEQ),
            passage_mask.transpose(1, 2, 0).reshape(SLOTS, QUERIES),
            (enc_weights, (2,)),
        ),
    )
    got = lax.all_to_all(pay_1, "psg", 0, 0, tiled=True)
    class_rows = call(
        class_kernel,
        shape((3, PAD_HEADS, D), f32),
        [],
        (z_rows, vectors, (agg_weights, (0, 1))),
    )
    score, own, normed, rscale, zagg, soft, small = call(
        score_kernel,
        (
            shape((DOC_DEV, 1, 128), f32),
            shape((QUERIES, 128), f32),
            group,
            shape((GROUP, 128), f32),
            shape((pairs, D), f32),
            shape((2, pairs, GROUP), f32),
            shape((3, QUERIES, D), f32),
        ),
        [],
        ((WHOLE, got), (enc_weights, (3,)), vectors, class_rows, (agg_weights, (2, 3))),
        limit=24,
    )
    everything = lax.all_to_all(score, "doc", 0, 0, tiled=True)
    pay_2, gatt, gmix, gpv, glogit, back = call(
        backward_kernel,
        (
            shape((PSG_DEV, 384, 128), bf16),
            group,
            group,
            shape((pairs, D), f32),
            shape((2, pairs, GROUP), f32),
            shape((2, QUERIES, D), f32),
        ),
        [head_scratch, head_scratch],
        (
            z_rows,
            vectors,
            small,
            (agg_weights, (3, 2)),
            zagg,
            normed,
            soft,
            class_rows,
            rscale,
            (enc_weights, (3, 2)),
            (states, tuple(range(QUERIES))),
            soft_e,
            (enc_weights, (1,)),
        ),
    )
    recv = lax.all_to_all(pay_2, "psg", 0, 0, tiled=True)
    early, loss, g16, right, left, scores = call(
        early_kernel,
        (
            shape((DOC_DEV, EARLY, 128), bf16),
            shape((1, 1), f32),
            shape((LOCAL, D), f32),
            shape((2, GROUP, D), bf16),
            shape((ROWS, GROUP), bf16),
            shape((1, QUERIES), f32),
        ),
        [pltpu.VMEM((DOC_DEV * EARLY, 128), f32)],
        (
            everything,
            own,
            labels.reshape(1, QUERIES),
            gatt,
            gmix,
            got,
            zagg,
            back,
            small,
            vectors,
            soft,
            gpv,
            glogit,
            normed,
            (enc_weights, (0,)),
            (agg_weights, (1,)),
        ),
    )
    pay_3 = call(
        late_kernel,
        shape((DOC_DEV, EARLY + LATE, 128), bf16),
        [pltpu.VMEM((DOC_DEV * LATE, 128), f32)],
        ((WHOLE, recv), left, right, g16, early),
        limit=24,
    )
    shares = lax.all_to_all(pay_3, "doc", 0, 0, tiled=True)
    weight_grads = call(
        finish_kernel,
        shape((2, 4, SHARE * D), f32),
        [],
        ((WHOLE, shares), class_rows, vectors),
        limit=16,
    )
    return (scores.reshape(QUERIES, 1), loss.reshape(()), weight_grads)


def solution(mesh):
    placed = (
        P(None, "doc", "psg", None, None),
        P(None, "doc", "psg", None),
        P(None, "doc", "psg"),
        P(),
        P(),
        P(),
        P(),
        P(),
        P(),
        P(),
        P(),
    )
    return jax.shard_map(
        per_device,
        mesh=mesh,
        in_specs=placed,
        out_specs=(P(None, "doc"), P(), P(None, None, ("psg", "doc"))),
        check_vma=False,
    )
```

time: 119 us -> 106 us (0.89)
  waiting for transfers between devices: 41.6 us -> 9.46 us
  blocking collectives: 21.3 us -> 36.3 us
  local copies, waits for them, and re-layouts: 8.43 us -> 0.71 us
  starting transfers between devices: 14.5 us -> 21.2 us
  Pallas kernels: 30.2 us -> 34.9 us
    all_to_all x1, waiting for transfers between devices: 25.7 us -> 0.01 us  [per_device(): everything = lax.all_to_all(score, 'doc', 0, 0, tiled=True)]
    all_to_all x1, blocking collectives: 21.3 us -> 36.3 us  [per_device(): shares = lax.all_to_all(pay_3, 'doc', 0, 0, tiled=True)]
    all_to_all x1, starting transfers between devices: 3.93 us -> 10.7 us  [per_device(): everything = lax.all_to_all(score, 'doc', 0, 0, tiled=True)]
    all_to_all x1, waiting for transfers between devices: 11 us -> 6.1 us  [per_device(): recv = lax.all_to_all(pay_2, 'psg', 0, 0, tiled=True)]
    pallas_call x4 -> x7, Pallas kernels: 30.2 us -> 34.9 us  [call(): pl.pallas_call(body, out_shape=tuple((pltpu.HBM(leaf.shape, leaf.dtype) f...]
    reshape x6 -> x0, local copies, waits for them, and re-layouts: 4.42 us -> none  [the longest x1 1.37 us: per_device(): passage_mask.reshape(QUERIES, SLOTS)]
    unnamed x16 -> x12, local copies, waits for them, and re-layouts: 2.71 us -> 0.02 us
    all_to_all x1, waiting for transfers between devices: 4.82 us -> 3.35 us  [per_device(): got = lax.all_to_all(pay_1, 'psg', 0, 0, tiled=True)]
  transfers between devices with their start and end apart: 3 -> 3, of which waited for: 3 -> 2; matrix products, arithmetic and copies ran while one was open for 4% -> 1% of each run, Pallas kernels for 0% -> 18%
where the time goes in v2:
time: 106 us; the launch traced here: 104 us
  blocking collectives  36.3 us (34%)
  Pallas kernels  34.9 us (33%)
  starting transfers between devices  21.2 us (20%)
  waiting for transfers between devices  9.46 us (9%)
  between operations  1.64 us (2%)
    all_to_all x1, blocking collectives, per_device(): shares = lax.all_to_all(pay_3, 'doc', 0, 0, tiled=True)  36.3 us
    pallas_call x7, Pallas kernels, call(): pl.pallas_call(body, out_shape=tuple((pltpu.HBM(leaf.shape, leaf.dtype) f...  34.9 us
    all_to_all x1, starting transfers between devices, per_device(): everything = lax.all_to_all(score, 'doc', 0, 0, tiled=True)  10.7 us
    all_to_all x1, waiting for transfers between devices, per_device(): recv = lax.all_to_all(pay_2, 'psg', 0, 0, tiled=True)  6.1 us
    all_to_all x1, starting transfers between devices, per_device(): got = lax.all_to_all(pay_1, 'psg', 0, 0, tiled=True)  5.66 us
    all_to_all x1, starting transfers between devices, per_device(): recv = lax.all_to_all(pay_2, 'psg', 0, 0, tiled=True)  4.93 us
    all_to_all x1, waiting for transfers between devices, per_device(): got = lax.all_to_all(pay_1, 'psg', 0, 0, tiled=True)  3.35 us
  transfers between devices with their start and end apart: 3, of which 2 were waited for; matrix products, arithmetic and copies ran while one was open for 1% of the time, Pallas kernels for 18%

profile of v2, /device:TPU:2, one launch (start us, length us, event | category | flops | bytes accessed | tf_op | source)
XLA Modules:
  0.0 104.3 jit_solution(240014398050601019)
XLA Ops:
  0.6 0.0 copy-start.2
  0.6 0.0 copy-start.3
  0.7 0.0 copy-start.5
  0.7 0.0 copy-start.4
  0.7 6.7 %forward_kernel.1 = (bf16[8,16,1664]{2,1,0:T(8,128)(2,1)}, f32[256,128]{1,0:T(8,128)}, bf16[192,768]{1,0:T(8,128)(2,1)}) custom-call(bf16[8,2,128,768]{3,2,1,0:T(8,128)(2,1)} %bitcast.8, bf16[4,768,768]{2,1,0:T(8,128)(2,1)} %refs_14_.1, bf16[8,2,128,768]{3,2,1,0:T(8,128)(2,1)} %bitcast.9, s32[8,2,128]{2,1,0:T(2,128)} %bitcast.11, s32[2,8]{1,0:T(2,128)} %bitcast.12, ...), custom_call_target="tpu_custom_call" | custom-call | tf_op jit(solution)/shard_map/forward_kernel/pallas_call | solution.py:639
  7.4 5.7 %all-to-all-start = ((bf16[8,16,1664]{2,1,0:T(8,128)(2,1)}), bf16[8,16,1664]{2,1,0:T(8,128)(2,1)S(1)}, u32[]{:S(2)}, u32[]{:S(2)}) async-start(bf16[8,16,1664]{2,1,0:T(8,128)(2,1)} %get-tuple-element.25), calls=%async_computation | async-start | bytes 851968 | tf_op jit(solution)/shard_map/all_to_all | solution.py:691
  13.7 0.0 copy-done.2
  13.7 0.0 copy-done.3
  13.7 0.0 copy-done.5
  13.7 0.0 copy-done.4
  13.8 0.7 stack.27.refs_1_.refs_2_.refs_9_
  14.4 3.1 %class_kernel.1.refs_3_.refs_7_.refs_1_ = f32[3,16,768]{2,1,0:T(8,128)} custom-call(bf16[192,768]{1,0:T(8,128)(2,1)} %get-tuple-element.26.refs_0_, f32[8,768]{1,0:T(8,128)} %stack.27.refs_1_.refs_2_.refs_9_, bf16[4,768,768]{2,1,0:T(8,128)(2,1)} %refs_15_.1), custom_call_target="tpu_custom_call" | custom-call | tf_op jit(solution)/shard_map/class_kernel/pallas_call | solution.py:639
  17.5 3.4 %all-to-all-done.refs_0_.refs_5_ = bf16[8,16,1664]{2,1,0:T(8,128)(2,1)S(1)} async-done(((bf16[8,16,1664]{2,1,0:T(8,128)(2,1)}), bf16[8,16,1664]{2,1,0:T(8,128)(2,1)S(1)}, u32[]{:S(2)}, u32[]{:S(2)}) %all-to-all-start) | async-done | bytes 426016 | tf_op jit(solution)/shard_map/all_to_all | solution.py:691
  20.9 0.0 copy-start
  20.9 4.5 %score_kernel.1 = (f32[32,1,128]{2,1,0:T(1,128)}, f32[8,128]{1,0:T(8,128)}, f32[128,768]{1,0:T(8,128)}, f32[128,128]{1,0:T(8,128)}, f32[96,768]{1,0:T(8,128)}, /...) custom-call(bf16[8,16,1664]{2,1,0:T(8,128)(2,1)S(1)} %all-to-all-done.refs_0_.refs_5_, bf16[4,768,768]{2,1,0:T(8,128)(2,1)} %refs_14_.1, ...), custom_call_target="tpu_custom_call" | custom-call | tf_op jit(solution)/shard_map/score_kernel/pallas_call | solution.py:639
  25.3 0.0 copy-done
  25.4 10.7 %all-to-all-start.1 = ((f32[32,1,128]{2,1,0:T(1,128)}), f32[32,1,128]{2,1,0:T(1,128)S(1)}, u32[]{:S(2)}, u32[]{:S(2)}) async-start(f32[32,1,128]{2,1,0:T(1,128)} %get-tuple-element.27), calls=%async_computation.1 | async-start | bytes 32768 | tf_op jit(solution)/shard_map/all_to_all | solution.py:713
  36.0 9.7 %backward_kernel.1 = (bf16[8,384,128]{2,1,0:T(8,128)(2,1)}, f32[128,768]{1,0:T(8,128)}, f32[128,768]{1,0:T(8,128)}, f32[96,768]{1,0:T(8,128)}, f32[2,96,128]{2,1,0:T(8,128)}, /*index=5*/f32[2,8,768]{2,1,0:T(8,128)}) custom-call(bf16[192,768]{1,0:T(8,128)(2,1)} %get-tuple-element.26.refs_0_, f32[8,768]{1,0:T(8,128)} %stack.27.refs_1_.refs_2_.refs_9_, ...), custom_call_target="tpu_custom_call" | custom-call | tf_op jit(solution)/shard_map/backward_kernel/pallas_call | solution.py:639
  45.7 0.0 all-to-all-done.1.refs_0_
  45.7 0.0 copy-start.1
  45.8 4.9 %all-to-all-start.2 = ((bf16[8,384,128]{2,1,0:T(8,128)(2,1)}), bf16[8,384,128]{2,1,0:T(8,128)(2,1)S(1)}, u32[]{:S(2)}, u32[]{:S(2)}) async-start(bf16[8,384,128]{2,1,0:T(8,128)(2,1)} %get-tuple-element.42), calls=%async_computation.2 | async-start | bytes 1572864 | tf_op jit(solution)/shard_map/all_to_all | solution.py:741
  50.7 0.0 copy-done.1
  50.7 5.6 %early_kernel.1 = (bf16[32,64,128]{2,1,0:T(8,128)(2,1)}, f32[1,1]{1,0:T(1,128)}, f32[16,768]{1,0:T(8,128)}, bf16[2,128,768]{2,1,0:T(8,128)(2,1)}, bf16[96,128]{1,0:T(8,128)(2,1)}, /*index=5*/f32[1,8]{1,0:T(1,128)}) custom-call(f32[32,1,128]{2,1,0:T(1,128)} %copy-done.1, f32[8,128]{1,0:T(8,128)} %get-tuple-element.28.refs_1_, s32[1,8]{1,0:T(1,128)} %bitcast.13, ...), custom_call_target="tpu_custom_call" | custom-call | tf_op jit(solution)/shard_map/early_kernel/pallas_call | solution.py:639
  56.3 6.1 %all-to-all-done.2.refs_0_ = bf16[8,384,128]{2,1,0:T(8,128)(2,1)S(1)} async-done(((bf16[8,384,128]{2,1,0:T(8,128)(2,1)}), bf16[8,384,128]{2,1,0:T(8,128)(2,1)S(1)}, u32[]{:S(2)}, u32[]{:S(2)}) %all-to-all-start.2) | async-done | bytes 786464 | tf_op jit(solution)/shard_map/all_to_all | solution.py:741
  62.4 3.6 %late_kernel.1 = bf16[32,120,128]{2,1,0:T(8,128)(2,1)} custom-call(bf16[8,384,128]{2,1,0:T(8,128)(2,1)S(1)} %all-to-all-done.2.refs_0_, bf16[96,128]{1,0:T(8,128)(2,1)} %get-tuple-element.43.refs_1_, bf16[2,128,768]{2,1,0:T(8,128)(2,1)} %get-tuple-element.44.refs_2_, f32[16,768]{1,0:T(8,128)} %get-tuple-element.45.refs_3_, ...), custom_call_target="tpu_custom_call" | custom-call | tf_op jit(solution)/shard_map/late_kernel/pallas_call | solution.py:639
  66.1 36.3 %all_to_all.20.refs_0_ = bf16[32,120,128]{2,1,0:T(8,128)(2,1)S(1)} all-to-all(bf16[32,120,128]{2,1,0:T(8,128)(2,1)} %late_kernel.1), channel_id=1, replica_groups=mesh['psg'=8,'doc'=32] {'doc'}, dimensions={0} | all-to-all | bytes 1966080 | tf_op jit(solution)/shard_map/all_to_all | solution.py:779
  102.4 1.7 %finish_kernel.1 = f32[2,4,2304]{2,1,0:T(4,128)} custom-call(bf16[32,120,128]{2,1,0:T(8,128)(2,1)S(1)} %all_to_all.20.refs_0_, f32[3,16,768]{2,1,0:T(8,128)} %class_kernel.1.refs_3_.refs_7_.refs_1_, f32[8,768]{1,0:T(8,128)} %stack.27.refs_1_.refs_2_.refs_9_), custom_call_target="tpu_custom_call" | custom-call | tf_op jit(solution)/shard_map/finish_kernel/pallas_call | solution.py:639
  (7 shorter events, 0.0 us)
Async XLA Ops:
  0.6 13.0 %copy-start.2 = (f32[768]{0:T(1024)S(1)}, f32[768]{0:T(1024)}, u32[]{:S(2)}) copy-start(f32[768]{0:T(1024)} %param.16) | copy-start | bytes 9220
  0.6 13.0 %copy-start.3 = (f32[768]{0:T(1024)S(1)}, f32[768]{0:T(1024)}, u32[]{:S(2)}) copy-start(f32[768]{0:T(1024)} %param.18) | copy-start | bytes 9220
  0.7 13.1 %copy-start.5 = (bf16[768]{0:T(1024)(128)(2,1)S(1)}, bf16[768]{0:T(1024)(128)(2,1)}, u32[]{:S(2)}) copy-start(bf16[768]{0:T(1024)(128)(2,1)} %param.19) | copy-start | bytes 4612
  0.7 13.1 %copy-start.4 = (f32[768]{0:T(1024)S(1)}, f32[768]{0:T(1024)}, u32[]{:S(2)}) copy-start(f32[768]{0:T(1024)} %param.20) | copy-start | bytes 9220
  7.4 13.5 %all-to-all-start = ((bf16[8,16,1664]{2,1,0:T(8,128)(2,1)}), bf16[8,16,1664]{2,1,0:T(8,128)(2,1)S(1)}, u32[]{:S(2)}, u32[]{:S(2)}) async-start(bf16[8,16,1664]{2,1,0:T(8,128)(2,1)} %get-tuple-element.25), calls=%async_computation | async-start | bytes 851968 | tf_op jit(solution)/shard_map/all_to_all | solution.py:691
  20.9 4.5 %copy-start = (bf16[8,16,1664]{2,1,0:T(8,128)(2,1)}, bf16[8,16,1664]{2,1,0:T(8,128)(2,1)S(1)}, u32[]{:S(2)}) copy-start(bf16[8,16,1664]{2,1,0:T(8,128)(2,1)S(1)} %all-to-all-done.refs_0_.refs_5_) | copy-start | bytes 1277956
  25.4 20.4 %all-to-all-start.1 = ((f32[32,1,128]{2,1,0:T(1,128)}), f32[32,1,128]{2,1,0:T(1,128)S(1)}, u32[]{:S(2)}, u32[]{:S(2)}) async-start(f32[32,1,128]{2,1,0:T(1,128)} %get-tuple-element.27), calls=%async_computation.1 | async-start | bytes 32768 | tf_op jit(solution)/shard_map/all_to_all | solution.py:713
  45.7 4.9 %copy-start.1 = (f32[32,1,128]{2,1,0:T(1,128)}, f32[32,1,128]{2,1,0:T(1,128)S(1)}, u32[]{:S(2)}) copy-start(f32[32,1,128]{2,1,0:T(1,128)S(1)} %all-to-all-done.1.refs_0_) | copy-start | bytes 49156
  45.8 16.7 %all-to-all-start.2 = ((bf16[8,384,128]{2,1,0:T(8,128)(2,1)}), bf16[8,384,128]{2,1,0:T(8,128)(2,1)S(1)}, u32[]{:S(2)}, u32[]{:S(2)}) async-start(bf16[8,384,128]{2,1,0:T(8,128)(2,1)} %get-tuple-element.42), calls=%async_computation.2 | async-start | bytes 1572864 | tf_op jit(solution)/shard_map/all_to_all | solution.py:741

commit v3 on v2

--- a/solution.py
+++ b/solution.py
@@ -109,8 +109,10 @@
 
 
 def pick_rows(first):
+    me = lax.axis_index("doc")
     r = iota((ROWS, D), 0)
-    want = first + SHARE * (r & (DOC_DEV - 1)) + (r >> 5)
+    place = (((r & 7) << 2) + ((r >> 3) & 3)) ^ (me & 3)
+    want = first + SHARE * place + (r >> 5)
     return jnp.where(iota((ROWS, D), 1) == want, 1.0, 0.0).astype(bf16)
 
 
@@ -408,7 +410,10 @@
     normed_ref,
     we_ref,
     wa_ref,
-    pay_ref,
+    pay_0,
+    pay_1,
+    pay_2,
+    pay_3,
     loss_ref,
     g_ref,
     right_ref,
@@ -438,8 +443,8 @@
     g_ref[...] = g16
     g_group = jnp.concatenate([g16] * PSG_DEV, axis=0)
     g_heads = jnp.concatenate([g8] * HEADS, axis=0)
+    got = got_ref[...].reshape(GROUP, 2 * D + 128)
     pick = pick_rows(me * ROWS)
-    got = got_ref[...].reshape(GROUP, 2 * D + 128)
     left_ref[...] = dot_nt(pick, got[:, :D]).astype(bf16)
     right_ref[1] = (gatt_ref[...] * g_group).astype(bf16)
     att_t = dot_nt(pick, got[:, D : 2 * D]).astype(bf16)
@@ -476,10 +481,12 @@
     out_s[pl.ds(60, DOC_DEV, stride=EARLY), :] = m_row
     for r in range(61, EARLY):
         out_s[pl.ds(r, DOC_DEV, stride=EARLY), :] = jnp.zeros((DOC_DEV, 128), f32)
-    pay_ref[...] = out_s[...].astype(bf16).reshape(DOC_DEV, EARLY, 128)
-
-
-def late_kernel(recv_ref, left_ref, right_ref, g_ref, early_ref, pay_ref, out_s):
+    out = out_s[...].astype(bf16).reshape(4, 8, EARLY, 128)
+    for n, pay_ref in enumerate((pay_0, pay_1, pay_2, pay_3)):
+        pay_ref.send(out[n])
+
+
+def late_kernel(recv_ref, left_ref, right_ref, g_ref, pay_0, pay_1, pay_2, pay_3, out_s):
     g16 = g_ref[...]
     gq = []
     gk = jnp.zeros((ROWS, D), f32)
@@ -498,15 +505,26 @@
     put(out_s, 36, gv, LATE)
     for r in range(54, LATE):
         out_s[pl.ds(r, DOC_DEV, stride=LATE), :] = jnp.zeros((DOC_DEV, 128), f32)
-    late = out_s[...].astype(bf16).reshape(DOC_DEV, LATE, 128)
-    pay_ref[...] = jnp.concatenate([early_ref[...], late], axis=1)
-
-
-def finish_kernel(recv_ref, class_ref, vec_ref, out_ref):
+    out = out_s[...].astype(bf16).reshape(4, 8, LATE, 128)
+    for n, pay_ref in enumerate((pay_0, pay_1, pay_2, pay_3)):
+        pay_ref.send(out[n])
+
+
+def middle_kernel(*refs):
+    late = [ref[...].astype(f32) for ref in refs[:4]]
+    early = [ref[...].astype(f32) for ref in refs[4:8]]
+    late = (late[0] + late[1]) + (late[2] + late[3])
+    early = (early[0] + early[1]) + (early[2] + early[3])
+    total = jnp.concatenate([early, late], axis=1).astype(bf16)
+    refs[8][...] = total
+
+
+def finish_kernel(class_ref, vec_ref, *refs):
+    out_ref = refs[-1]
     first = lax.axis_index("psg") * ROWS + lax.axis_index("doc") * SHARE
-    total = recv_ref[0].astype(f32)
-    for j in range(1, DOC_DEV):
-        total = total + recv_ref[j].astype(f32)
+    total = refs[0][0].astype(f32)
+    for n in range(1, 8):
+        total = total + refs[0][n].astype(f32)
     place = [
         (EARLY, 0, 0),
         (EARLY + 18, 0, 1),
@@ -649,6 +667,13 @@
         name=kernel.__name__,
     )(*values)
     return outs[0] if single else outs
+
+
+def hops(blocks, order, step):
+    def hop(n):
+        return lax.ppermute(blocks[n], "doc", [(j, j ^ (n * step)) for j in range(DOC_DEV)])
+
+    return [hop(n) for n in order]
 
 
 def per_device(
@@ -739,10 +764,10 @@
         ),
     )
     recv = lax.all_to_all(pay_2, "psg", 0, 0, tiled=True)
-    early, loss, g16, right, left, scores = call(
+    e_0, e_1, e_2, e_3, loss, g16, right, left, scores = call(
         early_kernel,
         (
-            shape((DOC_DEV, EARLY, 128), bf16),
+            *[shape((8, EARLY, 128), bf16)] * 4,
             shape((1, 1), f32),
             shape((LOCAL, D), f32),
             shape((2, GROUP, D), bf16),
@@ -769,19 +794,29 @@
             (agg_weights, (1,)),
         ),
     )
-    pay_3 = call(
+    early = [e_0] + hops((e_0, e_1, e_2, e_3), (2, 1, 3), 1)
+    left, early[1] = lax.optimization_barrier((left, early[1]))
+    late = call(
         late_kernel,
-        shape((DOC_DEV, EARLY + LATE, 128), bf16),
+        (shape((8, LATE, 128), bf16),) * 4,
         [pltpu.VMEM((DOC_DEV * LATE, 128), f32)],
-        ((WHOLE, recv), left, right, g16, early),
+        ((WHOLE, recv), left, right, g16),
         limit=24,
     )
-    shares = lax.all_to_all(pay_3, "doc", 0, 0, tiled=True)
+    late = [late[0]] + hops(late, (2, 1, 3), 1)
+    shares = call(
+        middle_kernel,
+        shape((8, EARLY + LATE, 128), bf16),
+        [],
+        (*late, *early),
+    )
+    same_y = [[4 * z + y for z in range(8)] for y in range(4)]
+    shares = lax.all_to_all(shares, "doc", 0, 0, tiled=True, axis_index_groups=same_y)
     weight_grads = call(
         finish_kernel,
         shape((2, 4, SHARE * D), f32),
         [],
-        ((WHOLE, shares), class_rows, vectors),
+        (class_rows, vectors, (WHOLE, shares)),
         limit=16,
     )
     return (scores.reshape(QUERIES, 1), loss.reshape(()), weight_grads)

time: 106 us -> 100 us (0.943); the launches traced: 104 us -> 99.6 us
  blocking collectives: 36.3 us -> 17 us
  starting transfers between devices: 21.2 us -> 30.4 us
  waiting for transfers between devices: 9.46 us -> 12.5 us
  Pallas kernels: 34.9 us -> 36.7 us
    all_to_all x1, blocking collectives: 36.3 us -> 17 us  [per_device(): lax.all_to_all(shares, 'doc', 0, 0, tiled=True, axis_index_groups=same_y)]
    ppermute x0 -> x6, starting transfers between devices: none -> 9.15 us  [hop(): lax.ppermute(blocks[n], 'doc', [(j, j ^ n * step) for j in range(DOC_DEV)])]
    ppermute x0 -> x6, waiting for transfers between devices: none -> 9.13 us  [hop(): lax.ppermute(blocks[n], 'doc', [(j, j ^ n * step) for j in range(DOC_DEV)])]
    all_to_all x1, waiting for transfers between devices: 6.1 us -> 0.01 us  [per_device(): recv = lax.all_to_all(pay_2, 'psg', 0, 0, tiled=True)]
    pallas_call x7 -> x8, Pallas kernels: 34.9 us -> 36.7 us  [call(): pl.pallas_call(body, out_shape=tuple((pltpu.HBM(leaf.shape, leaf.dtype) f...]
  transfers between devices with their start and end apart: 3 -> 9, of which waited for: 2 -> 5; matrix products, arithmetic and copies ran while one was open for 1% -> 1% of each run, Pallas kernels for 18% -> 22%
where the time goes in v3:
time: 100 us; the launch traced here: 99.6 us
  Pallas kernels  36.7 us (37%)
  starting transfers between devices  30.4 us (30%)
  blocking collectives  17 us (17%)
  waiting for transfers between devices  12.5 us (12%)
  between operations  1.68 us (2%)
  local copies, waits for them, and re-layouts  1.32 us (1%)
    pallas_call x8, Pallas kernels, call(): pl.pallas_call(body, out_shape=tuple((pltpu.HBM(leaf.shape, leaf.dtype) f...  36.7 us
    all_to_all x1, blocking collectives, per_device(): lax.all_to_all(shares, 'doc', 0, 0, tiled=True, axis_index_groups=same_y)  17 us
    all_to_all x1, starting transfers between devices, per_device(): everything = lax.all_to_all(score, 'doc', 0, 0, tiled=True)  10.7 us
    ppermute x6, starting transfers between devices, hop(): lax.ppermute(blocks[n], 'doc', [(j, j ^ n * step) for j in range(DOC_DEV)])  9.15 us
    ppermute x6, waiting for transfers between devices, hop(): lax.ppermute(blocks[n], 'doc', [(j, j ^ n * step) for j in range(DOC_DEV)])  9.13 us
    all_to_all x1, starting transfers between devices, per_device(): got = lax.all_to_all(pay_1, 'psg', 0, 0, tiled=True)  5.66 us
    all_to_all x1, starting transfers between devices, per_device(): recv = lax.all_to_all(pay_2, 'psg', 0, 0, tiled=True)  4.92 us
    all_to_all x1, waiting for transfers between devices, per_device(): got = lax.all_to_all(pay_1, 'psg', 0, 0, tiled=True)  3.37 us
  transfers between devices with their start and end apart: 9, of which 5 were waited for; matrix products, arithmetic and copies ran while one was open for 1% of the time, Pallas kernels for 22%

profile of v3, /device:TPU:2, one launch (start us, length us, event | category | flops | bytes accessed | tf_op | source)
XLA Modules:
  0.0 99.6 jit_solution(9955183096600553526)
XLA Ops:
  0.7 6.7 %forward_kernel.1 = (bf16[8,16,1664]{2,1,0:T(8,128)(2,1)}, f32[256,128]{1,0:T(8,128)}, bf16[192,768]{1,0:T(8,128)(2,1)}) custom-call(bf16[8,2,128,768]{3,2,1,0:T(8,128)(2,1)} %bitcast.8, bf16[4,768,768]{2,1,0:T(8,128)(2,1)} %refs_14_.1, bf16[8,2,128,768]{3,2,1,0:T(8,128)(2,1)} %bitcast.9, s32[8,2,128]{2,1,0:T(2,128)} %bitcast.11, s32[2,8]{1,0:T(2,128)} %bitcast.12, ...), custom_call_target="tpu_custom_call" | custom-call | tf_op jit(solution)/shard_map/forward_kernel/pallas_call | solution.py:657
  7.4 5.7 %all-to-all-start = ((bf16[8,16,1664]{2,1,0:T(8,128)(2,1)}), bf16[8,16,1664]{2,1,0:T(8,128)(2,1)S(1)}, u32[]{:S(2)}, u32[]{:S(2)}) async-start(bf16[8,16,1664]{2,1,0:T(8,128)(2,1)} %get-tuple-element.34), calls=%async_computation | async-start | bytes 851968 | tf_op jit(solution)/shard_map/all_to_all | solution.py:716
  13.7 0.0 copy-done.11
  13.8 0.6 stack.27.refs_1_.refs_2_.refs_9_
  14.4 3.1 %class_kernel.1.refs_3_.refs_7_.refs_0_ = f32[3,16,768]{2,1,0:T(8,128)} custom-call(bf16[192,768]{1,0:T(8,128)(2,1)} %get-tuple-element.35.refs_0_, f32[8,768]{1,0:T(8,128)} %stack.27.refs_1_.refs_2_.refs_9_, bf16[4,768,768]{2,1,0:T(8,128)(2,1)} %refs_15_.1), custom_call_target="tpu_custom_call" | custom-call | tf_op jit(solution)/shard_map/class_kernel/pallas_call | solution.py:657
  17.5 3.4 %all-to-all-done.refs_0_.refs_5_ = bf16[8,16,1664]{2,1,0:T(8,128)(2,1)S(1)} async-done(((bf16[8,16,1664]{2,1,0:T(8,128)(2,1)}), bf16[8,16,1664]{2,1,0:T(8,128)(2,1)S(1)}, u32[]{:S(2)}, u32[]{:S(2)}) %all-to-all-start) | async-done | bytes 426016 | tf_op jit(solution)/shard_map/all_to_all | solution.py:716
  20.9 4.5 %score_kernel.1 = (f32[32,1,128]{2,1,0:T(1,128)}, f32[8,128]{1,0:T(8,128)}, f32[128,768]{1,0:T(8,128)}, f32[128,128]{1,0:T(8,128)}, f32[96,768]{1,0:T(8,128)}, /...) custom-call(bf16[8,16,1664]{2,1,0:T(8,128)(2,1)S(1)} %all-to-all-done.refs_0_.refs_5_, bf16[4,768,768]{2,1,0:T(8,128)(2,1)} %refs_14_.1, ...), custom_call_target="tpu_custom_call" | custom-call | tf_op jit(solution)/shard_map/score_kernel/pallas_call | solution.py:657
  25.4 0.0 copy-done
  25.4 10.7 %all-to-all-start.1 = ((f32[32,1,128]{2,1,0:T(1,128)}), f32[32,1,128]{2,1,0:T(1,128)S(1)}, u32[]{:S(2)}, u32[]{:S(2)}) async-start(f32[32,1,128]{2,1,0:T(1,128)} %get-tuple-element.36), calls=%async_computation.1 | async-start | bytes 32768 | tf_op jit(solution)/shard_map/all_to_all | solution.py:738
  36.0 9.7 %backward_kernel.1 = (bf16[8,384,128]{2,1,0:T(8,128)(2,1)}, f32[128,768]{1,0:T(8,128)}, f32[128,768]{1,0:T(8,128)}, f32[96,768]{1,0:T(8,128)}, f32[2,96,128]{2,1,0:T(8,128)}, /*index=5*/f32[2,8,768]{2,1,0:T(8,128)}) custom-call(bf16[192,768]{1,0:T(8,128)(2,1)} %get-tuple-element.35.refs_0_, f32[8,768]{1,0:T(8,128)} %stack.27.refs_1_.refs_2_.refs_9_, ...), custom_call_target="tpu_custom_call" | custom-call | tf_op jit(solution)/shard_map/backward_kernel/pallas_call | solution.py:657
  45.7 0.0 all-to-all-done.1.refs_0_
  45.8 4.9 %all-to-all-start.2 = ((bf16[8,384,128]{2,1,0:T(8,128)(2,1)}), bf16[8,384,128]{2,1,0:T(8,128)(2,1)S(1)}, u32[]{:S(2)}, u32[]{:S(2)}) async-start(bf16[8,384,128]{2,1,0:T(8,128)(2,1)} %get-tuple-element.51), calls=%async_computation.2 | async-start | bytes 1572864 | tf_op jit(solution)/shard_map/all_to_all | solution.py:766
  50.7 5.6 %early_kernel.1 = (bf16[8,64,128]{2,1,0:T(8,128)(2,1)}, bf16[8,64,128]{2,1,0:T(8,128)(2,1)}, bf16[8,64,128]{2,1,0:T(8,128)(2,1)}, bf16[8,64,128]{2,1,0:T(8,128)(...) custom-call(f32[32,1,128]{2,1,0:T(1,128)} %copy-done.7, ...), custom_call_target="tpu_custom_call" | custom-call | tf_op jit(solution)/shard_map/early_kernel/pallas_call | solution.py:657
  56.3 3.4 %collective-permute-start = (bf16[8,64,128]{2,1,0:T(8,128)(2,1)}, bf16[8,64,128]{2,1,0:T(8,128)(2,1)S(1)}, u32[]{:S(2)}, u32[]{:S(2)}) collective-permute-start(bf16[8,64,128]{2,1,0:T(8,128)(2,1)} %get-tuple-element.53), channel_id=1, source_target_pairs={{0,2},{1,3},{2,0},{3,1},{4,6},{5,7},{6,4},{7,5},{8,10},{9,11},{10,... | collective-permute-start | bytes 393224 | tf_op jit(solution)/shard_map/ppermute | solution.py:674
  59.7 0.6 collective-permute-start.4
  60.3 0.6 collective-permute-start.5
  60.9 3.5 %collective-permute-done.refs_5_ = bf16[8,64,128]{2,1,0:T(8,128)(2,1)S(1)} collective-permute-done((bf16[8,64,128]{2,1,0:T(8,128)(2,1)}, bf16[8,64,128]{2,1,0:T(8,128)(2,1)S(1)}, u32[]{:S(2)}, u32[]{:S(2)}) %collective-permute-start) | collective-permute-done | bytes 131104 | tf_op jit(solution)/shard_map/ppermute | solution.py:674
  64.5 0.0 all-to-all-done.2.refs_0_
  64.5 3.3 %late_kernel.1 = (bf16[8,56,128]{2,1,0:T(8,128)(2,1)}, bf16[8,56,128]{2,1,0:T(8,128)(2,1)}, bf16[8,56,128]{2,1,0:T(8,128)(2,1)}, bf16[8,56,128]{2,1,0:T(8,128)(2,1)}) custom-call(bf16[8,384,128]{2,1,0:T(8,128)(2,1)S(1)} %all-to-all-done.2.refs_0_, bf16[96,128]{1,0:T(8,128)(2,1)} %get-tuple-element.54.refs_1_, ...), custom_call_target="tpu_custom_call" | custom-call | tf_op jit(solution)/shard_map/late_kernel/pallas_call | solution.py:657
  67.8 3.4 %collective-permute-start.1 = (bf16[8,56,128]{2,1,0:T(8,128)(2,1)}, bf16[8,56,128]{2,1,0:T(8,128)(2,1)S(1)}, u32[]{:S(2)}, u32[]{:S(2)}) collective-permute-start(bf16[8,56,128]{2,1,0:T(8,128)(2,1)} %get-tuple-element.58), channel_id=1, source_target_pairs={{0,2},{1,3},{2,0},{3,1},{4,6},{5,7},{6,4},{7,5},{8,10},{9,11},{10,... | collective-permute-start | bytes 344072 | tf_op jit(solution)/shard_map/ppermute | solution.py:674
  71.2 0.6 collective-permute-start.2
  71.8 0.6 collective-permute-start.3
  72.4 0.0 collective-permute-done.4.refs_6_
  72.4 0.0 collective-permute-done.5.refs_7_
  72.4 0.0 copy-start.3
  72.4 3.0 %collective-permute-done.1.refs_1_ = bf16[8,56,128]{2,1,0:T(8,128)(2,1)S(1)} collective-permute-done((bf16[8,56,128]{2,1,0:T(8,128)(2,1)}, bf16[8,56,128]{2,1,0:T(8,128)(2,1)S(1)}, u32[]{:S(2)}, u32[]{:S(2)}) %collective-permute-start.1) | collective-permute-done | bytes 114720 | tf_op jit(solution)/shard_map/ppermute | solution.py:674
  75.5 0.8 collective-permute-done.2.refs_2_
  76.2 1.8 %collective-permute-done.3.refs_3_ = bf16[8,56,128]{2,1,0:T(8,128)(2,1)S(1)} collective-permute-done((bf16[8,56,128]{2,1,0:T(8,128)(2,1)}, bf16[8,56,128]{2,1,0:T(8,128)(2,1)S(1)}, u32[]{:S(2)}, u32[]{:S(2)}) %collective-permute-start.3) | collective-permute-done | bytes 114720 | tf_op jit(solution)/shard_map/ppermute | solution.py:674
  78.0 0.6 copy-done.6
  78.7 2.1 %middle_kernel.1 = bf16[8,120,128]{2,1,0:T(8,128)(2,1)} custom-call(bf16[8,56,128]{2,1,0:T(8,128)(2,1)} %get-tuple-element.57.refs_0_, bf16[8,56,128]{2,1,0:T(8,128)(2,1)} %copy-done.4, bf16[8,56,128]{2,1,0:T(8,128)(2,1)} %copy-done.5, bf16[8,56,128]{2,1,0:T(8,128)(2,1)} %copy-done.6, bf16[8,64,128]{2,1,0:T(8,128)(2,1)} %get-tuple-element.61.refs_4_, ...), custom_call_target="tpu_custom_call" | custom-call | tf_op jit(solution)/shard_map/middle_kernel/pallas_call | solution.py:657
  80.8 17.0 %all_to_all.20.refs_2_ = bf16[8,120,128]{2,1,0:T(8,128)(2,1)S(1)} all-to-all(bf16[8,120,128]{2,1,0:T(8,128)(2,1)} %middle_kernel.1), channel_id=1, replica_groups={{0,4,8,12,16,20,24,28},{1,5,9,13,17,21,25,29},{2,6,10,14,18,22,26,30},{..., dimensions={0} | all-to-all | bytes 491520 | tf_op jit(solution)/shard_map/all_to_all | solution.py:814
  97.7 1.7 %finish_kernel.1 = f32[2,4,2304]{2,1,0:T(4,128)} custom-call(f32[3,16,768]{2,1,0:T(8,128)} %class_kernel.1.refs_3_.refs_7_.refs_0_, f32[8,768]{1,0:T(8,128)} %stack.27.refs_1_.refs_2_.refs_9_, bf16[8,120,128]{2,1,0:T(8,128)(2,1)S(1)} %all_to_all.20.refs_2_), custom_call_target="tpu_custom_call" | custom-call | tf_op jit(solution)/shard_map/finish_kernel/pallas_call | solution.py:657
  (27 shorter events, 0.1 us)
Async XLA Ops:
  0.6 13.1 %copy-start.8 = (f32[768]{0:T(1024)S(1)}, f32[768]{0:T(1024)}, u32[]{:S(2)}) copy-start(f32[768]{0:T(1024)} %param.16) | copy-start | bytes 9220
  0.6 13.1 %copy-start.9 = (f32[768]{0:T(1024)S(1)}, f32[768]{0:T(1024)}, u32[]{:S(2)}) copy-start(f32[768]{0:T(1024)} %param.18) | copy-start | bytes 9220
  0.7 13.1 %copy-start.11 = (bf16[768]{0:T(1024)(128)(2,1)S(1)}, bf16[768]{0:T(1024)(128)(2,1)}, u32[]{:S(2)}) copy-start(bf16[768]{0:T(1024)(128)(2,1)} %param.19) | copy-start | bytes 4612
  0.7 13.1 %copy-start.10 = (f32[768]{0:T(1024)S(1)}, f32[768]{0:T(1024)}, u32[]{:S(2)}) copy-start(f32[768]{0:T(1024)} %param.20) | copy-start | bytes 9220
  7.4 13.5 %all-to-all-start = ((bf16[8,16,1664]{2,1,0:T(8,128)(2,1)}), bf16[8,16,1664]{2,1,0:T(8,128)(2,1)S(1)}, u32[]{:S(2)}, u32[]{:S(2)}) async-start(bf16[8,16,1664]{2,1,0:T(8,128)(2,1)} %get-tuple-element.34), calls=%async_computation | async-start | bytes 851968 | tf_op jit(solution)/shard_map/all_to_all | solution.py:716
  20.9 4.5 %copy-start = (bf16[8,16,1664]{2,1,0:T(8,128)(2,1)}, bf16[8,16,1664]{2,1,0:T(8,128)(2,1)S(1)}, u32[]{:S(2)}) copy-start(bf16[8,16,1664]{2,1,0:T(8,128)(2,1)S(1)} %all-to-all-done.refs_0_.refs_5_) | copy-start | bytes 1277956
  25.4 20.4 %all-to-all-start.1 = ((f32[32,1,128]{2,1,0:T(1,128)}), f32[32,1,128]{2,1,0:T(1,128)S(1)}, u32[]{:S(2)}, u32[]{:S(2)}) async-start(f32[32,1,128]{2,1,0:T(1,128)} %get-tuple-element.36), calls=%async_computation.1 | async-start | bytes 32768 | tf_op jit(solution)/shard_map/all_to_all | solution.py:738
  45.8 4.9 %copy-start.7 = (f32[32,1,128]{2,1,0:T(1,128)}, f32[32,1,128]{2,1,0:T(1,128)S(1)}, u32[]{:S(2)}) copy-start(f32[32,1,128]{2,1,0:T(1,128)S(1)} %all-to-all-done.1.refs_0_) | copy-start | bytes 49156
  45.8 18.7 %all-to-all-start.2 = ((bf16[8,384,128]{2,1,0:T(8,128)(2,1)}), bf16[8,384,128]{2,1,0:T(8,128)(2,1)S(1)}, u32[]{:S(2)}, u32[]{:S(2)}) async-start(bf16[8,384,128]{2,1,0:T(8,128)(2,1)} %get-tuple-element.51), calls=%async_computation.2 | async-start | bytes 1572864 | tf_op jit(solution)/shard_map/all_to_all | solution.py:766
  56.3 8.1 %collective-permute-start = (bf16[8,64,128]{2,1,0:T(8,128)(2,1)}, bf16[8,64,128]{2,1,0:T(8,128)(2,1)S(1)}, u32[]{:S(2)}, u32[]{:S(2)}) collective-permute-start(bf16[8,64,128]{2,1,0:T(8,128)(2,1)} %get-tuple-element.53), channel_id=1, source_target_pairs={{0,2},{1,3},{2,0},{3,1},{4,6},{5,7},{6,4},{7,5},{8,10},{9,11},{10,... | collective-permute-start | bytes 393224 | tf_op jit(solution)/shard_map/ppermute | solution.py:674
  59.7 12.7 %collective-permute-start.4 = (bf16[8,64,128]{2,1,0:T(8,128)(2,1)}, bf16[8,64,128]{2,1,0:T(8,128)(2,1)S(1)}, u32[]{:S(2)}, u32[]{:S(2)}) collective-permute-start(bf16[8,64,128]{2,1,0:T(8,128)(2,1)} %get-tuple-element.63), channel_id=1, source_target_pairs={{0,1},{1,0},{2,3},{3,2},{4,5},{5,4},{6,7},{7,6},{8,9},{9,8},{10,11... | collective-permute-start | bytes 393224 | tf_op jit(solution)/shard_map/ppermute | solution.py:674
  60.3 12.1 %collective-permute-start.5 = (bf16[8,64,128]{2,1,0:T(8,128)(2,1)}, bf16[8,64,128]{2,1,0:T(8,128)(2,1)S(1)}, u32[]{:S(2)}, u32[]{:S(2)}) collective-permute-start(bf16[8,64,128]{2,1,0:T(8,128)(2,1)} %get-tuple-element.64), channel_id=1, source_target_pairs={{0,3},{1,2},{2,1},{3,0},{4,7},{5,6},{6,5},{7,4},{8,11},{9,10},{10,... | collective-permute-start | bytes 393224 | tf_op jit(solution)/shard_map/ppermute | solution.py:674
  64.5 13.6 %copy-start.1 = (bf16[8,64,128]{2,1,0:T(8,128)(2,1)}, bf16[8,64,128]{2,1,0:T(8,128)(2,1)S(1)}, u32[]{:S(2)}) copy-start(bf16[8,64,128]{2,1,0:T(8,128)(2,1)S(1)} %collective-permute-done.refs_5_) | copy-start | bytes 393220
  67.8 7.6 %collective-permute-start.1 = (bf16[8,56,128]{2,1,0:T(8,128)(2,1)}, bf16[8,56,128]{2,1,0:T(8,128)(2,1)S(1)}, u32[]{:S(2)}, u32[]{:S(2)}) collective-permute-start(bf16[8,56,128]{2,1,0:T(8,128)(2,1)} %get-tuple-element.58), channel_id=1, source_target_pairs={{0,2},{1,3},{2,0},{3,1},{4,6},{5,7},{6,4},{7,5},{8,10},{9,11},{10,... | collective-permute-start | bytes 344072 | tf_op jit(solution)/shard_map/ppermute | solution.py:674
  71.2 5.0 %collective-permute-start.2 = (bf16[8,56,128]{2,1,0:T(8,128)(2,1)}, bf16[8,56,128]{2,1,0:T(8,128)(2,1)S(1)}, u32[]{:S(2)}, u32[]{:S(2)}) collective-permute-start(bf16[8,56,128]{2,1,0:T(8,128)(2,1)} %get-tuple-element.59), channel_id=1, source_target_pairs={{0,1},{1,0},{2,3},{3,2},{4,5},{5,4},{6,7},{7,6},{8,9},{9,8},{10,11... | collective-permute-start | bytes 344072 | tf_op jit(solution)/shard_map/ppermute | solution.py:674
  71.8 6.2 %collective-permute-start.3 = (bf16[8,56,128]{2,1,0:T(8,128)(2,1)}, bf16[8,56,128]{2,1,0:T(8,128)(2,1)S(1)}, u32[]{:S(2)}, u32[]{:S(2)}) collective-permute-start(bf16[8,56,128]{2,1,0:T(8,128)(2,1)} %get-tuple-element.60), channel_id=1, source_target_pairs={{0,3},{1,2},{2,1},{3,0},{4,7},{5,6},{6,5},{7,4},{8,11},{9,10},{10,... | collective-permute-start | bytes 344072 | tf_op jit(solution)/shard_map/ppermute | solution.py:674
  72.4 5.6 %copy-start.2 = (bf16[8,64,128]{2,1,0:T(8,128)(2,1)}, bf16[8,64,128]{2,1,0:T(8,128)(2,1)S(1)}, u32[]{:S(2)}) copy-start(bf16[8,64,128]{2,1,0:T(8,128)(2,1)S(1)} %collective-permute-done.4.refs_6_) | copy-start | bytes 393220
  72.4 5.6 %copy-start.3 = (bf16[8,64,128]{2,1,0:T(8,128)(2,1)}, bf16[8,64,128]{2,1,0:T(8,128)(2,1)S(1)}, u32[]{:S(2)}) copy-start(bf16[8,64,128]{2,1,0:T(8,128)(2,1)S(1)} %collective-permute-done.5.refs_7_) | copy-start | bytes 393220
  75.5 2.6 %copy-start.4 = (bf16[8,56,128]{2,1,0:T(8,128)(2,1)}, bf16[8,56,128]{2,1,0:T(8,128)(2,1)S(1)}, u32[]{:S(2)}) copy-start(bf16[8,56,128]{2,1,0:T(8,128)(2,1)S(1)} %collective-permute-done.1.refs_1_) | copy-start | bytes 344068
  76.2 1.8 %copy-start.5 = (bf16[8,56,128]{2,1,0:T(8,128)(2,1)}, bf16[8,56,128]{2,1,0:T(8,128)(2,1)S(1)}, u32[]{:S(2)}) copy-start(bf16[8,56,128]{2,1,0:T(8,128)(2,1)S(1)} %collective-permute-done.2.refs_2_) | copy-start | bytes 344068
  78.0 0.6 copy-start.6

commit v4 on v3

--- a/solution.py
+++ b/solution.py
@@ -231,9 +231,7 @@
         jnp.broadcast_to(column(mask_ref[sl : sl + 1, :]), (QUERIES, 128)) for sl in range(SLOTS)
     ]
     keep = jnp.where(jnp.concatenate(keep, axis=0) != 0, 1.0, 0.0).astype(bf16)
-    row = jnp.concatenate([h0, attended.astype(bf16), keep], axis=1)
-    for i in range(PSG_DEV):
-        pay_ref[i] = row
+    pay_ref[...] = jnp.concatenate([h0, attended.astype(bf16), keep], axis=1)
 
 
 def class_kernel(after_ref, vec_ref, wa_ref, out_ref):
@@ -248,20 +246,15 @@
 
 
 def score_kernel(
-    got_ref,
     we_ref,
     vec_ref,
     class_ref,
     wa_ref,
-    score_ref,
-    own_ref,
-    normed_ref,
-    rscale_ref,
-    zagg_ref,
-    soft_ref,
-    small_ref,
+    *refs,
 ):
-    got = got_ref[...].reshape(GROUP, 2 * D + 128)
+    got_ref, score_ref, own_ref, normed_ref, rscale_ref, zagg_ref, soft_ref, small_ref = refs[8:]
+    got = jnp.concatenate([ref[...] for ref in refs[:8]], axis=0)
+    got_ref.send(got[:, : 2 * D])
     h0 = got[:, :D]
     att = got[:, D : 2 * D]
     keep = got[:, 2 * D :]
@@ -342,7 +335,6 @@
     we_ref[3].begin()
     we_ref[2].begin()
     pay(0, z_ref[...])
-    me = lax.axis_index("psg")
     head = jnp.broadcast_to(vec_ref[2:3, :], (QUERIES, D))
     gmix_a = norm_back(head, vec_ref[1:2, :], small_ref[0], small_ref[1][:, 0:1])
     back_ref[1] = gmix_a
@@ -375,7 +367,7 @@
     gmix_e = norm_back(gpass, gain_e, normed_e, rscale_ref[:, 0:1])
     gmix_ref.send(gmix_e)
     gatt_ref.send(dot_nt(gmix_e.astype(bf16), we_ref[3][...]))
-    mine = gatt_ref[pl.ds(pl.multiple_of(me * LOCAL, LOCAL), LOCAL), :]
+    mine = gatt_ref[0:LOCAL, :]
     to_scratch(images(mine, we_ref[2].ready()), wv_s)
     rows_of = lambda q: hid_ref[q][...].reshape(SLOTS * SEQ, D)
     along_e = against_rows(wv_s, rows_of)
@@ -443,7 +435,7 @@
     g_ref[...] = g16
     g_group = jnp.concatenate([g16] * PSG_DEV, axis=0)
     g_heads = jnp.concatenate([g8] * HEADS, axis=0)
-    got = got_ref[...].reshape(GROUP, 2 * D + 128)
+    got = got_ref[...]
     pick = pick_rows(me * ROWS)
     left_ref[...] = dot_nt(pick, got[:, :D]).astype(bf16)
     right_ref[1] = (gatt_ref[...] * g_group).astype(bf16)
@@ -493,7 +485,7 @@
     gv = jnp.zeros((ROWS, D), f32)
     for s in range(PSG_DEV):
         at = slice(s * LOCAL, (s + 1) * LOCAL)
-        block = recv_ref[s]
+        block = recv_ref[lax.axis_index("psg") ^ s]
         gv = gv + dot_nn(unpack_columns(block[:96], block[96:144]), head_rows(right_ref[1, at, :]))
         gk = gk + dot_nn(
             unpack_columns(block[144:240], block[240:288]), head_rows(right_ref[0, at, :])
@@ -669,6 +661,10 @@
     return outs[0] if single else outs
 
 
+def psg_hop(x, flip):
+    return lax.ppermute(x, "psg", [(i, i ^ flip) for i in range(PSG_DEV)])
+
+
 def hops(blocks, order, step):
     def hop(n):
         return lax.ppermute(blocks[n], "doc", [(j, j ^ (n * step)) for j in range(DOC_DEV)])
@@ -699,7 +695,7 @@
     pay_1, soft_e, z_rows = call(
         forward_kernel,
         (
-            shape((PSG_DEV, LOCAL, 2 * D + 128), bf16),
+            shape((LOCAL, 2 * D + 128), bf16),
             shape((LOCAL * PAD_HEADS, SEQ), f32),
             shape((HEADS * LOCAL, D), bf16),
         ),
@@ -713,16 +709,19 @@
             (enc_weights, (2,)),
         ),
     )
-    got = lax.all_to_all(pay_1, "psg", 0, 0, tiled=True)
+    near = {0: pay_1, **{n: psg_hop(pay_1, n) for n in (4, 6, 2)}}
     class_rows = call(
         class_kernel,
         shape((3, PAD_HEADS, D), f32),
         [],
         (z_rows, vectors, (agg_weights, (0, 1))),
     )
-    score, own, normed, rscale, zagg, soft, small = call(
+    near[2], class_rows = lax.optimization_barrier((near[2], class_rows))
+    blocks = {**near, **{n + 1: psg_hop(near[n], 1) for n in (0, 4, 6, 2)}}
+    got, score, own, normed, rscale, zagg, soft, small = call(
         score_kernel,
         (
+            shape((GROUP, 2 * D), bf16),
             shape((DOC_DEV, 1, 128), f32),
             shape((QUERIES, 128), f32),
             group,
@@ -732,7 +731,7 @@
             shape((3, QUERIES, D), f32),
         ),
         [],
-        ((WHOLE, got), (enc_weights, (3,)), vectors, class_rows, (agg_weights, (2, 3))),
+        ((enc_weights, (3,)), vectors, class_rows, (agg_weights, (2, 3)), *[(WHOLE, blocks[n]) for n in range(8)]),
         limit=24,
     )
     everything = lax.all_to_all(score, "doc", 0, 0, tiled=True)

time: 100 us -> 97.8 us (0.978)
  waiting for transfers between devices: 12.5 us -> 10.2 us
    all_to_all x1 -> x0, starting transfers between devices: 5.66 us -> none  [per_device(): got = lax.all_to_all(pay_1, 'psg', 0, 0, tiled=True)]
    ppermute x0 -> x7, starting transfers between devices: none -> 5.63 us  [psg_hop(): return lax.ppermute(x, 'psg', [(i, i ^ flip) for i in range(PSG_DEV)])]
    all_to_all x1 -> x0, waiting for transfers between devices: 3.37 us -> none  [per_device(): got = lax.all_to_all(pay_1, 'psg', 0, 0, tiled=True)]
  transfers between devices with their start and end apart: 9 -> 15, of which waited for: 5 -> 7; matrix products, arithmetic and copies ran while one was open for 1% -> 1% of each run, Pallas kernels for 22% -> 22%
where the time goes in v4:
time: 97.8 us; the launch traced here: 97.4 us
  Pallas kernels  36.6 us (37%)
  starting transfers between devices  30.6 us (31%)
  blocking collectives  17 us (17%)
  waiting for transfers between devices  10.2 us (10%)
  between operations  1.72 us (2%)
  local copies, waits for them, and re-layouts  1.33 us (1%)
    pallas_call x8, Pallas kernels, call(): pl.pallas_call(body, out_shape=tuple((pltpu.HBM(leaf.shape, leaf.dtype) f...  36.6 us
    all_to_all x1, blocking collectives, per_device(): lax.all_to_all(shares, 'doc', 0, 0, tiled=True, axis_index_groups=same_y)  17 us
    all_to_all x1, starting transfers between devices, per_device(): everything = lax.all_to_all(score, 'doc', 0, 0, tiled=True)  11.3 us
    ppermute x6, waiting for transfers between devices, hop(): lax.ppermute(blocks[n], 'doc', [(j, j ^ n * step) for j in range(DOC_DEV)])  9.34 us
    ppermute x6, starting transfers between devices, hop(): lax.ppermute(blocks[n], 'doc', [(j, j ^ n * step) for j in range(DOC_DEV)])  8.78 us
    ppermute x7, starting transfers between devices, psg_hop(): return lax.ppermute(x, 'psg', [(i, i ^ flip) for i in range(PSG_DEV)])  5.63 us
    all_to_all x1, starting transfers between devices, per_device(): recv = lax.all_to_all(pay_2, 'psg', 0, 0, tiled=True)  4.84 us
  transfers between devices with their start and end apart: 15, of which 7 were waited for; matrix products, arithmetic and copies ran while one was open for 1% of the time, Pallas kernels for 22%

profile of v4, /device:TPU:2, one launch (start us, length us, event | category | flops | bytes accessed | tf_op | source)
XLA Modules:
  0.0 97.4 jit_solution(4239429006044802393)
XLA Ops:
  0.7 6.5 %forward_kernel.1 = (bf16[16,1664]{1,0:T(8,128)(2,1)}, f32[256,128]{1,0:T(8,128)}, bf16[192,768]{1,0:T(8,128)(2,1)}) custom-call(bf16[8,2,128,768]{3,2,1,0:T(8,128)(2,1)} %bitcast.8, bf16[4,768,768]{2,1,0:T(8,128)(2,1)} %refs_14_.1, bf16[8,2,128,768]{3,2,1,0:T(8,128)(2,1)} %bitcast.9, s32[8,2,128]{2,1,0:T(2,128)} %bitcast.11, s32[2,8]{1,0:T(2,128)} %bitcast.12, ...), custom_call_target="tpu_custom_call" | custom-call | tf_op jit(solution)/shard_map/forward_kernel/pallas_call | solution.py:649
  7.2 2.4 %collective-permute-start = (bf16[16,1664]{1,0:T(8,128)(2,1)}, bf16[16,1664]{1,0:T(8,128)(2,1)S(1)}, u32[]{:S(2)}, u32[]{:S(2)}) collective-permute-start(bf16[16,1664]{1,0:T(8,128)(2,1)} %get-tuple-element.37.refs_4_), channel_id=1, source_target_pairs={{0,64},{32,96},{64,0},{96,32},{128,192},{160,224},{192,128},{224,1... | collective-permute-start | bytes 159752 | tf_op jit(solution)/shard_map/ppermute | solution.py:665
  9.6 0.4 collective-permute-start.5
  10.0 1.7 %collective-permute-start.3 = (bf16[16,1664]{1,0:T(8,128)(2,1)}, bf16[16,1664]{1,0:T(8,128)(2,1)S(1)}, u32[]{:S(2)}, u32[]{:S(2)}) collective-permute-start(bf16[16,1664]{1,0:T(8,128)(2,1)} %get-tuple-element.37.refs_4_), channel_id=1, source_target_pairs={{0,128},{32,160},{64,192},{96,224},{128,0},{160,32},{192,64},{224,... | collective-permute-start | bytes 159752 | tf_op jit(solution)/shard_map/ppermute | solution.py:665
  12.5 0.6 stack.27.refs_1_.refs_9_
  13.2 3.1 %class_kernel.1.refs_2_.refs_7_.refs_0_ = f32[3,16,768]{2,1,0:T(8,128)} custom-call(bf16[192,768]{1,0:T(8,128)(2,1)} %get-tuple-element.38.refs_0_, f32[8,768]{1,0:T(8,128)} %stack.27.refs_1_.refs_9_, bf16[4,768,768]{2,1,0:T(8,128)(2,1)} %refs_15_.1), custom_call_target="tpu_custom_call" | custom-call | tf_op jit(solution)/shard_map/class_kernel/pallas_call | solution.py:649
  16.3 0.6 collective-permute-start.6
  16.9 0.1 collective-permute-start.4
  17.0 0.4 collective-permute-start.2
  17.4 0.4 collective-permute-done.6.refs_11_
  17.7 0.4 collective-permute-done.4.refs_9_
  18.1 0.2 collective-permute-done.2.refs_7_
  18.3 4.5 %score_kernel.1 = (bf16[128,1536]{1,0:T(8,128)(2,1)}, f32[32,1,128]{2,1,0:T(1,128)}, f32[8,128]{1,0:T(8,128)}, f32[128,768]{1,0:T(8,128)}, f32[128,128]{1,0:T(8,...) custom-call(bf16[4,768,768]{2,1,0:T(8,128)(2,1)} %refs_14_.1, ...), custom_call_target="tpu_custom_call" | custom-call | tf_op jit(solution)/shard_map/score_kernel/pallas_call | solution.py:649
  22.8 11.3 %all-to-all-start = ((f32[32,1,128]{2,1,0:T(1,128)}), f32[32,1,128]{2,1,0:T(1,128)S(1)}, u32[]{:S(2)}, u32[]{:S(2)}) async-start(f32[32,1,128]{2,1,0:T(1,128)} %get-tuple-element.41), calls=%async_computation | async-start | bytes 32768 | tf_op jit(solution)/shard_map/all_to_all | solution.py:737
  34.1 9.7 %backward_kernel.1 = (bf16[8,384,128]{2,1,0:T(8,128)(2,1)}, f32[128,768]{1,0:T(8,128)}, f32[128,768]{1,0:T(8,128)}, f32[96,768]{1,0:T(8,128)}, f32[2,96,128]{2,1,0:T(8,128)}, /*index=5*/f32[2,8,768]{2,1,0:T(8,128)}) custom-call(bf16[192,768]{1,0:T(8,128)(2,1)} %get-tuple-element.38.refs_0_, f32[8,768]{1,0:T(8,128)} %stack.27.refs_1_.refs_9_, ...), custom_call_target="tpu_custom_call" | custom-call | tf_op jit(solution)/shard_map/backward_kernel/pallas_call | solution.py:649
  43.8 4.8 %all-to-all-start.1 = ((bf16[8,384,128]{2,1,0:T(8,128)(2,1)}), bf16[8,384,128]{2,1,0:T(8,128)(2,1)S(1)}, u32[]{:S(2)}, u32[]{:S(2)}) async-start(bf16[8,384,128]{2,1,0:T(8,128)(2,1)} %get-tuple-element.57), calls=%async_computation.1 | async-start | bytes 1572864 | tf_op jit(solution)/shard_map/all_to_all | solution.py:765
  48.7 5.6 %early_kernel.1 = (bf16[8,64,128]{2,1,0:T(8,128)(2,1)}, bf16[8,64,128]{2,1,0:T(8,128)(2,1)}, bf16[8,64,128]{2,1,0:T(8,128)(2,1)}, bf16[8,64,128]{2,1,0:T(8,128)(...) custom-call(f32[32,1,128]{2,1,0:T(1,128)} %copy-done.7, ...), custom_call_target="tpu_custom_call" | custom-call | tf_op jit(solution)/shard_map/early_kernel/pallas_call | solution.py:649
  54.3 3.2 %collective-permute-start.7 = (bf16[8,64,128]{2,1,0:T(8,128)(2,1)}, bf16[8,64,128]{2,1,0:T(8,128)(2,1)S(1)}, u32[]{:S(2)}, u32[]{:S(2)}) collective-permute-start(bf16[8,64,128]{2,1,0:T(8,128)(2,1)} %get-tuple-element.59), channel_id=1, source_target_pairs={{0,2},{1,3},{2,0},{3,1},{4,6},{5,7},{6,4},{7,5},{8,10},{9,11},{10,... | collective-permute-start | bytes 393224 | tf_op jit(solution)/shard_map/ppermute | solution.py:670
  57.5 0.6 collective-permute-start.11
  58.1 0.6 collective-permute-start.12
  58.7 3.8 %collective-permute-done.7.refs_5_ = bf16[8,64,128]{2,1,0:T(8,128)(2,1)S(1)} collective-permute-done((bf16[8,64,128]{2,1,0:T(8,128)(2,1)}, bf16[8,64,128]{2,1,0:T(8,128)(2,1)S(1)}, u32[]{:S(2)}, u32[]{:S(2)}) %collective-permute-start.7) | collective-permute-done | bytes 131104 | tf_op jit(solution)/shard_map/ppermute | solution.py:670
  62.5 3.3 %late_kernel.1 = (bf16[8,56,128]{2,1,0:T(8,128)(2,1)}, bf16[8,56,128]{2,1,0:T(8,128)(2,1)}, bf16[8,56,128]{2,1,0:T(8,128)(2,1)}, bf16[8,56,128]{2,1,0:T(8,128)(2,1)}) custom-call(bf16[8,384,128]{2,1,0:T(8,128)(2,1)S(1)} %all-to-all-done.1.refs_0_, bf16[96,128]{1,0:T(8,128)(2,1)} %get-tuple-element.60.refs_1_, ...), custom_call_target="tpu_custom_call" | custom-call | tf_op jit(solution)/shard_map/late_kernel/pallas_call | solution.py:649
  65.8 3.2 %collective-permute-start.8 = (bf16[8,56,128]{2,1,0:T(8,128)(2,1)}, bf16[8,56,128]{2,1,0:T(8,128)(2,1)S(1)}, u32[]{:S(2)}, u32[]{:S(2)}) collective-permute-start(bf16[8,56,128]{2,1,0:T(8,128)(2,1)} %get-tuple-element.64), channel_id=1, source_target_pairs={{0,2},{1,3},{2,0},{3,1},{4,6},{5,7},{6,4},{7,5},{8,10},{9,11},{10,... | collective-permute-start | bytes 344072 | tf_op jit(solution)/shard_map/ppermute | solution.py:670
  69.0 0.6 collective-permute-start.9
  69.6 0.6 collective-permute-start.10
  70.2 3.0 %collective-permute-done.8.refs_1_ = bf16[8,56,128]{2,1,0:T(8,128)(2,1)S(1)} collective-permute-done((bf16[8,56,128]{2,1,0:T(8,128)(2,1)}, bf16[8,56,128]{2,1,0:T(8,128)(2,1)S(1)}, u32[]{:S(2)}, u32[]{:S(2)}) %collective-permute-start.8) | collective-permute-done | bytes 114720 | tf_op jit(solution)/shard_map/ppermute | solution.py:670
  73.3 0.8 collective-permute-done.9.refs_2_
  74.0 1.8 %collective-permute-done.10.refs_3_ = bf16[8,56,128]{2,1,0:T(8,128)(2,1)S(1)} collective-permute-done((bf16[8,56,128]{2,1,0:T(8,128)(2,1)}, bf16[8,56,128]{2,1,0:T(8,128)(2,1)S(1)}, u32[]{:S(2)}, u32[]{:S(2)}) %collective-permute-start.10) | collective-permute-done | bytes 114720 | tf_op jit(solution)/shard_map/ppermute | solution.py:670
  75.8 0.6 copy-done.6
  76.5 2.1 %middle_kernel.1 = bf16[8,120,128]{2,1,0:T(8,128)(2,1)} custom-call(bf16[8,56,128]{2,1,0:T(8,128)(2,1)} %get-tuple-element.63.refs_0_, bf16[8,56,128]{2,1,0:T(8,128)(2,1)} %copy-done.4, bf16[8,56,128]{2,1,0:T(8,128)(2,1)} %copy-done.5, bf16[8,56,128]{2,1,0:T(8,128)(2,1)} %copy-done.6, bf16[8,64,128]{2,1,0:T(8,128)(2,1)} %get-tuple-element.67.refs_4_, ...), custom_call_target="tpu_custom_call" | custom-call | tf_op jit(solution)/shard_map/middle_kernel/pallas_call | solution.py:649
  78.6 17.0 %all_to_all.15.refs_2_ = bf16[8,120,128]{2,1,0:T(8,128)(2,1)S(1)} all-to-all(bf16[8,120,128]{2,1,0:T(8,128)(2,1)} %middle_kernel.1), channel_id=1, replica_groups={{0,4,8,12,16,20,24,28},{1,5,9,13,17,21,25,29},{2,6,10,14,18,22,26,30},{..., dimensions={0} | all-to-all | bytes 491520 | tf_op jit(solution)/shard_map/all_to_all | solution.py:813
  95.5 1.7 %finish_kernel.1 = f32[2,4,2304]{2,1,0:T(4,128)} custom-call(f32[3,16,768]{2,1,0:T(8,128)} %class_kernel.1.refs_2_.refs_7_.refs_0_, f32[8,768]{1,0:T(8,128)} %stack.27.refs_1_.refs_9_, bf16[8,120,128]{2,1,0:T(8,128)(2,1)S(1)} %all_to_all.15.refs_2_), custom_call_target="tpu_custom_call" | custom-call | tf_op jit(solution)/shard_map/finish_kernel/pallas_call | solution.py:649
  (39 shorter events, 0.1 us)
Async XLA Ops:
  0.6 11.8 %copy-start.8 = (f32[768]{0:T(1024)S(1)}, f32[768]{0:T(1024)}, u32[]{:S(2)}) copy-start(f32[768]{0:T(1024)} %param.16) | copy-start | bytes 9220
  0.6 11.8 %copy-start.9 = (f32[768]{0:T(1024)S(1)}, f32[768]{0:T(1024)}, u32[]{:S(2)}) copy-start(f32[768]{0:T(1024)} %param.18) | copy-start | bytes 9220
  0.7 11.8 %copy-start.11 = (bf16[768]{0:T(1024)(128)(2,1)S(1)}, bf16[768]{0:T(1024)(128)(2,1)}, u32[]{:S(2)}) copy-start(bf16[768]{0:T(1024)(128)(2,1)} %param.19) | copy-start | bytes 4612
  0.7 11.8 %copy-start.10 = (f32[768]{0:T(1024)S(1)}, f32[768]{0:T(1024)}, u32[]{:S(2)}) copy-start(f32[768]{0:T(1024)} %param.20) | copy-start | bytes 9220
  7.2 11.0 %copy-start = (bf16[16,1664]{1,0:T(8,128)(2,1)S(1)}, bf16[16,1664]{1,0:T(8,128)(2,1)}, u32[]{:S(2)}) copy-start(bf16[16,1664]{1,0:T(8,128)(2,1)} %get-tuple-element.37.refs_4_) | copy-start | bytes 159748
  7.2 9.0 %collective-permute-start = (bf16[16,1664]{1,0:T(8,128)(2,1)}, bf16[16,1664]{1,0:T(8,128)(2,1)S(1)}, u32[]{:S(2)}, u32[]{:S(2)}) collective-permute-start(bf16[16,1664]{1,0:T(8,128)(2,1)} %get-tuple-element.37.refs_4_), channel_id=1, source_target_pairs={{0,64},{32,96},{64,0},{96,32},{128,192},{160,224},{192,128},{224,1... | collective-permute-start | bytes 159752 | tf_op jit(solution)/shard_map/ppermute | solution.py:665
  9.6 6.7 %collective-permute-start.5 = (bf16[16,1664]{1,0:T(8,128)(2,1)}, bf16[16,1664]{1,0:T(8,128)(2,1)S(1)}, u32[]{:S(2)}, u32[]{:S(2)}) collective-permute-start(bf16[16,1664]{1,0:T(8,128)(2,1)} %get-tuple-element.37.refs_4_), channel_id=1, source_target_pairs={{0,192},{32,224},{64,128},{96,160},{128,64},{160,96},{192,0},{224,... | collective-permute-start | bytes 159752 | tf_op jit(solution)/shard_map/ppermute | solution.py:665
  10.0 6.8 %collective-permute-start.3 = (bf16[16,1664]{1,0:T(8,128)(2,1)}, bf16[16,1664]{1,0:T(8,128)(2,1)S(1)}, u32[]{:S(2)}, u32[]{:S(2)}) collective-permute-start(bf16[16,1664]{1,0:T(8,128)(2,1)} %get-tuple-element.37.refs_4_), channel_id=1, source_target_pairs={{0,128},{32,160},{64,192},{96,224},{128,0},{160,32},{192,64},{224,... | collective-permute-start | bytes 159752 | tf_op jit(solution)/shard_map/ppermute | solution.py:665
  11.8 5.6 %collective-permute-start.1 = (bf16[16,1664]{1,0:T(8,128)(2,1)}, bf16[16,1664]{1,0:T(8,128)(2,1)S(1)}, u32[]{:S(2)}, u32[]{:S(2)}) collective-permute-start(bf16[16,1664]{1,0:T(8,128)(2,1)} %get-tuple-element.37.refs_4_), channel_id=1, source_target_pairs={{0,32},{32,0},{64,96},{96,64},{128,160},{160,128},{192,224},{224,1... | collective-permute-start | bytes 159752 | tf_op jit(solution)/shard_map/ppermute | solution.py:665
  16.3 1.5 %collective-permute-start.6 = (bf16[16,1664]{1,0:T(8,128)(2,1)S(1)}, bf16[16,1664]{1,0:T(8,128)(2,1)S(1)}, u32[]{:S(2)}, u32[]{:S(2)}) collective-permute-start(bf16[16,1664]{1,0:T(8,128)(2,1)S(1)} %collective-permute-done.5.refs_10_), channel_id=1, source_target_pairs={{0,32},{32,0},{64,96},{96,64},{128,160},{160,128},{192,224},{224,1... | collective-permute-start | bytes 159752 | tf_op jit(solution)/shard_map/ppermute | solution.py:665
  16.9 1.2 %collective-permute-start.4 = (bf16[16,1664]{1,0:T(8,128)(2,1)S(1)}, bf16[16,1664]{1,0:T(8,128)(2,1)S(1)}, u32[]{:S(2)}, u32[]{:S(2)}) collective-permute-start(bf16[16,1664]{1,0:T(8,128)(2,1)S(1)} %collective-permute-done.3.refs_8_), channel_id=1, source_target_pairs={{0,32},{32,0},{64,96},{96,64},{128,160},{160,128},{192,224},{224,1... | collective-permute-start | bytes 159752 | tf_op jit(solution)/shard_map/ppermute | solution.py:665
  17.0 1.3 %collective-permute-start.2 = (bf16[16,1664]{1,0:T(8,128)(2,1)S(1)}, bf16[16,1664]{1,0:T(8,128)(2,1)S(1)}, u32[]{:S(2)}, u32[]{:S(2)}) collective-permute-start(bf16[16,1664]{1,0:T(8,128)(2,1)S(1)} %collective-permute-done.refs_6_), channel_id=1, source_target_pairs={{0,32},{32,0},{64,96},{96,64},{128,160},{160,128},{192,224},{224,1... | collective-permute-start | bytes 159752 | tf_op jit(solution)/shard_map/ppermute | solution.py:665
  22.8 21.1 %all-to-all-start = ((f32[32,1,128]{2,1,0:T(1,128)}), f32[32,1,128]{2,1,0:T(1,128)S(1)}, u32[]{:S(2)}, u32[]{:S(2)}) async-start(f32[32,1,128]{2,1,0:T(1,128)} %get-tuple-element.41), calls=%async_computation | async-start | bytes 32768 | tf_op jit(solution)/shard_map/all_to_all | solution.py:737
  43.8 4.9 %copy-start.7 = (f32[32,1,128]{2,1,0:T(1,128)}, f32[32,1,128]{2,1,0:T(1,128)S(1)}, u32[]{:S(2)}) copy-start(f32[32,1,128]{2,1,0:T(1,128)S(1)} %all-to-all-done.refs_0_) | copy-start | bytes 49156
  43.8 18.6 %all-to-all-start.1 = ((bf16[8,384,128]{2,1,0:T(8,128)(2,1)}), bf16[8,384,128]{2,1,0:T(8,128)(2,1)S(1)}, u32[]{:S(2)}, u32[]{:S(2)}) async-start(bf16[8,384,128]{2,1,0:T(8,128)(2,1)} %get-tuple-element.57), calls=%async_computation.1 | async-start | bytes 1572864 | tf_op jit(solution)/shard_map/all_to_all | solution.py:765
  54.3 8.1 %collective-permute-start.7 = (bf16[8,64,128]{2,1,0:T(8,128)(2,1)}, bf16[8,64,128]{2,1,0:T(8,128)(2,1)S(1)}, u32[]{:S(2)}, u32[]{:S(2)}) collective-permute-start(bf16[8,64,128]{2,1,0:T(8,128)(2,1)} %get-tuple-element.59), channel_id=1, source_target_pairs={{0,2},{1,3},{2,0},{3,1},{4,6},{5,7},{6,4},{7,5},{8,10},{9,11},{10,... | collective-permute-start | bytes 393224 | tf_op jit(solution)/shard_map/ppermute | solution.py:670
  57.5 12.7 %collective-permute-start.11 = (bf16[8,64,128]{2,1,0:T(8,128)(2,1)}, bf16[8,64,128]{2,1,0:T(8,128)(2,1)S(1)}, u32[]{:S(2)}, u32[]{:S(2)}) collective-permute-start(bf16[8,64,128]{2,1,0:T(8,128)(2,1)} %get-tuple-element.69), channel_id=1, source_target_pairs={{0,1},{1,0},{2,3},{3,2},{4,5},{5,4},{6,7},{7,6},{8,9},{9,8},{10,11... | collective-permute-start | bytes 393224 | tf_op jit(solution)/shard_map/ppermute | solution.py:670
  58.1 12.1 %collective-permute-start.12 = (bf16[8,64,128]{2,1,0:T(8,128)(2,1)}, bf16[8,64,128]{2,1,0:T(8,128)(2,1)S(1)}, u32[]{:S(2)}, u32[]{:S(2)}) collective-permute-start(bf16[8,64,128]{2,1,0:T(8,128)(2,1)} %get-tuple-element.70), channel_id=1, source_target_pairs={{0,3},{1,2},{2,1},{3,0},{4,7},{5,6},{6,5},{7,4},{8,11},{9,10},{10,... | collective-permute-start | bytes 393224 | tf_op jit(solution)/shard_map/ppermute | solution.py:670
  62.5 13.4 %copy-start.1 = (bf16[8,64,128]{2,1,0:T(8,128)(2,1)}, bf16[8,64,128]{2,1,0:T(8,128)(2,1)S(1)}, u32[]{:S(2)}) copy-start(bf16[8,64,128]{2,1,0:T(8,128)(2,1)S(1)} %collective-permute-done.7.refs_5_) | copy-start | bytes 393220
  65.8 7.4 %collective-permute-start.8 = (bf16[8,56,128]{2,1,0:T(8,128)(2,1)}, bf16[8,56,128]{2,1,0:T(8,128)(2,1)S(1)}, u32[]{:S(2)}, u32[]{:S(2)}) collective-permute-start(bf16[8,56,128]{2,1,0:T(8,128)(2,1)} %get-tuple-element.64), channel_id=1, source_target_pairs={{0,2},{1,3},{2,0},{3,1},{4,6},{5,7},{6,4},{7,5},{8,10},{9,11},{10,... | collective-permute-start | bytes 344072 | tf_op jit(solution)/shard_map/ppermute | solution.py:670
  69.0 5.0 %collective-permute-start.9 = (bf16[8,56,128]{2,1,0:T(8,128)(2,1)}, bf16[8,56,128]{2,1,0:T(8,128)(2,1)S(1)}, u32[]{:S(2)}, u32[]{:S(2)}) collective-permute-start(bf16[8,56,128]{2,1,0:T(8,128)(2,1)} %get-tuple-element.65), channel_id=1, source_target_pairs={{0,1},{1,0},{2,3},{3,2},{4,5},{5,4},{6,7},{7,6},{8,9},{9,8},{10,11... | collective-permute-start | bytes 344072 | tf_op jit(solution)/shard_map/ppermute | solution.py:670
  69.6 6.2 %collective-permute-start.10 = (bf16[8,56,128]{2,1,0:T(8,128)(2,1)}, bf16[8,56,128]{2,1,0:T(8,128)(2,1)S(1)}, u32[]{:S(2)}, u32[]{:S(2)}) collective-permute-start(bf16[8,56,128]{2,1,0:T(8,128)(2,1)} %get-tuple-element.66), channel_id=1, source_target_pairs={{0,3},{1,2},{2,1},{3,0},{4,7},{5,6},{6,5},{7,4},{8,11},{9,10},{10,... | collective-permute-start | bytes 344072 | tf_op jit(solution)/shard_map/ppermute | solution.py:670
  70.2 5.6 %copy-start.2 = (bf16[8,64,128]{2,1,0:T(8,128)(2,1)}, bf16[8,64,128]{2,1,0:T(8,128)(2,1)S(1)}, u32[]{:S(2)}) copy-start(bf16[8,64,128]{2,1,0:T(8,128)(2,1)S(1)} %collective-permute-done.11.refs_6_) | copy-start | bytes 393220
  70.2 5.6 %copy-start.3 = (bf16[8,64,128]{2,1,0:T(8,128)(2,1)}, bf16[8,64,128]{2,1,0:T(8,128)(2,1)S(1)}, u32[]{:S(2)}) copy-start(bf16[8,64,128]{2,1,0:T(8,128)(2,1)S(1)} %collective-permute-done.12.refs_7_) | copy-start | bytes 393220
  73.3 2.6 %copy-start.4 = (bf16[8,56,128]{2,1,0:T(8,128)(2,1)}, bf16[8,56,128]{2,1,0:T(8,128)(2,1)S(1)}, u32[]{:S(2)}) copy-start(bf16[8,56,128]{2,1,0:T(8,128)(2,1)S(1)} %collective-permute-done.8.refs_1_) | copy-start | bytes 344068
  74.0 1.8 %copy-start.5 = (bf16[8,56,128]{2,1,0:T(8,128)(2,1)}, bf16[8,56,128]{2,1,0:T(8,128)(2,1)S(1)}, u32[]{:S(2)}) copy-start(bf16[8,56,128]{2,1,0:T(8,128)(2,1)S(1)} %collective-permute-done.9.refs_2_) | copy-start | bytes 344068
  75.8 0.6 copy-start.6

commit v5 on v4

--- a/solution.py
+++ b/solution.py
@@ -389,7 +389,6 @@
     all_ref,
     own_ref,
     labels_ref,
-    gatt_ref,
     gmix_ref,
     got_ref,
     zagg_ref,
@@ -400,7 +399,6 @@
     gpv_ref,
     glogit_ref,
     normed_ref,
-    we_ref,
     wa_ref,
     pay_0,
     pay_1,
@@ -408,8 +406,6 @@
     pay_3,
     loss_ref,
     g_ref,
-    right_ref,
-    left_ref,
     score_ref,
     out_s,
 ):
@@ -437,8 +433,6 @@
     g_heads = jnp.concatenate([g8] * HEADS, axis=0)
     got = got_ref[...]
     pick = pick_rows(me * ROWS)
-    left_ref[...] = dot_nt(pick, got[:, :D]).astype(bf16)
-    right_ref[1] = (gatt_ref[...] * g_group).astype(bf16)
     att_t = dot_nt(pick, got[:, D : 2 * D]).astype(bf16)
     put(out_s, 0, dot_nn(att_t, (gmix_ref[...] * g_group).astype(bf16)), EARLY)
     zagg_t = dot_nt(pick, zagg_ref[...].astype(bf16)).astype(bf16)
@@ -458,7 +452,6 @@
     m = two_part(dot_nn, glogit_ref[0], passage) + cls_glogit * cls_f
     m_sum = jnp.sum((m * g_heads).reshape(HEADS, QUERIES, D), axis=1)
     m_sum = jnp.concatenate([m_sum, jnp.zeros((PAD_HEADS - HEADS, D), f32)], axis=0)
-    right_ref[0] = (dot_nn(got[:, :D], we_ref[0][...]) * g_group).astype(bf16)
     qvec = fold(two_part(dot_nn, m_sum, wa_ref[1][...]), head_mask())
     for c in range(D // 128):
         out_s[pl.ds(54 + c, DOC_DEV, stride=EARLY), :] = jnp.broadcast_to(
@@ -476,6 +469,14 @@
     out = out_s[...].astype(bf16).reshape(4, 8, EARLY, 128)
     for n, pay_ref in enumerate((pay_0, pay_1, pay_2, pay_3)):
         pay_ref.send(out[n])
+
+
+def side_kernel(g_ref, got_ref, gatt_ref, we_ref, left_ref, right_ref):
+    g_group = jnp.concatenate([g_ref[...]] * PSG_DEV, axis=0)
+    h0 = got_ref[:, :D]
+    left_ref.send(dot_nt(pick_rows(lax.axis_index("psg") * ROWS), h0).astype(bf16))
+    right_ref[1] = (gatt_ref[...] * g_group).astype(bf16)
+    right_ref[0] = (dot_nn(h0, we_ref[0][...]) * g_group).astype(bf16)
 
 
 def late_kernel(recv_ref, left_ref, right_ref, g_ref, pay_0, pay_1, pay_2, pay_3, out_s):
@@ -502,13 +503,15 @@
         pay_ref.send(out[n])
 
 
-def middle_kernel(*refs):
+def early_sum_kernel(*refs):
+    parts = [ref[...].astype(f32) for ref in refs[:4]]
+    refs[4][...] = ((parts[0] + parts[1]) + (parts[2] + parts[3])).astype(bf16)
+
+
+def middle_kernel(early_ref, *refs):
     late = [ref[...].astype(f32) for ref in refs[:4]]
-    early = [ref[...].astype(f32) for ref in refs[4:8]]
-    late = (late[0] + late[1]) + (late[2] + late[3])
-    early = (early[0] + early[1]) + (early[2] + early[3])
-    total = jnp.concatenate([early, late], axis=1).astype(bf16)
-    refs[8][...] = total
+    late = ((late[0] + late[1]) + (late[2] + late[3])).astype(bf16)
+    refs[4][...] = jnp.concatenate([early_ref[...], late], axis=1)
 
 
 def finish_kernel(class_ref, vec_ref, *refs):
@@ -763,14 +766,12 @@
         ),
     )
     recv = lax.all_to_all(pay_2, "psg", 0, 0, tiled=True)
-    e_0, e_1, e_2, e_3, loss, g16, right, left, scores = call(
+    e_0, e_1, e_2, e_3, loss, g16, scores = call(
         early_kernel,
         (
             *[shape((8, EARLY, 128), bf16)] * 4,
             shape((1, 1), f32),
             shape((LOCAL, D), f32),
-            shape((2, GROUP, D), bf16),
-            shape((ROWS, GROUP), bf16),
             shape((1, QUERIES), f32),
         ),
         [pltpu.VMEM((DOC_DEV * EARLY, 128), f32)],
@@ -778,7 +779,6 @@
             everything,
             own,
             labels.reshape(1, QUERIES),
-            gatt,
             gmix,
             got,
             zagg,
@@ -789,9 +789,14 @@
             gpv,
             glogit,
             normed,
-            (enc_weights, (0,)),
             (agg_weights, (1,)),
         ),
+    )
+    left, right = call(
+        side_kernel,
+        (shape((ROWS, GROUP), bf16), shape((2, GROUP, D), bf16)),
+        [],
+        (g16, got, gatt, (enc_weights, (0,))),
     )
     early = [e_0] + hops((e_0, e_1, e_2, e_3), (2, 1, 3), 1)
     left, early[1] = lax.optimization_barrier((left, early[1]))
@@ -802,12 +807,14 @@
         ((WHOLE, recv), left, right, g16),
         limit=24,
     )
-    late = [late[0]] + hops(late, (2, 1, 3), 1)
+    g_late, early[0] = lax.optimization_barrier((late[0], early[0]))
+    early = call(early_sum_kernel, shape((8, EARLY, 128), bf16), [], tuple(early))
+    late = [g_late] + hops(late, (2, 1, 3), 1)
     shares = call(
         middle_kernel,
         shape((8, EARLY + LATE, 128), bf16),
         [],
-        (*late, *early),
+        (early, *late),
     )
     same_y = [[4 * z + y for z in range(8)] for y in range(4)]
     shares = lax.all_to_all(shares, "doc", 0, 0, tiled=True, axis_index_groups=same_y)

time: 97.8 us -> 96.8 us (0.990)
  waiting for transfers between devices: 10.2 us -> 4.42 us
  Pallas kernels: 36.6 us -> 40 us
  local copies, waits for them, and re-layouts: 1.33 us -> 2.63 us
    ppermute x6, waiting for transfers between devices: 9.34 us -> 3.52 us  [hop(): lax.ppermute(blocks[n], 'doc', [(j, j ^ n * step) for j in range(DOC_DEV)])]
    pallas_call x8 -> x10, Pallas kernels: 36.6 us -> 40 us  [call(): pl.pallas_call(body, out_shape=tuple((pltpu.HBM(leaf.shape, leaf.dtype) f...]
    unnamed x24, local copies, waits for them, and re-layouts: 0.66 us -> 1.96 us
  transfers between devices with their start and end apart: 15 -> 15, of which waited for: 7 -> 6; matrix products, arithmetic and copies ran while one was open for 1% -> 1% of each run, Pallas kernels for 22% -> 26%
where the time goes in v5:
time: 96.8 us; the launch traced here: 96.3 us
  Pallas kernels  40 us (41%)
  starting transfers between devices  30.6 us (32%)
  blocking collectives  17 us (18%)
  waiting for transfers between devices  4.42 us (5%)
  local copies, waits for them, and re-layouts  2.63 us (3%)
  between operations  1.73 us (2%)
    pallas_call x10, Pallas kernels, call(): pl.pallas_call(body, out_shape=tuple((pltpu.HBM(leaf.shape, leaf.dtype) f...  40 us
    all_to_all x1, blocking collectives, per_device(): lax.all_to_all(shares, 'doc', 0, 0, tiled=True, axis_index_groups=same_y)  17 us
    all_to_all x1, starting transfers between devices, per_device(): everything = lax.all_to_all(score, 'doc', 0, 0, tiled=True)  11.3 us
    ppermute x6, starting transfers between devices, hop(): lax.ppermute(blocks[n], 'doc', [(j, j ^ n * step) for j in range(DOC_DEV)])  8.75 us
    ppermute x7, starting transfers between devices, psg_hop(): return lax.ppermute(x, 'psg', [(i, i ^ flip) for i in range(PSG_DEV)])  5.63 us
    all_to_all x1, starting transfers between devices, per_device(): recv = lax.all_to_all(pay_2, 'psg', 0, 0, tiled=True)  4.85 us
    ppermute x6, waiting for transfers between devices, hop(): lax.ppermute(blocks[n], 'doc', [(j, j ^ n * step) for j in range(DOC_DEV)])  3.52 us
    unnamed x24, local copies, waits for them, and re-layouts  1.96 us
  transfers between devices with their start and end apart: 15, of which 6 were waited for; matrix products, arithmetic and copies ran while one was open for 1% of the time, Pallas kernels for 26%

profile of v5, /device:TPU:2, one launch (start us, length us, event | category | flops | bytes accessed | tf_op | source)
XLA Modules:
  0.0 96.3 jit_solution(18141015722967403795)
XLA Ops:
  0.7 6.5 %forward_kernel.1 = (bf16[16,1664]{1,0:T(8,128)(2,1)}, f32[256,128]{1,0:T(8,128)}, bf16[192,768]{1,0:T(8,128)(2,1)}) custom-call(bf16[8,2,128,768]{3,2,1,0:T(8,128)(2,1)} %bitcast.8, bf16[4,768,768]{2,1,0:T(8,128)(2,1)} %refs_3_.5, bf16[8,2,128,768]{3,2,1,0:T(8,128)(2,1)} %bitcast.9, s32[8,2,128]{2,1,0:T(2,128)} %bitcast.11, s32[2,8]{1,0:T(2,128)} %bitcast.12, ...), custom_call_target="tpu_custom_call" | custom-call | tf_op jit(solution)/shard_map/forward_kernel/pallas_call | solution.py:652
  7.2 2.4 %collective-permute-start = (bf16[16,1664]{1,0:T(8,128)(2,1)}, bf16[16,1664]{1,0:T(8,128)(2,1)S(1)}, u32[]{:S(2)}, u32[]{:S(2)}) collective-permute-start(bf16[16,1664]{1,0:T(8,128)(2,1)} %get-tuple-element.39.refs_4_), channel_id=1, source_target_pairs={{0,64},{32,96},{64,0},{96,32},{128,192},{160,224},{192,128},{224,1... | collective-permute-start | bytes 159752 | tf_op jit(solution)/shard_map/ppermute | solution.py:668
  9.6 0.4 collective-permute-start.5
  10.0 1.7 %collective-permute-start.3 = (bf16[16,1664]{1,0:T(8,128)(2,1)}, bf16[16,1664]{1,0:T(8,128)(2,1)S(1)}, u32[]{:S(2)}, u32[]{:S(2)}) collective-permute-start(bf16[16,1664]{1,0:T(8,128)(2,1)} %get-tuple-element.39.refs_4_), channel_id=1, source_target_pairs={{0,128},{32,160},{64,192},{96,224},{128,0},{160,32},{192,64},{224,... | collective-permute-start | bytes 159752 | tf_op jit(solution)/shard_map/ppermute | solution.py:668
  12.5 0.6 stack.27.refs_1_.refs_8_
  13.2 3.1 %class_kernel.1.refs_2_.refs_7_.refs_0_ = f32[3,16,768]{2,1,0:T(8,128)} custom-call(bf16[192,768]{1,0:T(8,128)(2,1)} %get-tuple-element.40.refs_0_, f32[8,768]{1,0:T(8,128)} %stack.27.refs_1_.refs_8_, bf16[4,768,768]{2,1,0:T(8,128)(2,1)} %refs_13_.1), custom_call_target="tpu_custom_call" | custom-call | tf_op jit(solution)/shard_map/class_kernel/pallas_call | solution.py:652
  16.3 0.6 collective-permute-start.6
  17.0 0.4 collective-permute-start.2
  17.4 0.4 collective-permute-done.6.refs_11_
  18.3 4.5 %score_kernel.1 = (bf16[128,1536]{1,0:T(8,128)(2,1)}, f32[32,1,128]{2,1,0:T(1,128)}, f32[8,128]{1,0:T(8,128)}, f32[128,768]{1,0:T(8,128)}, f32[128,128]{1,0:T(8,...) custom-call(bf16[4,768,768]{2,1,0:T(8,128)(2,1)} %refs_3_.5, ...), custom_call_target="tpu_custom_call" | custom-call | tf_op jit(solution)/shard_map/score_kernel/pallas_call | solution.py:652
  22.8 11.3 %all-to-all-start = ((f32[32,1,128]{2,1,0:T(1,128)}), f32[32,1,128]{2,1,0:T(1,128)S(1)}, u32[]{:S(2)}, u32[]{:S(2)}) async-start(f32[32,1,128]{2,1,0:T(1,128)} %get-tuple-element.43), calls=%async_computation | async-start | bytes 32768 | tf_op jit(solution)/shard_map/all_to_all | solution.py:740
  34.1 9.7 %backward_kernel.1 = (bf16[8,384,128]{2,1,0:T(8,128)(2,1)}, f32[128,768]{1,0:T(8,128)}, f32[128,768]{1,0:T(8,128)}, f32[96,768]{1,0:T(8,128)}, f32[2,96,128]{2,1,0:T(8,128)}, /*index=5*/f32[2,8,768]{2,1,0:T(8,128)}) custom-call(bf16[192,768]{1,0:T(8,128)(2,1)} %get-tuple-element.40.refs_0_, f32[8,768]{1,0:T(8,128)} %stack.27.refs_1_.refs_8_, ...), custom_call_target="tpu_custom_call" | custom-call | tf_op jit(solution)/shard_map/backward_kernel/pallas_call | solution.py:652
  43.8 4.8 %all-to-all-start.1 = ((bf16[8,384,128]{2,1,0:T(8,128)(2,1)}), bf16[8,384,128]{2,1,0:T(8,128)(2,1)S(1)}, u32[]{:S(2)}, u32[]{:S(2)}) async-start(bf16[8,384,128]{2,1,0:T(8,128)(2,1)} %get-tuple-element.58), calls=%async_computation.1 | async-start | bytes 1572864 | tf_op jit(solution)/shard_map/all_to_all | solution.py:768
  48.7 4.7 %early_kernel.1 = (bf16[8,64,128]{2,1,0:T(8,128)(2,1)}, bf16[8,64,128]{2,1,0:T(8,128)(2,1)}, bf16[8,64,128]{2,1,0:T(8,128)(2,1)}, bf16[8,64,128]{2,1,0:T(8,128)(...) custom-call(f32[32,1,128]{2,1,0:T(1,128)} %copy-done.7, f32[8,128]{1,0:T(8,128)} %get-tuple-element.44.refs_1_, ...), custom_call_target="tpu_custom_call" | custom-call | tf_op jit(solution)/shard_map/early_kernel/pallas_call | solution.py:652
  53.4 3.2 %collective-permute-start.7 = (bf16[8,64,128]{2,1,0:T(8,128)(2,1)}, bf16[8,64,128]{2,1,0:T(8,128)(2,1)S(1)}, u32[]{:S(2)}, u32[]{:S(2)}) collective-permute-start(bf16[8,64,128]{2,1,0:T(8,128)(2,1)} %get-tuple-element.62), channel_id=1, source_target_pairs={{0,2},{1,3},{2,0},{3,1},{4,6},{5,7},{6,4},{7,5},{8,10},{9,11},{10,... | collective-permute-start | bytes 393224 | tf_op jit(solution)/shard_map/ppermute | solution.py:673
  56.6 0.6 collective-permute-start.8
  57.2 0.6 collective-permute-start.9
  57.8 2.7 %side_kernel.1 = (bf16[96,128]{1,0:T(8,128)(2,1)}, bf16[2,128,768]{2,1,0:T(8,128)(2,1)}) custom-call(f32[16,768]{1,0:T(8,128)} %get-tuple-element.59.refs_0_.refs_3_, bf16[128,1536]{1,0:T(8,128)(2,1)} %get-tuple-element.52.refs_4_.refs_1_, f32[128,768]{1,0:T(8,128)} %get-tuple-element.60.refs_2_, bf16[4,768,768]{2,1,0:T(8,128)(2,1)} %refs_3_.5), custom_call_target="tpu_custom_call" | custom-call | tf_op jit(solution)/shard_map/side_kernel/pallas_call | solution.py:652
  60.5 1.0 %collective-permute-done.7.refs_1_ = bf16[8,64,128]{2,1,0:T(8,128)(2,1)S(1)} collective-permute-done((bf16[8,64,128]{2,1,0:T(8,128)(2,1)}, bf16[8,64,128]{2,1,0:T(8,128)(2,1)S(1)}, u32[]{:S(2)}, u32[]{:S(2)}) %collective-permute-start.7) | collective-permute-done | bytes 131104 | tf_op jit(solution)/shard_map/ppermute | solution.py:673
  61.5 3.3 %late_kernel.1 = (bf16[8,56,128]{2,1,0:T(8,128)(2,1)}, bf16[8,56,128]{2,1,0:T(8,128)(2,1)}, bf16[8,56,128]{2,1,0:T(8,128)(2,1)}, bf16[8,56,128]{2,1,0:T(8,128)(2,1)}) custom-call(bf16[8,384,128]{2,1,0:T(8,128)(2,1)S(1)} %all-to-all-done.1.refs_0_, bf16[96,128]{1,0:T(8,128)(2,1)} %get-tuple-element.63.refs_1_, ...), custom_call_target="tpu_custom_call" | custom-call | tf_op jit(solution)/shard_map/late_kernel/pallas_call | solution.py:652
  64.9 3.2 %collective-permute-start.10 = (bf16[8,56,128]{2,1,0:T(8,128)(2,1)}, bf16[8,56,128]{2,1,0:T(8,128)(2,1)S(1)}, u32[]{:S(2)}, u32[]{:S(2)}) collective-permute-start(bf16[8,56,128]{2,1,0:T(8,128)(2,1)} %get-tuple-element.72), channel_id=1, source_target_pairs={{0,2},{1,3},{2,0},{3,1},{4,6},{5,7},{6,4},{7,5},{8,10},{9,11},{10,... | collective-permute-start | bytes 344072 | tf_op jit(solution)/shard_map/ppermute | solution.py:673
  68.1 0.6 collective-permute-start.11
  68.6 0.6 collective-permute-start.12
  69.3 0.6 copy-done.2
  69.9 0.6 copy-done.3
  70.5 1.8 %early_sum_kernel.1.refs_0_ = bf16[8,64,128]{2,1,0:T(8,128)(2,1)} custom-call(bf16[8,64,128]{2,1,0:T(8,128)(2,1)} %get-tuple-element.67.refs_0_, bf16[8,64,128]{2,1,0:T(8,128)(2,1)} %copy-done.1, bf16[8,64,128]{2,1,0:T(8,128)(2,1)} %copy-done.2, bf16[8,64,128]{2,1,0:T(8,128)(2,1)} %copy-done.3), custom_call_target="tpu_custom_call" | custom-call | tf_op jit(solution)/shard_map/early_sum_kernel/pallas_call | solution.py:652
  72.4 0.7 collective-permute-done.11.refs_3_
  73.1 1.8 %collective-permute-done.12.refs_4_ = bf16[8,56,128]{2,1,0:T(8,128)(2,1)S(1)} collective-permute-done((bf16[8,56,128]{2,1,0:T(8,128)(2,1)}, bf16[8,56,128]{2,1,0:T(8,128)(2,1)S(1)}, u32[]{:S(2)}, u32[]{:S(2)}) %collective-permute-start.12) | collective-permute-done | bytes 114720 | tf_op jit(solution)/shard_map/ppermute | solution.py:673
  74.9 0.7 copy-done.6
  75.5 1.9 %middle_kernel.1 = bf16[8,120,128]{2,1,0:T(8,128)(2,1)} custom-call(bf16[8,64,128]{2,1,0:T(8,128)(2,1)} %early_sum_kernel.1.refs_0_, bf16[8,56,128]{2,1,0:T(8,128)(2,1)} %get-tuple-element.71.refs_1_, bf16[8,56,128]{2,1,0:T(8,128)(2,1)} %copy-done.4, bf16[8,56,128]{2,1,0:T(8,128)(2,1)} %copy-done.5, bf16[8,56,128]{2,1,0:T(8,128)(2,1)} %copy-done.6), custom_call_target="tpu_custom_call" | custom-call | tf_op jit(solution)/shard_map/middle_kernel/pallas_call | solution.py:652
  77.5 17.0 %all_to_all.15.refs_2_ = bf16[8,120,128]{2,1,0:T(8,128)(2,1)S(1)} all-to-all(bf16[8,120,128]{2,1,0:T(8,128)(2,1)} %middle_kernel.1), channel_id=1, replica_groups={{0,4,8,12,16,20,24,28},{1,5,9,13,17,21,25,29},{2,6,10,14,18,22,26,30},{..., dimensions={0} | all-to-all | bytes 491520 | tf_op jit(solution)/shard_map/all_to_all | solution.py:820
  94.4 1.7 %finish_kernel.1 = f32[2,4,2304]{2,1,0:T(4,128)} custom-call(f32[3,16,768]{2,1,0:T(8,128)} %class_kernel.1.refs_2_.refs_7_.refs_0_, f32[8,768]{1,0:T(8,128)} %stack.27.refs_1_.refs_8_, bf16[8,120,128]{2,1,0:T(8,128)(2,1)S(1)} %all_to_all.15.refs_2_), custom_call_target="tpu_custom_call" | custom-call | tf_op jit(solution)/shard_map/finish_kernel/pallas_call | solution.py:652
  (41 shorter events, 0.7 us)
Async XLA Ops:
  0.6 11.8 %copy-start.8 = (f32[768]{0:T(1024)S(1)}, f32[768]{0:T(1024)}, u32[]{:S(2)}) copy-start(f32[768]{0:T(1024)} %param.16) | copy-start | bytes 9220
  0.6 11.8 %copy-start.9 = (f32[768]{0:T(1024)S(1)}, f32[768]{0:T(1024)}, u32[]{:S(2)}) copy-start(f32[768]{0:T(1024)} %param.18) | copy-start | bytes 9220
  0.7 11.8 %copy-start.11 = (bf16[768]{0:T(1024)(128)(2,1)S(1)}, bf16[768]{0:T(1024)(128)(2,1)}, u32[]{:S(2)}) copy-start(bf16[768]{0:T(1024)(128)(2,1)} %param.19) | copy-start | bytes 4612
  0.7 11.8 %copy-start.10 = (f32[768]{0:T(1024)S(1)}, f32[768]{0:T(1024)}, u32[]{:S(2)}) copy-start(f32[768]{0:T(1024)} %param.20) | copy-start | bytes 9220
  7.2 11.0 %copy-start = (bf16[16,1664]{1,0:T(8,128)(2,1)S(1)}, bf16[16,1664]{1,0:T(8,128)(2,1)}, u32[]{:S(2)}) copy-start(bf16[16,1664]{1,0:T(8,128)(2,1)} %get-tuple-element.39.refs_4_) | copy-start | bytes 159748
  7.2 9.0 %collective-permute-start = (bf16[16,1664]{1,0:T(8,128)(2,1)}, bf16[16,1664]{1,0:T(8,128)(2,1)S(1)}, u32[]{:S(2)}, u32[]{:S(2)}) collective-permute-start(bf16[16,1664]{1,0:T(8,128)(2,1)} %get-tuple-element.39.refs_4_), channel_id=1, source_target_pairs={{0,64},{32,96},{64,0},{96,32},{128,192},{160,224},{192,128},{224,1... | collective-permute-start | bytes 159752 | tf_op jit(solution)/shard_map/ppermute | solution.py:668
  9.6 6.7 %collective-permute-start.5 = (bf16[16,1664]{1,0:T(8,128)(2,1)}, bf16[16,1664]{1,0:T(8,128)(2,1)S(1)}, u32[]{:S(2)}, u32[]{:S(2)}) collective-permute-start(bf16[16,1664]{1,0:T(8,128)(2,1)} %get-tuple-element.39.refs_4_), channel_id=1, source_target_pairs={{0,192},{32,224},{64,128},{96,160},{128,64},{160,96},{192,0},{224,... | collective-permute-start | bytes 159752 | tf_op jit(solution)/shard_map/ppermute | solution.py:668
  10.0 6.8 %collective-permute-start.3 = (bf16[16,1664]{1,0:T(8,128)(2,1)}, bf16[16,1664]{1,0:T(8,128)(2,1)S(1)}, u32[]{:S(2)}, u32[]{:S(2)}) collective-permute-start(bf16[16,1664]{1,0:T(8,128)(2,1)} %get-tuple-element.39.refs_4_), channel_id=1, source_target_pairs={{0,128},{32,160},{64,192},{96,224},{128,0},{160,32},{192,64},{224,... | collective-permute-start | bytes 159752 | tf_op jit(solution)/shard_map/ppermute | solution.py:668
  11.8 5.6 %collective-permute-start.1 = (bf16[16,1664]{1,0:T(8,128)(2,1)}, bf16[16,1664]{1,0:T(8,128)(2,1)S(1)}, u32[]{:S(2)}, u32[]{:S(2)}) collective-permute-start(bf16[16,1664]{1,0:T(8,128)(2,1)} %get-tuple-element.39.refs_4_), channel_id=1, source_target_pairs={{0,32},{32,0},{64,96},{96,64},{128,160},{160,128},{192,224},{224,1... | collective-permute-start | bytes 159752 | tf_op jit(solution)/shard_map/ppermute | solution.py:668
  16.3 1.5 %collective-permute-start.6 = (bf16[16,1664]{1,0:T(8,128)(2,1)S(1)}, bf16[16,1664]{1,0:T(8,128)(2,1)S(1)}, u32[]{:S(2)}, u32[]{:S(2)}) collective-permute-start(bf16[16,1664]{1,0:T(8,128)(2,1)S(1)} %collective-permute-done.5.refs_10_), channel_id=1, source_target_pairs={{0,32},{32,0},{64,96},{96,64},{128,160},{160,128},{192,224},{224,1... | collective-permute-start | bytes 159752 | tf_op jit(solution)/shard_map/ppermute | solution.py:668
  16.9 1.2 %collective-permute-start.4 = (bf16[16,1664]{1,0:T(8,128)(2,1)S(1)}, bf16[16,1664]{1,0:T(8,128)(2,1)S(1)}, u32[]{:S(2)}, u32[]{:S(2)}) collective-permute-start(bf16[16,1664]{1,0:T(8,128)(2,1)S(1)} %collective-permute-done.3.refs_8_), channel_id=1, source_target_pairs={{0,32},{32,0},{64,96},{96,64},{128,160},{160,128},{192,224},{224,1... | collective-permute-start | bytes 159752 | tf_op jit(solution)/shard_map/ppermute | solution.py:668
  17.0 1.3 %collective-permute-start.2 = (bf16[16,1664]{1,0:T(8,128)(2,1)S(1)}, bf16[16,1664]{1,0:T(8,128)(2,1)S(1)}, u32[]{:S(2)}, u32[]{:S(2)}) collective-permute-start(bf16[16,1664]{1,0:T(8,128)(2,1)S(1)} %collective-permute-done.refs_6_), channel_id=1, source_target_pairs={{0,32},{32,0},{64,96},{96,64},{128,160},{160,128},{192,224},{224,1... | collective-permute-start | bytes 159752 | tf_op jit(solution)/shard_map/ppermute | solution.py:668
  22.8 21.1 %all-to-all-start = ((f32[32,1,128]{2,1,0:T(1,128)}), f32[32,1,128]{2,1,0:T(1,128)S(1)}, u32[]{:S(2)}, u32[]{:S(2)}) async-start(f32[32,1,128]{2,1,0:T(1,128)} %get-tuple-element.43), calls=%async_computation | async-start | bytes 32768 | tf_op jit(solution)/shard_map/all_to_all | solution.py:740
  43.8 4.9 %copy-start.7 = (f32[32,1,128]{2,1,0:T(1,128)}, f32[32,1,128]{2,1,0:T(1,128)S(1)}, u32[]{:S(2)}) copy-start(f32[32,1,128]{2,1,0:T(1,128)S(1)} %all-to-all-done.refs_0_) | copy-start | bytes 49156
  43.8 17.7 %all-to-all-start.1 = ((bf16[8,384,128]{2,1,0:T(8,128)(2,1)}), bf16[8,384,128]{2,1,0:T(8,128)(2,1)S(1)}, u32[]{:S(2)}, u32[]{:S(2)}) async-start(bf16[8,384,128]{2,1,0:T(8,128)(2,1)} %get-tuple-element.58), calls=%async_computation.1 | async-start | bytes 1572864 | tf_op jit(solution)/shard_map/all_to_all | solution.py:768
  53.4 8.1 %collective-permute-start.7 = (bf16[8,64,128]{2,1,0:T(8,128)(2,1)}, bf16[8,64,128]{2,1,0:T(8,128)(2,1)S(1)}, u32[]{:S(2)}, u32[]{:S(2)}) collective-permute-start(bf16[8,64,128]{2,1,0:T(8,128)(2,1)} %get-tuple-element.62), channel_id=1, source_target_pairs={{0,2},{1,3},{2,0},{3,1},{4,6},{5,7},{6,4},{7,5},{8,10},{9,11},{10,... | collective-permute-start | bytes 393224 | tf_op jit(solution)/shard_map/ppermute | solution.py:673
  56.6 12.6 %collective-permute-start.8 = (bf16[8,64,128]{2,1,0:T(8,128)(2,1)}, bf16[8,64,128]{2,1,0:T(8,128)(2,1)S(1)}, u32[]{:S(2)}, u32[]{:S(2)}) collective-permute-start(bf16[8,64,128]{2,1,0:T(8,128)(2,1)} %get-tuple-element.69), channel_id=1, source_target_pairs={{0,1},{1,0},{2,3},{3,2},{4,5},{5,4},{6,7},{7,6},{8,9},{9,8},{10,11... | collective-permute-start | bytes 393224 | tf_op jit(solution)/shard_map/ppermute | solution.py:673
  57.2 12.1 %collective-permute-start.9 = (bf16[8,64,128]{2,1,0:T(8,128)(2,1)}, bf16[8,64,128]{2,1,0:T(8,128)(2,1)S(1)}, u32[]{:S(2)}, u32[]{:S(2)}) collective-permute-start(bf16[8,64,128]{2,1,0:T(8,128)(2,1)} %get-tuple-element.70), channel_id=1, source_target_pairs={{0,3},{1,2},{2,1},{3,0},{4,7},{5,6},{6,5},{7,4},{8,11},{9,10},{10,... | collective-permute-start | bytes 393224 | tf_op jit(solution)/shard_map/ppermute | solution.py:673
  61.5 7.7 %copy-start.1 = (bf16[8,64,128]{2,1,0:T(8,128)(2,1)}, bf16[8,64,128]{2,1,0:T(8,128)(2,1)S(1)}, u32[]{:S(2)}) copy-start(bf16[8,64,128]{2,1,0:T(8,128)(2,1)S(1)} %collective-permute-done.7.refs_1_) | copy-start | bytes 393220
  64.9 7.5 %collective-permute-start.10 = (bf16[8,56,128]{2,1,0:T(8,128)(2,1)}, bf16[8,56,128]{2,1,0:T(8,128)(2,1)S(1)}, u32[]{:S(2)}, u32[]{:S(2)}) collective-permute-start(bf16[8,56,128]{2,1,0:T(8,128)(2,1)} %get-tuple-element.72), channel_id=1, source_target_pairs={{0,2},{1,3},{2,0},{3,1},{4,6},{5,7},{6,4},{7,5},{8,10},{9,11},{10,... | collective-permute-start | bytes 344072 | tf_op jit(solution)/shard_map/ppermute | solution.py:673
  68.1 5.0 %collective-permute-start.11 = (bf16[8,56,128]{2,1,0:T(8,128)(2,1)}, bf16[8,56,128]{2,1,0:T(8,128)(2,1)S(1)}, u32[]{:S(2)}, u32[]{:S(2)}) collective-permute-start(bf16[8,56,128]{2,1,0:T(8,128)(2,1)} %get-tuple-element.73), channel_id=1, source_target_pairs={{0,1},{1,0},{2,3},{3,2},{4,5},{5,4},{6,7},{7,6},{8,9},{9,8},{10,11... | collective-permute-start | bytes 344072 | tf_op jit(solution)/shard_map/ppermute | solution.py:673
  68.6 6.2 %collective-permute-start.12 = (bf16[8,56,128]{2,1,0:T(8,128)(2,1)}, bf16[8,56,128]{2,1,0:T(8,128)(2,1)S(1)}, u32[]{:S(2)}, u32[]{:S(2)}) collective-permute-start(bf16[8,56,128]{2,1,0:T(8,128)(2,1)} %get-tuple-element.74), channel_id=1, source_target_pairs={{0,3},{1,2},{2,1},{3,0},{4,7},{5,6},{6,5},{7,4},{8,11},{9,10},{10,... | collective-permute-start | bytes 344072 | tf_op jit(solution)/shard_map/ppermute | solution.py:673
  69.3 0.6 copy-start.2
  69.9 0.6 copy-start.3
  72.4 2.5 %copy-start.4 = (bf16[8,56,128]{2,1,0:T(8,128)(2,1)}, bf16[8,56,128]{2,1,0:T(8,128)(2,1)S(1)}, u32[]{:S(2)}) copy-start(bf16[8,56,128]{2,1,0:T(8,128)(2,1)S(1)} %collective-permute-done.10.refs_2_) | copy-start | bytes 344068
  73.1 1.8 %copy-start.5 = (bf16[8,56,128]{2,1,0:T(8,128)(2,1)}, bf16[8,56,128]{2,1,0:T(8,128)(2,1)S(1)}, u32[]{:S(2)}) copy-start(bf16[8,56,128]{2,1,0:T(8,128)(2,1)S(1)} %collective-permute-done.11.refs_3_) | copy-start | bytes 344068
  74.9 0.7 copy-start.6
